TPU v7x, 32 devices: a whole 2x2x4 slice. The times are simulated.
32 devices in a mesh: row: 8 (over y, x, core), col: 4 (over z).
Axes of the slice: x: 2, y: 2, z: 4, core: 2. Of those that a mesh axis runs over, the one named last changes fastest.
Arguments:
- slab_rows: bfloat16 [8832, 2208], P('row'), may hold values from -6 to 6
- slab_pattern: int32 [128, 32], P('row'), may hold values 0 or 1
- owned_rows: bfloat16 [2208, 4416], P(('row', 'col')), may hold values from -0.1875 to 0.1875
- owned_pattern: int32 [32, 64], P(('row', 'col')), may hold values 0 or 1
- placement: int32 [64], replicated, may hold values from 0 to 63, each once
Outputs:
- product: bfloat16 [8832, 4416], P('row', 'col')
Inputs may be any that keep to these rules, and one draw needn't show every extreme that they name: `placement`: each block column appears once.
All inputs are finite; a program needn't handle non-finite values. No bound on the sum of `slab_pattern` or of `owned_pattern` on one device may be relied on, other than what follows from the above.
Results may differ from a plain program's by a relative error of at most 0.001.
Values may be sent and summed in bfloat16 or wider, within the bound.
No kernel may reach another device: no remote copies, remote signals or barrier semaphores. Data moves between devices by JAX's collectives and lax.ppermute only.
A program may use at most 192 MiB of HBM per device.

v0:
```python
import jax
import jax.numpy as jnp
from jax import lax
from jax.sharding import PartitionSpec as P

BS = 69


def per_device(slab_rows, slab_pattern, owned_rows, owned_pattern, placement):
    rows_here = slab_pattern.shape[0]
    depth_blocks = slab_pattern.shape[1]
    owned_count = owned_pattern.shape[0]
    column_blocks = owned_pattern.shape[1]
    slab_mask = slab_pattern[:, None, :, None].astype(jnp.bfloat16)
    slab_full = (slab_rows.reshape(rows_here, BS, depth_blocks, BS) * slab_mask).reshape(
        rows_here * BS, depth_blocks * BS
    )
    owned_mask = owned_pattern[:, None, :, None].astype(jnp.bfloat16)
    owned_blocks = owned_rows.reshape(owned_count, BS, column_blocks, BS) * owned_mask
    owned_blocks = jnp.take(owned_blocks, placement, axis=2).reshape(
        owned_count * BS, column_blocks * BS
    )
    panel_here = lax.all_to_all(owned_blocks, "col", split_axis=1, concat_axis=0, tiled=True)
    result = jnp.dot(
        slab_full,
        lax.all_gather(panel_here, "row", axis=0, tiled=True),
        preferred_element_type=jnp.float32,
    )
    return result.astype(jnp.bfloat16)


def solution(mesh):
    return jax.shard_map(
        per_device,
        mesh=mesh,
        in_specs=(
            P("row", None),
            P("row", None),
            P(("row", "col"), None),
            P(("row", "col"), None),
            P(),
        ),
        out_specs=P("row", "col"),
        check_vma=False,
    )
```

profile of v0, /device:TPU:0, one launch (start us, length us, event | category | flops | bytes accessed | tf_op | source)
XLA Modules:
  0.0 107.7 jit_solution(13725803988092087369)
XLA Ops:
  6.5 0.0 all-gather.3.cloned.1.call-start
  6.5 0.7 compare_select_fusion
  7.2 0.7 compare_and_fusion
  7.9 4.7 %reshape.51 = bf16[1,69,64,69]{3,2,1,0:T(8,128)(2,1)S(1)} reshape(bf16[69,4416]{1,0:T(8,128)(2,1)} %param.7) | data formatting | bytes 1218816 | tf_op jit(solution)/shard_map/reshape | solution.py:19
  12.6 0.7 convert_bitcast_fusion
  13.3 0.9 fusion.1
  14.2 0.8 gather_fusion
  15.0 0.0 copy-start
  15.0 0.3 copy.10
  15.3 1.9 %gather.7 = bf16[69,4,1104]{2,1,0:T(4,128)(2,1)S(1)} reshape(bf16[69,64,69]{2,1,0:T(8,128)(2,1)S(1)} %copy.10) | data formatting | bytes 1218816 | tf_op jit(solution)/shard_map/jit(_take)/gather | solution.py:20
  17.2 0.1 broadcast_in_dim.20
  17.3 0.1 broadcast_in_dim.21
  17.4 0.1 broadcast_in_dim.22
  17.5 0.3 broadcast_select_fusion
  17.8 0.1 copy.11
  17.9 23.6 %all_to_all.16 = bf16[69,4,1104]{2,0,1:T(8,128)(2,1)S(1)} all-to-all(bf16[69,4,1104]{2,0,1:T(8,128)(2,1)S(1)} %copy.11), channel_id=1, replica_groups=mesh['row'=8,'col'=4] {'col'}, dimensions={1} | all-to-all | bytes 1218816 | tf_op jit(solution)/shard_map/all_to_all | solution.py:23
  41.5 1.1 %reshape.64 = bf16[1,276,1104]{2,1,0:T(8,128)(2,1)} reshape(bf16[4,69,1104]{2,1,0:T(8,128)(2,1)S(1)} %bitcast.10) | data formatting | bytes 1218816
  42.6 0.0 all-gather.3.cloned.1.call-update
  42.6 0.0 copy-done
  42.6 4.7 %mul.27 = bf16[16,69,32,69]{3,2,1,0:T(8,128)(2,1)} broadcast(bf16[16,32]{1,0:T(8,128)(2,1)S(1)} %convert_element_type.18), dimensions={0,2} | broadcast | bytes 4876288 | tf_op jit(solution)/shard_map/mul | solution.py:15
  47.3 16.5 %mul.28 = bf16[1104,2208]{1,0:T(8,128)(2,1)} reshape(bf16[16,69,32,69]{3,2,1,0:T(8,128)(2,1)} %mul.27) | data formatting | bytes 9750528 | tf_op jit(solution)/shard_map/mul | solution.py:15
  63.8 18.8 %all-gather.3.cloned.1.call-done = bf16[8,276,1104]{2,1,0:T(8,128)(2,1)} async-done(((bf16[1,276,1104]{2,1,0:T(8,128)(2,1)}), bf16[8,276,1104]{2,1,0:T(8,128)(2,1)}) %all-gather.3.cloned.1.call-update) | async-done | bytes 4875280 | tf_op jit(solution)/shard_map/all_gather | solution.py:26
  82.6 6.2 %reshape.65 = bf16[2208,1104]{1,0:T(8,128)(2,1)} reshape(bf16[8,276,1104]{2,1,0:T(8,128)(2,1)} %all-gather.3.cloned.1.call-done) | data formatting | bytes 9750528
  88.8 12.0 %convolution_convert_fusion = bf16[1104,1104]{1,0:T(8,128)(2,1)} fusion(bf16[2208,1104]{1,0:T(8,128)(2,1)} %reshape.65, bf16[1104,2208]{1,0:T(8,128)(2,1)} %param.5, bf16[1104,2208]{1,0:T(8,128)(2,1)} %mul.28), kind=kOutput, calls=%fused_computation.1 | convolution fusion | flops 5385948160 | bytes 17063424 | tf_op jit(solution)/shard_map/dot_general | solution.py:24
  (2 shorter events, 0.0 us)
Async XLA Ops:
  6.5 76.1 %all-gather.3.cloned.1.call-start = ((), (), s32[]{:S(2)}) async-start(), calls=%async_computation.1 | async-start | bytes 5806080 | tf_op jit(solution)/shard_map/all_gather | solution.py:26
  15.0 27.6 %copy-start = (s32[16,32]{1,0:T(8,128)S(1)}, s32[16,32]{1,0:T(8,128)}, u32[]{:S(2)}) copy-start(s32[16,32]{1,0:T(8,128)} %param.6) | copy-start | bytes 6148
Sparse Core Ops, SparseCore 0:
  42.7 39.8 all-gather.2
where the time goes:
time: 108 us
  local copies, waits for them, and re-layouts  36.6 us (34%)
  blocking collectives  23.6 us (22%)
  waiting for transfers between devices  18.8 us (17%)
  between operations  13.5 us (12%)
  matrix products  12 us (11%)
  other arithmetic  3.19 us (3%)
    all_to_all x1, blocking collectives, per_device(): lax.all_to_all(owned_blocks, 'col', split_axis=1, concat_axis=0, tiled=True)  23.6 us
    mul x2, local copies, waits for them, and re-layouts, per_device(): slab_rows.reshape(rows_here, BS, depth_blocks, BS) * slab_mask  21.2 us
    all_gather x1, waiting for transfers between devices, per_device(): lax.all_gather(panel_here, 'row', axis=0, tiled=True)  18.8 us
    dot_general x1, matrix products, per_device(): jnp.dot(slab_full, lax.all_gather(panel_here, 'row', axis=0, tiled=True),...  12 us
    unnamed x4, local copies, waits for them, and re-layouts  7.32 us
    reshape x1, local copies, waits for them, and re-layouts, per_device(): owned_rows.reshape(owned_count, BS, column_blocks, BS) * owned_mask  4.73 us
    gather x3, local copies, waits for them, and re-layouts, per_device(): jnp.take(owned_blocks, placement, axis=2)  3 us
  transfers between devices with their start and end apart: 1, of which 1 were waited for; matrix products, arithmetic and copies ran while one was open for 20% of the time, Pallas kernels for 0%

commit v1 on v0

v1 whole, which is shorter than its diff:
```python
import functools

import jax
import jax.numpy as jnp
from jax import lax
from jax.experimental import pallas as pl
from jax.experimental.pallas import tpu as pltpu
from jax.sharding import PartitionSpec as P

BS = 69
LANES = 128
UNIT = 72
SLOT = 80
DEPTH = 256
VMEM_LIMIT = 28 * 2**20
X_SPLIT = False


def up(n, m):
    return (n + m - 1) // m * m


def moved(load, start, at, width):
    base = start // LANES
    off = start - base * LANES
    first = load(base)
    second = load(base + 1)
    lane_at = at % LANES
    turn = lax.rem(lane_at - off + LANES, LANES)
    first = pltpu.roll(first, turn, 1)
    second = pltpu.roll(second, turn, 1)
    lane = lax.broadcasted_iota(jnp.int32, first.shape, 1)
    pieces = []
    tile = at // LANES
    lo, hi = lane_at, min(lane_at + width, LANES)
    pieces.append((tile, jnp.where(lane < LANES - off + lane_at, first, second), lo, hi))
    if lane_at + width > LANES:
        pieces.append((tile + 1, jnp.where(lane < lane_at - off, first, second), 0, lane_at + width - LANES))
    return pieces


def right_kernel(n_col, placement, pattern, rows, *outs):
    width = outs[0].shape[1]
    here = placement.shape[0] // n_col
    me = lax.axis_index("col")
    shape = (UNIT, LANES)
    lane = lax.broadcasted_iota(jnp.int32, shape, 1)
    real = lax.broadcasted_iota(jnp.int32, shape, 0) < BS

    def load(tile):
        return rows[:, pl.ds(pl.multiple_of(tile * LANES, LANES), LANES)].astype(jnp.float32)

    for step in range(n_col):
        tiles = [jnp.zeros(shape, jnp.float32) for _ in range(width // LANES)]
        for t in range(here):
            source = placement[(me ^ step) * here + t]
            keep = real & (jnp.full(shape, pattern[0, source]) > 0)
            for tile, value, lo, hi in moved(load, source * BS, t * BS, BS):
                tiles[tile] = jnp.where((lane >= lo) & (lane < hi) & keep, value, tiles[tile])
        for at, value in enumerate(tiles):
            outs[step][:, at * LANES : (at + 1) * LANES] = value.astype(jnp.bfloat16)


def right_units(owned_rows, owned_pattern, placement, n_col):
    columns = owned_rows.shape[1]
    width = up(columns // n_col, LANES)
    return pl.pallas_call(
        functools.partial(right_kernel, n_col),
        grid=(1,),
        out_shape=[jax.ShapeDtypeStruct((UNIT, width), jnp.bfloat16)] * n_col,
        in_specs=[
            pl.BlockSpec(memory_space=pltpu.SMEM),
            pl.BlockSpec(memory_space=pltpu.SMEM),
            pl.BlockSpec((UNIT, up(columns, LANES) + LANES), lambda i: (0, 0)),
        ],
        out_specs=[pl.BlockSpec((UNIT, width), lambda i: (0, 0))] * n_col,
        compiler_params=pltpu.CompilerParams(vmem_limit_bytes=VMEM_LIMIT),
        name="right_units",
    )(placement, owned_pattern, owned_rows)


def place(slot):
    return slot // 3 * DEPTH + slot % 3 * SLOT


def left_kernel(n_col, columns, masks, pattern, rows, *refs):
    outs, pick, by_block = refs[:n_col], refs[-2], refs[-1]
    core = lax.axis_index("row") & 1
    block_rows, depth = pattern.shape
    high, width = outs[0].shape
    mine = [lax.axis_index("row") ^ jnp.where(core == 0, m0, m1) for m0, m1 in masks]
    blocks = [[m * n_col + (lax.axis_index("col") ^ step) for m in mine] for step in range(n_col)]

    @pl.when(pl.program_id(0) == 0)
    def _():
        lane = lax.broadcasted_iota(jnp.int32, (depth, width), 1)
        which = lax.broadcasted_iota(jnp.int32, (depth, width), 0)
        col = lax.broadcasted_iota(jnp.int32, (DEPTH, DEPTH), 1)
        ahead = lax.broadcasted_iota(jnp.int32, (DEPTH, DEPTH), 0) - col
        some = pattern[...].astype(jnp.bfloat16)
        for step in range(n_col):
            chosen = jnp.full((depth, width), -1, jnp.int32)
            for t, block in enumerate(blocks[step]):
                chosen = jnp.where((lane >= place(t)) & (lane < place(t) + BS), block, chosen)
                off = lax.rem(block * BS, LANES)
                at = t % 3 * SLOT
                hit = (ahead == off - at) & (col >= at) & (col < at + BS)
                pick[step * len(masks) + t] = jnp.where(hit, 1.0, 0.0).astype(jnp.bfloat16)
            spread = jnp.where(chosen == which, 1.0, 0.0).astype(jnp.bfloat16)
            by_block[step] = jnp.dot(some, spread, preferred_element_type=jnp.float32).astype(jnp.bfloat16)

    row = lax.broadcasted_iota(jnp.int32, (high, block_rows), 0) + pl.program_id(0) * high
    owner = lax.broadcasted_iota(jnp.int32, (high, block_rows), 1) * BS
    owned = jnp.where((row >= owner) & (row < owner + BS), 1.0, 0.0).astype(jnp.bfloat16)
    lane = lax.broadcasted_iota(jnp.int32, (high, DEPTH), 1)
    for step in range(n_col):
        for first in range(0, len(masks), 3):
            total = jnp.zeros((high, DEPTH), jnp.float32)
            for t in range(first, min(first + 3, len(masks))):
                tile = blocks[step][t] * BS // LANES
                part = rows[:, pl.ds(pl.multiple_of(tile * LANES, LANES), DEPTH)]
                part = jnp.where(lane < columns - tile * LANES, part, jnp.zeros_like(part))
                total += jnp.dot(part, pick[step * len(masks) + t], preferred_element_type=jnp.float32)
            at = first // 3 * DEPTH
            keep = jnp.dot(owned, by_block[step, :, at : at + DEPTH], preferred_element_type=jnp.float32)
            outs[step][:, at : at + DEPTH] = jnp.where(keep > 0.5, total, 0.0).astype(jnp.bfloat16)


def left_sides(slab_rows, slab_pattern, n_col, masks):
    height, columns = slab_rows.shape
    width = up(len(masks), 3) // 3 * DEPTH
    wide = up(columns, LANES) + LANES
    high = next(h for h in (368, 48, 16) if height % h == 0 and h * (wide + n_col * width) * 4 <= 12 * 2**20)
    return pl.pallas_call(
        functools.partial(left_kernel, n_col, columns, masks),
        grid=(height // high,),
        out_shape=[jax.ShapeDtypeStruct((height, width), jnp.bfloat16)] * n_col,
        in_specs=[
            pl.BlockSpec(slab_pattern.shape, lambda i: (0, 0)),
            pl.BlockSpec((high, wide), lambda i: (i, 0)),
        ],
        out_specs=[pl.BlockSpec((high, width), lambda i: (i, 0))] * n_col,
        scratch_shapes=[
            pltpu.VMEM((n_col * len(masks), DEPTH, DEPTH), jnp.bfloat16),
            pltpu.VMEM((n_col, slab_pattern.shape[0], width), jnp.bfloat16),
        ],
        compiler_params=pltpu.CompilerParams(vmem_limit_bytes=VMEM_LIMIT),
        cost_estimate=pl.CostEstimate(flops=height * n_col * len(masks) * DEPTH * DEPTH * 2, bytes_accessed=height * (columns + n_col * width) * 2, transcendentals=0),
        name="left_sides",
    )(slab_pattern, slab_rows)


def multiply_kernel(parts, with_total, *refs):
    lefts, places, n_pieces = parts
    pieces = refs[lefts : lefts + n_pieces]
    total = refs[lefts + n_pieces] if with_total else None
    out, right = refs[-2], refs[-1]

    @pl.when(pl.program_id(0) == 0)
    def _():
        right[...] = jnp.zeros_like(right)
        for at, piece, unit in places:
            right[at : at + UNIT, :] = pieces[piece][unit * UNIT : (unit + 1) * UNIT, :]

    width = refs[0].shape[1]
    value = total[...] if with_total else None
    for i in range(lefts):
        part = jnp.dot(refs[i][...], right[i * width : (i + 1) * width, :], preferred_element_type=jnp.float32)
        value = part if value is None else value + part
    out[...] = value[:, : out.shape[1]].astype(out.dtype)


def multiply(lefts, parts, total, columns, dtype):
    height, width = lefts[0].shape
    pieces, places = [], []
    base = 0
    for steps, group in parts:
        for slots, piece in group:
            for unit, (step, slot) in enumerate((step, slot) for slot in slots for step in range(steps)):
                places.append(((base + step) * width + place(slot), len(pieces), unit))
            pieces.append(piece)
        base += steps
    high = 368
    operands = [*lefts, *pieces]
    whole = lambda a: pl.BlockSpec(a.shape, lambda i: (0, 0))
    rows = lambda a: pl.BlockSpec((high, a.shape[1]), lambda i: (i, 0))
    in_specs = [rows(a) for a in lefts] + [whole(a) for a in pieces]
    if total is not None:
        operands.append(total)
        in_specs.append(rows(total))
    wide = pieces[0].shape[1]
    out = jax.ShapeDtypeStruct((height, columns if dtype == jnp.bfloat16 else wide), dtype)
    return pl.pallas_call(
        functools.partial(multiply_kernel, (len(lefts), places, len(pieces)), total is not None),
        grid=(height // high,),
        out_shape=out,
        in_specs=in_specs,
        out_specs=rows(out),
        scratch_shapes=[pltpu.VMEM((width * len(lefts), wide), jnp.bfloat16)],
        compiler_params=pltpu.CompilerParams(vmem_limit_bytes=VMEM_LIMIT),
        cost_estimate=pl.CostEstimate(flops=2 * height * width * len(lefts) * wide, bytes_accessed=height * columns * 4, transcendentals=0),
        name="multiply",
    )(*operands)


def per_device(n_row, n_col, slab_rows, slab_pattern, owned_rows, owned_pattern, placement):
    columns = owned_rows.shape[1] // n_col
    bits = [1 << b for b in range(1, n_row.bit_length() - 1)]
    orders = (bits, bits[::-1])

    def along_row(value, move):
        return lax.ppermute(value, "row", [(i, i ^ move[i & 1]) for i in range(n_row)])

    units = right_units(owned_rows, owned_pattern, placement, n_col)
    arrived = [units[0]]
    for step in range(1, n_col):
        arrived.append(lax.ppermute(units[step], "col", [(i, i ^ step) for i in range(n_col)]))

    masks = [(0, 0)]
    for move in zip(*orders):
        masks += [(m[0] ^ move[0], m[1] ^ move[1]) for m in masks]
    masks += [(1 ^ m[1], 1 ^ m[0]) for m in masks]
    lefts = left_sides(slab_rows, slab_pattern, n_col, masks)

    def gathered(steps):
        first = jnp.concatenate([arrived[s] for s in steps]) if len(steps) > 1 else arrived[steps[0]]
        pieces = [((0,), first)]
        for move in zip(*orders):
            at = len(pieces)
            pieces += [((slots[0] + at,), along_row(value, move)) for slots, value in pieces]
        half = len(masks) // 2
        if X_SPLIT:
            pieces += [((slots[0] + half,), along_row(value, (1, 1))) for slots, value in pieces]
        else:
            every = jnp.concatenate([value for _, value in pieces])
            pieces.append((tuple(range(half, 2 * half)), along_row(every, (1, 1))))
        return len(steps), pieces

    GROUPS = [[step] for step in range(n_col)]
    most = max(1, 24 // len(masks))
    CALLS = [GROUPS[at : min(at + most, n_col - 1)] for at in range(0, n_col - 1, most)] + [GROUPS[-1:]]
    total = None
    for at, call in enumerate(CALLS):
        mine = [lefts[step] for group in call for step in group]
        last = at == len(CALLS) - 1
        total = multiply(mine, [gathered(group) for group in call], total, columns, jnp.bfloat16 if last else jnp.float32)
    return total


def solution(mesh):
    return jax.shard_map(
        functools.partial(per_device, mesh.shape["row"], mesh.shape["col"]),
        mesh=mesh,
        in_specs=(
            P("row", None),
            P("row", None),
            P(("row", "col"), None),
            P(("row", "col"), None),
            P(),
        ),
        out_specs=P("row", "col"),
        check_vma=False,
    )
```

time: 108 us -> 62 us (0.57)
  local copies, waits for them, and re-layouts: 36.6 us -> 2.4 us
  blocking collectives: 23.6 us -> 0 us
  Pallas kernels: 0 us -> 21.6 us
  starting transfers between devices: 0.01 us -> 20.7 us
  between operations: 13.5 us -> 0.15 us
  matrix products: 12 us -> 0 us
  other arithmetic: 3.19 us -> 0.21 us
  waiting for transfers between devices: 18.8 us -> 16.8 us
    all_to_all x1 -> x0, blocking collectives: 23.6 us -> none  [per_device(): lax.all_to_all(owned_blocks, 'col', split_axis=1, concat_axis=0, tiled=True)]
    pallas_call x0 -> x4, Pallas kernels: none -> 21.6 us  [the longest x2 11.7 us: multiply(): pl.pallas_call(functools.partial(multiply_kernel, (len(lefts), places, le...]
    mul x2 -> x0, local copies, waits for them, and re-layouts: 21.2 us -> none  [per_device(): slab_rows.reshape(rows_here, BS, depth_blocks, BS) * slab_mask]
    ppermute x0 -> x19, starting transfers between devices: none -> 20.7 us  [the longest x16 14.8 us: along_row(): lax.ppermute(value, 'row', [(i, i ^ move[i & 1]) for i in range(n_row)])]
    all_gather x1 -> x0, waiting for transfers between devices: 18.8 us -> none  [per_device(): lax.all_gather(panel_here, 'row', axis=0, tiled=True)]
    ppermute x0 -> x19, waiting for transfers between devices: none -> 16.8 us  [the longest x16 10.1 us: along_row(): lax.ppermute(value, 'row', [(i, i ^ move[i & 1]) for i in range(n_row)])]
    dot_general x1 -> x0, matrix products: 12 us -> none  [per_device(): jnp.dot(slab_full, lax.all_gather(panel_here, 'row', axis=0, tiled=True),...]
    unnamed x4 -> x10, local copies, waits for them, and re-layouts: 7.32 us -> 2.4 us
  transfers between devices with their start and end apart: 1 -> 19, of which waited for: 1 -> 6; matrix products, arithmetic and copies ran while one was open for 20% -> 0% of each run, Pallas kernels for 0% -> 26%
where the time goes in v1:
time: 62 us; the launch traced here: 61.8 us
  Pallas kernels  21.6 us (35%)
  starting transfers between devices  20.7 us (33%)
  waiting for transfers between devices  16.8 us (27%)
  local copies, waits for them, and re-layouts  2.4 us (4%)
    ppermute x16, starting transfers between devices, along_row(): lax.ppermute(value, 'row', [(i, i ^ move[i & 1]) for i in range(n_row)])  14.8 us
    pallas_call x2, Pallas kernels, multiply(): pl.pallas_call(functools.partial(multiply_kernel, (len(lefts), places, le...  11.7 us
    ppermute x16, waiting for transfers between devices, along_row(): lax.ppermute(value, 'row', [(i, i ^ move[i & 1]) for i in range(n_row)])  10.1 us
    pallas_call x1, Pallas kernels, left_sides(): pl.pallas_call(functools.partial(left_kernel, n_col, columns, masks), gri...  8.4 us
    ppermute x3, waiting for transfers between devices, per_device(): lax.ppermute(units[step], 'col', [(i, i ^ step) for i in range(n_col)])  6.7 us
    ppermute x3, starting transfers between devices, per_device(): lax.ppermute(units[step], 'col', [(i, i ^ step) for i in range(n_col)])  5.9 us
    unnamed x10, local copies, waits for them, and re-layouts  2.4 us
    pallas_call x1, Pallas kernels, right_units(): pl.pallas_call(functools.partial(right_kernel, n_col), grid=(1,), out_sha...  1.44 us
  transfers between devices with their start and end apart: 19, of which 6 were waited for; matrix products, arithmetic and copies ran while one was open for 0% of the time, Pallas kernels for 26%

profile of v1, /device:TPU:0, one launch (start us, length us, event | category | flops | bytes accessed | tf_op | source)
XLA Modules:
  0.0 61.8 jit_solution(5523183350254416283)
XLA Ops:
  0.0 1.1 %copy-done = bf16[69,4416]{1,0:T(8,128)(2,1)S(1)} copy-done((bf16[69,4416]{1,0:T(8,128)(2,1)S(1)}, bf16[69,4416]{1,0:T(8,128)(2,1)}, u32[]{:S(2)}) %copy-start) | copy-done | bytes 609432
  1.1 0.7 %copy-done.1 = s32[64]{0:T(128)S(1)} copy-done((s32[64]{0:T(128)S(1)}, s32[64]{0:T(128)}, u32[]{:S(2)}) %copy-start.1) | copy-done | bytes 280
  1.7 0.7 %copy-done.2 = s32[1,64]{1,0:T(1,128)S(1)} copy-done((s32[1,64]{1,0:T(1,128)S(1)}, s32[1,64]{1,0:T(1,128)}, u32[]{:S(2)}) %copy-start.2) | copy-done | bytes 280
  2.4 1.4 %right_units.1 = (bf16[72,1152]{1,0:T(8,128)(2,1)S(1)}, bf16[72,1152]{1,0:T(8,128)(2,1)S(1)}, bf16[72,1152]{1,0:T(8,128)(2,1)S(1)}, bf16[72,1152]{1,0:T(8,128)(2,1)S(1)}) custom-call(s32[64]{0:T(128)S(1)} %copy-done.1, s32[1,64]{1,0:T(1,128)S(1)} %copy-done.2, bf16[69,4416]{1,0:T(8,128)(2,1)S(1)} %copy-done), custom_call_target="tpu_custom_call" | custom-call | tf_op jit(solution)/shard_map/right_units/pallas_call | solution.py:67
  3.8 3.1 %collective-permute-start.9 = (bf16[72,1152]{1,0:T(8,128)(2,1)S(1)}, bf16[72,1152]{1,0:T(8,128)(2,1)S(1)}, u32[]{:S(2)}, u32[]{:S(2)}) collective-permute-start(bf16[72,1152]{1,0:T(8,128)(2,1)S(1)} %get-tuple-element.19), channel_id=1, source_target_pairs={{0,1},{1,0},{2,3},{3,2},{4,5},{5,4},{6,7},{7,6},{8,9},{9,8},{10,11... | collective-permute-start | bytes 497672 | tf_op jit(solution)/shard_map/ppermute | solution.py:217
  6.9 1.5 %collective-permute-start.5 = (bf16[72,1152]{1,0:T(8,128)(2,1)S(1)}, bf16[72,1152]{1,0:T(8,128)(2,1)S(1)}, u32[]{:S(2)}, u32[]{:S(2)}) collective-permute-start(bf16[72,1152]{1,0:T(8,128)(2,1)S(1)} %get-tuple-element.18.refs_3_), channel_id=1, source_target_pairs={{0,8},{4,20},{8,0},{12,28},{16,24},{20,4},{24,16},{28,12},{1,9},{5... | collective-permute-start | bytes 497672 | tf_op jit(solution)/shard_map/ppermute | solution.py:212
  8.4 2.6 %collective-permute-start.14 = (bf16[72,1152]{1,0:T(8,128)(2,1)S(1)}, bf16[72,1152]{1,0:T(8,128)(2,1)S(1)}, u32[]{:S(2)}, u32[]{:S(2)}) collective-permute-start(bf16[72,1152]{1,0:T(8,128)(2,1)S(1)} %get-tuple-element.20), channel_id=1, source_target_pairs={{0,2},{1,3},{2,0},{3,1},{4,6},{5,7},{6,4},{7,5},{8,10},{9,11},{10,... | collective-permute-start | bytes 497672 | tf_op jit(solution)/shard_map/ppermute | solution.py:217
  11.0 1.5 %collective-permute-start.6 = (bf16[72,1152]{1,0:T(8,128)(2,1)S(1)}, bf16[72,1152]{1,0:T(8,128)(2,1)S(1)}, u32[]{:S(2)}, u32[]{:S(2)}) collective-permute-start(bf16[72,1152]{1,0:T(8,128)(2,1)S(1)} %get-tuple-element.18.refs_3_), channel_id=1, source_target_pairs={{0,16},{4,12},{8,24},{12,4},{16,0},{20,28},{24,8},{28,20},{1,17},{... | collective-permute-start | bytes 497672 | tf_op jit(solution)/shard_map/ppermute | solution.py:212
  12.5 0.2 collective-permute-start
  12.8 0.0 collective-permute-done.9.refs_8_
  12.8 1.1 %collective-permute-start.10 = (bf16[72,1152]{1,0:T(8,128)(2,1)S(1)}, bf16[72,1152]{1,0:T(8,128)(2,1)S(1)}, u32[]{:S(2)}, u32[]{:S(2)}) collective-permute-start(bf16[72,1152]{1,0:T(8,128)(2,1)S(1)} %collective-permute-done.9.refs_8_), channel_id=1, source_target_pairs={{0,8},{4,20},{8,0},{12,28},{16,24},{20,4},{24,16},{28,12},{1,9},{5... | collective-permute-start | bytes 497672 | tf_op jit(solution)/shard_map/ppermute | solution.py:212
  13.9 0.0 collective-permute-done.5.refs_4_
  13.9 2.7 %collective-permute-start.7 = (bf16[72,1152]{1,0:T(8,128)(2,1)S(1)}, bf16[72,1152]{1,0:T(8,128)(2,1)S(1)}, u32[]{:S(2)}, u32[]{:S(2)}) collective-permute-start(bf16[72,1152]{1,0:T(8,128)(2,1)S(1)} %collective-permute-done.5.refs_4_), channel_id=1, source_target_pairs={{0,16},{4,12},{8,24},{12,4},{16,0},{20,28},{24,8},{28,20},{1,17},{... | collective-permute-start | bytes 497672 | tf_op jit(solution)/shard_map/ppermute | solution.py:212
  16.6 6.7 %collective-permute-done.14.refs_13_ = bf16[72,1152]{1,0:T(8,128)(2,1)S(1)} collective-permute-done((bf16[72,1152]{1,0:T(8,128)(2,1)S(1)}, bf16[72,1152]{1,0:T(8,128)(2,1)S(1)}, u32[]{:S(2)}, u32[]{:S(2)}) %collective-permute-start.14) | collective-permute-done | bytes 165920 | tf_op jit(solution)/shard_map/ppermute | solution.py:217
  23.3 1.4 %collective-permute-start.11 = (bf16[72,1152]{1,0:T(8,128)(2,1)S(1)}, bf16[72,1152]{1,0:T(8,128)(2,1)S(1)}, u32[]{:S(2)}, u32[]{:S(2)}) collective-permute-start(bf16[72,1152]{1,0:T(8,128)(2,1)S(1)} %collective-permute-done.9.refs_8_), channel_id=1, source_target_pairs={{0,16},{4,12},{8,24},{12,4},{16,0},{20,28},{24,8},{28,20},{1,17},{... | collective-permute-start | bytes 497672 | tf_op jit(solution)/shard_map/ppermute | solution.py:212
  24.6 0.0 collective-permute-done.6.refs_5_
  24.6 1.0 %collective-permute-start.15 = (bf16[72,1152]{1,0:T(8,128)(2,1)S(1)}, bf16[72,1152]{1,0:T(8,128)(2,1)S(1)}, u32[]{:S(2)}, u32[]{:S(2)}) collective-permute-start(bf16[72,1152]{1,0:T(8,128)(2,1)S(1)} %collective-permute-done.14.refs_13_), channel_id=1, source_target_pairs={{0,8},{4,20},{8,0},{12,28},{16,24},{20,4},{24,16},{28,12},{1,9},{5... | collective-permute-start | bytes 497672 | tf_op jit(solution)/shard_map/ppermute | solution.py:212
  25.7 0.0 collective-permute-done.refs_1_
  25.7 0.4 collective-permute-start.16
  26.1 0.0 collective-permute-done.10.refs_9_
  26.1 1.2 %collective-permute-start.1 = (bf16[72,1152]{1,0:T(8,128)(2,1)S(1)}, bf16[72,1152]{1,0:T(8,128)(2,1)S(1)}, u32[]{:S(2)}, u32[]{:S(2)}) collective-permute-start(bf16[72,1152]{1,0:T(8,128)(2,1)S(1)} %collective-permute-done.refs_1_), channel_id=1, source_target_pairs={{0,8},{4,20},{8,0},{12,28},{16,24},{20,4},{24,16},{28,12},{1,9},{5... | collective-permute-start | bytes 497672 | tf_op jit(solution)/shard_map/ppermute | solution.py:212
  27.3 0.0 collective-permute-done.7.refs_6_
  27.3 1.4 %collective-permute-start.12 = (bf16[72,1152]{1,0:T(8,128)(2,1)S(1)}, bf16[72,1152]{1,0:T(8,128)(2,1)S(1)}, u32[]{:S(2)}, u32[]{:S(2)}) collective-permute-start(bf16[72,1152]{1,0:T(8,128)(2,1)S(1)} %collective-permute-done.10.refs_9_), channel_id=1, source_target_pairs={{0,16},{4,12},{8,24},{12,4},{16,0},{20,28},{24,8},{28,20},{1,17},{... | collective-permute-start | bytes 497672 | tf_op jit(solution)/shard_map/ppermute | solution.py:212
  28.7 0.1 pad_maximum_fusion.1
  28.8 1.7 %collective-permute-done.11.refs_10_ = bf16[72,1152]{1,0:T(8,128)(2,1)S(1)} collective-permute-done((bf16[72,1152]{1,0:T(8,128)(2,1)S(1)}, bf16[72,1152]{1,0:T(8,128)(2,1)S(1)}, u32[]{:S(2)}, u32[]{:S(2)}) %collective-permute-start.11) | collective-permute-done | bytes 165920 | tf_op jit(solution)/shard_map/ppermute | solution.py:212
  30.5 0.3 collective-permute-start.2
  30.8 1.0 %collective-permute-done.15.refs_14_ = bf16[72,1152]{1,0:T(8,128)(2,1)S(1)} collective-permute-done((bf16[72,1152]{1,0:T(8,128)(2,1)S(1)}, bf16[72,1152]{1,0:T(8,128)(2,1)S(1)}, u32[]{:S(2)}, u32[]{:S(2)}) %collective-permute-start.15) | collective-permute-done | bytes 165920 | tf_op jit(solution)/shard_map/ppermute | solution.py:212
  31.8 0.0 collective-permute-start.8
  31.8 2.5 %collective-permute-done.1.refs_2_ = bf16[72,1152]{1,0:T(8,128)(2,1)S(1)} collective-permute-done((bf16[72,1152]{1,0:T(8,128)(2,1)S(1)}, bf16[72,1152]{1,0:T(8,128)(2,1)S(1)}, u32[]{:S(2)}, u32[]{:S(2)}) %collective-permute-start.1) | collective-permute-done | bytes 165920 | tf_op jit(solution)/shard_map/ppermute | solution.py:212
  34.4 1.6 %collective-permute-start.17 = (bf16[72,1152]{1,0:T(8,128)(2,1)S(1)}, bf16[72,1152]{1,0:T(8,128)(2,1)S(1)}, u32[]{:S(2)}, u32[]{:S(2)}) collective-permute-start(bf16[72,1152]{1,0:T(8,128)(2,1)S(1)} %collective-permute-done.15.refs_14_), channel_id=1, source_target_pairs={{0,16},{4,12},{8,24},{12,4},{16,0},{20,28},{24,8},{28,20},{1,17},{... | collective-permute-start | bytes 497672 | tf_op jit(solution)/shard_map/ppermute | solution.py:212
  36.0 0.0 collective-permute-done.12.refs_11_
  36.0 0.4 collective-permute-start.3
  36.4 0.1 pad_maximum_fusion.2
  36.5 0.0 copy-start.4
  36.5 0.0 collective-permute-done.16.refs_15_
  36.5 0.1 collective-permute-start.13
  36.6 3.2 %collective-permute-done.17.refs_16_ = bf16[72,1152]{1,0:T(8,128)(2,1)S(1)} collective-permute-done((bf16[72,1152]{1,0:T(8,128)(2,1)S(1)}, bf16[72,1152]{1,0:T(8,128)(2,1)S(1)}, u32[]{:S(2)}, u32[]{:S(2)}) %collective-permute-start.17) | collective-permute-done | bytes 165920 | tf_op jit(solution)/shard_map/ppermute | solution.py:212
  39.7 0.1 pad_maximum_fusion.3
  39.8 0.1 collective-permute-start.18
  39.9 1.6 %collective-permute-done.3.refs_4_ = bf16[72,1152]{1,0:T(8,128)(2,1)S(1)} collective-permute-done((bf16[72,1152]{1,0:T(8,128)(2,1)S(1)}, bf16[72,1152]{1,0:T(8,128)(2,1)S(1)}, u32[]{:S(2)}, u32[]{:S(2)}) %collective-permute-start.3) | collective-permute-done | bytes 165920 | tf_op jit(solution)/shard_map/ppermute | solution.py:212
  41.5 0.1 pad_maximum_fusion
  41.5 0.1 collective-permute-start.4
  41.6 8.4 %left_sides.1 = (bf16[1104,768]{1,0:T(8,128)(2,1)S(1)}, bf16[1104,768]{1,0:T(8,128)(2,1)S(1)}, bf16[1104,768]{1,0:T(8,128)(2,1)S(1)}, bf16[1104,768]{1,0:T(8,128)(2,1)S(1)}) custom-call(s32[16,32]{1,0:T(8,128)S(1)} %copy-done.4, bf16[1104,2208]{1,0:T(8,128)(2,1)S(1)} %copy-done.3), custom_call_target="tpu_custom_call" | custom-call | flops 4630511616 | bytes 11658240 | tf_op jit(solution)/shard_map/left_sides/pallas_call | solution.py:134
  50.1 0.0 collective-permute-done.13.refs_12_
  50.1 0.0 collective-permute-done.18.refs_17_
  50.1 7.7 %multiply.2.refs_6_ = f32[1104,1152]{1,0:T(8,128)S(1)} custom-call(bf16[1104,768]{1,0:T(8,128)(2,1)S(1)} %get-tuple-element.15.refs_0_, bf16[1104,768]{1,0:T(8,128)(2,1)S(1)} %get-tuple-element.16.refs_1_, bf16[1104,768]{1,0:T(8,128)(2,1)S(1)} %get-tuple-element.17.refs_2_, bf16[72,1152]{1,0:T(8,128)(2,1)S(1)} %get-tuple-element.18.refs_3_, ...), custom_call_target="tpu_custom_call" | custom-call | flops 5860491264 | bytes 4875264 | tf_op jit(solution)/shard_map/multiply/pallas_call | solution.py:193
  57.8 0.0 collective-permute-done.4.refs_5_
  57.8 4.0 %multiply.3 = bf16[1104,1104]{1,0:T(8,128)(2,1)} custom-call(bf16[1104,768]{1,0:T(8,128)(2,1)S(1)} %get-tuple-element.13.refs_0_, bf16[72,1152]{1,0:T(8,128)(2,1)S(1)} %collective-permute-done.refs_1_, bf16[72,1152]{1,0:T(8,128)(2,1)S(1)} %collective-permute-done.1.refs_2_, bf16[72,1152]{1,0:T(8,128)(2,1)S(1)} %collective-permute-done.2.refs_3_, ...), custom_call_target="tpu_custom_call" | custom-call | flops 1953497088 | bytes 4875264 | tf_op jit(solution)/shard_map/multiply/pallas_call | solution.py:193
  (8 shorter events, 0.0 us)
Async XLA Ops:
  0.0 1.1 %copy-start = (bf16[69,4416]{1,0:T(8,128)(2,1)S(1)}, bf16[69,4416]{1,0:T(8,128)(2,1)}, u32[]{:S(2)}) copy-start(bf16[69,4416]{1,0:T(8,128)(2,1)} %rows.3) | copy-start | bytes 1828228
  1.1 0.7 %copy-start.1 = (s32[64]{0:T(128)S(1)}, s32[64]{0:T(128)}, u32[]{:S(2)}) copy-start(s32[64]{0:T(128)} %placement.1) | copy-start | bytes 772
  1.7 0.7 %copy-start.2 = (s32[1,64]{1,0:T(1,128)S(1)}, s32[1,64]{1,0:T(1,128)}, u32[]{:S(2)}) copy-start(s32[1,64]{1,0:T(1,128)} %pattern.3) | copy-start | bytes 772
  3.8 8.9 %collective-permute-start.9 = (bf16[72,1152]{1,0:T(8,128)(2,1)S(1)}, bf16[72,1152]{1,0:T(8,128)(2,1)S(1)}, u32[]{:S(2)}, u32[]{:S(2)}) collective-permute-start(bf16[72,1152]{1,0:T(8,128)(2,1)S(1)} %get-tuple-element.19), channel_id=1, source_target_pairs={{0,1},{1,0},{2,3},{3,2},{4,5},{5,4},{6,7},{7,6},{8,9},{9,8},{10,11... | collective-permute-start | bytes 497672 | tf_op jit(solution)/shard_map/ppermute | solution.py:217
  6.9 7.0 %collective-permute-start.5 = (bf16[72,1152]{1,0:T(8,128)(2,1)S(1)}, bf16[72,1152]{1,0:T(8,128)(2,1)S(1)}, u32[]{:S(2)}, u32[]{:S(2)}) collective-permute-start(bf16[72,1152]{1,0:T(8,128)(2,1)S(1)} %get-tuple-element.18.refs_3_), channel_id=1, source_target_pairs={{0,8},{4,20},{8,0},{12,28},{16,24},{20,4},{24,16},{28,12},{1,9},{5... | collective-permute-start | bytes 497672 | tf_op jit(solution)/shard_map/ppermute | solution.py:212
  8.4 14.9 %collective-permute-start.14 = (bf16[72,1152]{1,0:T(8,128)(2,1)S(1)}, bf16[72,1152]{1,0:T(8,128)(2,1)S(1)}, u32[]{:S(2)}, u32[]{:S(2)}) collective-permute-start(bf16[72,1152]{1,0:T(8,128)(2,1)S(1)} %get-tuple-element.20), channel_id=1, source_target_pairs={{0,2},{1,3},{2,0},{3,1},{4,6},{5,7},{6,4},{7,5},{8,10},{9,11},{10,... | collective-permute-start | bytes 497672 | tf_op jit(solution)/shard_map/ppermute | solution.py:217
  11.0 13.6 %collective-permute-start.6 = (bf16[72,1152]{1,0:T(8,128)(2,1)S(1)}, bf16[72,1152]{1,0:T(8,128)(2,1)S(1)}, u32[]{:S(2)}, u32[]{:S(2)}) collective-permute-start(bf16[72,1152]{1,0:T(8,128)(2,1)S(1)} %get-tuple-element.18.refs_3_), channel_id=1, source_target_pairs={{0,16},{4,12},{8,24},{12,4},{16,0},{20,28},{24,8},{28,20},{1,17},{... | collective-permute-start | bytes 497672 | tf_op jit(solution)/shard_map/ppermute | solution.py:212
  12.5 13.1 %collective-permute-start = (bf16[72,1152]{1,0:T(8,128)(2,1)S(1)}, bf16[72,1152]{1,0:T(8,128)(2,1)S(1)}, u32[]{:S(2)}, u32[]{:S(2)}) collective-permute-start(bf16[72,1152]{1,0:T(8,128)(2,1)S(1)} %get-tuple-element.14), channel_id=1, source_target_pairs={{0,3},{1,2},{2,1},{3,0},{4,7},{5,6},{6,5},{7,4},{8,11},{9,10},{10,... | collective-permute-start | bytes 497672 | tf_op jit(solution)/shard_map/ppermute | solution.py:217
  12.8 13.4 %collective-permute-start.10 = (bf16[72,1152]{1,0:T(8,128)(2,1)S(1)}, bf16[72,1152]{1,0:T(8,128)(2,1)S(1)}, u32[]{:S(2)}, u32[]{:S(2)}) collective-permute-start(bf16[72,1152]{1,0:T(8,128)(2,1)S(1)} %collective-permute-done.9.refs_8_), channel_id=1, source_target_pairs={{0,8},{4,20},{8,0},{12,28},{16,24},{20,4},{24,16},{28,12},{1,9},{5... | collective-permute-start | bytes 497672 | tf_op jit(solution)/shard_map/ppermute | solution.py:212
  13.9 13.4 %collective-permute-start.7 = (bf16[72,1152]{1,0:T(8,128)(2,1)S(1)}, bf16[72,1152]{1,0:T(8,128)(2,1)S(1)}, u32[]{:S(2)}, u32[]{:S(2)}) collective-permute-start(bf16[72,1152]{1,0:T(8,128)(2,1)S(1)} %collective-permute-done.5.refs_4_), channel_id=1, source_target_pairs={{0,16},{4,12},{8,24},{12,4},{16,0},{20,28},{24,8},{28,20},{1,17},{... | collective-permute-start | bytes 497672 | tf_op jit(solution)/shard_map/ppermute | solution.py:212
  23.3 7.2 %collective-permute-start.11 = (bf16[72,1152]{1,0:T(8,128)(2,1)S(1)}, bf16[72,1152]{1,0:T(8,128)(2,1)S(1)}, u32[]{:S(2)}, u32[]{:S(2)}) collective-permute-start(bf16[72,1152]{1,0:T(8,128)(2,1)S(1)} %collective-permute-done.9.refs_8_), channel_id=1, source_target_pairs={{0,16},{4,12},{8,24},{12,4},{16,0},{20,28},{24,8},{28,20},{1,17},{... | collective-permute-start | bytes 497672 | tf_op jit(solution)/shard_map/ppermute | solution.py:212
  24.6 7.2 %collective-permute-start.15 = (bf16[72,1152]{1,0:T(8,128)(2,1)S(1)}, bf16[72,1152]{1,0:T(8,128)(2,1)S(1)}, u32[]{:S(2)}, u32[]{:S(2)}) collective-permute-start(bf16[72,1152]{1,0:T(8,128)(2,1)S(1)} %collective-permute-done.14.refs_13_), channel_id=1, source_target_pairs={{0,8},{4,20},{8,0},{12,28},{16,24},{20,4},{24,16},{28,12},{1,9},{5... | collective-permute-start | bytes 497672 | tf_op jit(solution)/shard_map/ppermute | solution.py:212
  25.7 10.8 %collective-permute-start.16 = (bf16[72,1152]{1,0:T(8,128)(2,1)S(1)}, bf16[72,1152]{1,0:T(8,128)(2,1)S(1)}, u32[]{:S(2)}, u32[]{:S(2)}) collective-permute-start(bf16[72,1152]{1,0:T(8,128)(2,1)S(1)} %collective-permute-done.14.refs_13_), channel_id=1, source_target_pairs={{0,16},{4,12},{8,24},{12,4},{16,0},{20,28},{24,8},{28,20},{1,17},{... | collective-permute-start | bytes 497672 | tf_op jit(solution)/shard_map/ppermute | solution.py:212
  26.1 8.3 %collective-permute-start.1 = (bf16[72,1152]{1,0:T(8,128)(2,1)S(1)}, bf16[72,1152]{1,0:T(8,128)(2,1)S(1)}, u32[]{:S(2)}, u32[]{:S(2)}) collective-permute-start(bf16[72,1152]{1,0:T(8,128)(2,1)S(1)} %collective-permute-done.refs_1_), channel_id=1, source_target_pairs={{0,8},{4,20},{8,0},{12,28},{16,24},{20,4},{24,16},{28,12},{1,9},{5... | collective-permute-start | bytes 497672 | tf_op jit(solution)/shard_map/ppermute | solution.py:212
  27.3 8.6 %collective-permute-start.12 = (bf16[72,1152]{1,0:T(8,128)(2,1)S(1)}, bf16[72,1152]{1,0:T(8,128)(2,1)S(1)}, u32[]{:S(2)}, u32[]{:S(2)}) collective-permute-start(bf16[72,1152]{1,0:T(8,128)(2,1)S(1)} %collective-permute-done.10.refs_9_), channel_id=1, source_target_pairs={{0,16},{4,12},{8,24},{12,4},{16,0},{20,28},{24,8},{28,20},{1,17},{... | collective-permute-start | bytes 497672 | tf_op jit(solution)/shard_map/ppermute | solution.py:212
  28.7 12.9 %copy-start.3 = (bf16[1104,2208]{1,0:T(8,128)(2,1)S(1)}, bf16[1104,2208]{1,0:T(8,128)(2,1)}, u32[]{:S(2)}) copy-start(bf16[1104,2208]{1,0:T(8,128)(2,1)} %rows.2) | copy-start | bytes 14625796
  30.5 9.4 %collective-permute-start.2 = (bf16[72,1152]{1,0:T(8,128)(2,1)S(1)}, bf16[72,1152]{1,0:T(8,128)(2,1)S(1)}, u32[]{:S(2)}, u32[]{:S(2)}) collective-permute-start(bf16[72,1152]{1,0:T(8,128)(2,1)S(1)} %collective-permute-done.refs_1_), channel_id=1, source_target_pairs={{0,16},{4,12},{8,24},{12,4},{16,0},{20,28},{24,8},{28,20},{1,17},{... | collective-permute-start | bytes 497672 | tf_op jit(solution)/shard_map/ppermute | solution.py:212
  31.8 18.2 %collective-permute-start.8 = (bf16[288,1152]{1,0:T(8,128)(2,1)S(1)}, bf16[288,1152]{1,0:T(8,128)(2,1)S(1)}, u32[]{:S(2)}, u32[]{:S(2)}) collective-permute-start(bf16[288,1152]{1,0:T(8,128)(2,1)S(1)} %pad_maximum_fusion.1), channel_id=1, source_target_pairs={{0,4},{4,0},{8,12},{12,8},{16,20},{20,16},{24,28},{28,24},{1,5},{5... | collective-permute-start | bytes 1990664 | tf_op jit(solution)/shard_map/ppermute | solution.py:212
  34.4 5.3 %collective-permute-start.17 = (bf16[72,1152]{1,0:T(8,128)(2,1)S(1)}, bf16[72,1152]{1,0:T(8,128)(2,1)S(1)}, u32[]{:S(2)}, u32[]{:S(2)}) collective-permute-start(bf16[72,1152]{1,0:T(8,128)(2,1)S(1)} %collective-permute-done.15.refs_14_), channel_id=1, source_target_pairs={{0,16},{4,12},{8,24},{12,4},{16,0},{20,28},{24,8},{28,20},{1,17},{... | collective-permute-start | bytes 497672 | tf_op jit(solution)/shard_map/ppermute | solution.py:212
  36.0 5.5 %collective-permute-start.3 = (bf16[72,1152]{1,0:T(8,128)(2,1)S(1)}, bf16[72,1152]{1,0:T(8,128)(2,1)S(1)}, u32[]{:S(2)}, u32[]{:S(2)}) collective-permute-start(bf16[72,1152]{1,0:T(8,128)(2,1)S(1)} %collective-permute-done.1.refs_2_), channel_id=1, source_target_pairs={{0,16},{4,12},{8,24},{12,4},{16,0},{20,28},{24,8},{28,20},{1,17},{... | collective-permute-start | bytes 497672 | tf_op jit(solution)/shard_map/ppermute | solution.py:212
  36.5 5.2 %copy-start.4 = (s32[16,32]{1,0:T(8,128)S(1)}, s32[16,32]{1,0:T(8,128)}, u32[]{:S(2)}) copy-start(s32[16,32]{1,0:T(8,128)} %pattern.2) | copy-start | bytes 6148
  36.5 13.6 %collective-permute-start.13 = (bf16[288,1152]{1,0:T(8,128)(2,1)S(1)}, bf16[288,1152]{1,0:T(8,128)(2,1)S(1)}, u32[]{:S(2)}, u32[]{:S(2)}) collective-permute-start(bf16[288,1152]{1,0:T(8,128)(2,1)S(1)} %pad_maximum_fusion.2), channel_id=1, source_target_pairs={{0,4},{4,0},{8,12},{12,8},{16,20},{20,16},{24,28},{28,24},{1,5},{5... | collective-permute-start | bytes 1990664 | tf_op jit(solution)/shard_map/ppermute | solution.py:212
  39.8 10.3 %collective-permute-start.18 = (bf16[288,1152]{1,0:T(8,128)(2,1)S(1)}, bf16[288,1152]{1,0:T(8,128)(2,1)S(1)}, u32[]{:S(2)}, u32[]{:S(2)}) collective-permute-start(bf16[288,1152]{1,0:T(8,128)(2,1)S(1)} %pad_maximum_fusion.3), channel_id=1, source_target_pairs={{0,4},{4,0},{8,12},{12,8},{16,20},{20,16},{24,28},{28,24},{1,5},{5... | collective-permute-start | bytes 1990664 | tf_op jit(solution)/shard_map/ppermute | solution.py:212
  41.5 16.3 %collective-permute-start.4 = (bf16[288,1152]{1,0:T(8,128)(2,1)S(1)}, bf16[288,1152]{1,0:T(8,128)(2,1)S(1)}, u32[]{:S(2)}, u32[]{:S(2)}) collective-permute-start(bf16[288,1152]{1,0:T(8,128)(2,1)S(1)} %pad_maximum_fusion), channel_id=1, source_target_pairs={{0,4},{4,0},{8,12},{12,8},{16,20},{20,16},{24,28},{28,24},{1,5},{5... | collective-permute-start | bytes 1990664 | tf_op jit(solution)/shard_map/ppermute | solution.py:212

commit v2 on v0

v2 whole, which is shorter than its diff:
```python
import functools

import jax
import jax.numpy as jnp
from jax import lax
from jax.experimental import pallas as pl
from jax.experimental.pallas import tpu as pltpu
from jax.sharding import PartitionSpec as P

BS = 69
LANES = 128
UNIT = 72
PACK = 16
DEPTH = 256
SLOT = 80


def up(n, m):
    return (n + m - 1) // m * m


def moved(load, start, at, width):
    base = start // LANES
    off = start - base * LANES
    first = load(base)
    second = load(base + 1)
    lane_at = at % LANES
    turn = lax.rem(lane_at - off + LANES, LANES)
    first = pltpu.roll(first, turn, 1)
    second = pltpu.roll(second, turn, 1)
    lane = lax.broadcasted_iota(jnp.int32, first.shape, 1)
    pieces = []
    tile = at // LANES
    lo, hi = lane_at, min(lane_at + width, LANES)
    pieces.append((tile, jnp.where(lane < LANES - off + lane_at, first, second), lo, hi))
    if lane_at + width > LANES:
        pieces.append((tile + 1, jnp.where(lane < lane_at - off, first, second), 0, lane_at + width - LANES))
    return pieces


def limit(need):
    return pltpu.CompilerParams(vmem_limit_bytes=min(need + 8 * 2**20, 60 * 2**20))


def crossed(mask):
    return (1 ^ mask[1], 1 ^ mask[0])


def tie(values):
    arrays = [v[0] if isinstance(v, tuple) else v for v in values]
    arrays = lax.optimization_barrier(tuple(arrays))
    return tuple((a, v[1]) if isinstance(v, tuple) else a for a, v in zip(arrays, values))


def right_kernel(n_col, steps, scalars, raw, *refs):
    outs, rows = refs[-1 - len(steps) : -1], refs[-1]
    rows[: raw.shape[0], : raw.shape[1]] = raw[...]
    width = outs[0].shape[1]
    here = scalars.shape[1] // n_col
    me = lax.axis_index("col")
    shape = (UNIT, LANES)
    lane = lax.broadcasted_iota(jnp.int32, shape, 1)
    real = lax.broadcasted_iota(jnp.int32, shape, 0) < BS

    def load(tile):
        return rows[:, pl.ds(pl.multiple_of(tile * LANES, LANES), LANES)].astype(jnp.float32)

    for out, step in zip(outs, steps):
        tiles = [jnp.zeros(shape, jnp.float32) for _ in range(width // LANES)]
        for t in range(here):
            source = scalars[0, (me ^ step) * here + t]
            keep = real & (jnp.full(shape, scalars[1, source]) > 0)
            for tile, value, lo, hi in moved(load, source * BS, t * BS, BS):
                tiles[tile] = jnp.where((lane >= lo) & (lane < hi) & keep, value, tiles[tile])
        for at, value in enumerate(tiles):
            out[:, at * LANES : (at + 1) * LANES] = value.astype(jnp.bfloat16)


def right_units(scalars, owned_rows, n_col, steps, after=()):
    columns = owned_rows.shape[1]
    width = up(columns // n_col, LANES)
    return pl.pallas_call(
        functools.partial(right_kernel, n_col, steps),
        out_shape=[jax.ShapeDtypeStruct((UNIT, width), jnp.bfloat16)] * len(steps),
        in_specs=[pl.BlockSpec(memory_space=pltpu.SMEM)] + [pl.BlockSpec(memory_space=pltpu.VMEM)] * (1 + len(after)),
        out_specs=[pl.BlockSpec(memory_space=pltpu.VMEM)] * len(steps),
        scratch_shapes=[pltpu.VMEM((UNIT, up(columns, LANES) + LANES), jnp.bfloat16)],
        compiler_params=limit(2**22),
        cost_estimate=pl.CostEstimate(flops=8 * 10**9, bytes_accessed=0, transcendentals=0),
        name="right_units",
    )(scalars, owned_rows, *after)


def left_kernel(high, pattern, rows_in, out, rows, sems):
    height, columns = rows_in.shape
    block_rows, depth = pattern.shape
    width = out.shape[1]
    count = height // high

    def copy(i):
        return pltpu.make_async_copy(rows_in.at[pl.ds(i * high, high), :], rows.at[pl.ds(i * high, high), :], sems.at[i])

    for i in range(count):
        copy(i).start()
    lane = lax.broadcasted_iota(jnp.int32, (depth, width), 1)
    block = lax.broadcasted_iota(jnp.int32, (depth, width), 0) * BS
    spread = jnp.where((lane >= block) & (lane < block + BS), 1.0, 0.0).astype(jnp.bfloat16)
    by_block = jnp.dot(pattern[...].astype(jnp.bfloat16), spread, preferred_element_type=jnp.float32)
    for at in range(0, width, LANES):
        wide = min(LANES, columns - at)
        if wide <= 0:
            out[:, at:] = jnp.zeros((height, width - at), jnp.bfloat16)
            break
        if wide < LANES:
            out[:, at : at + LANES] = jnp.zeros((height, LANES), jnp.bfloat16)
    row = lax.broadcasted_iota(jnp.int32, (PACK, columns), 0)
    keeps = {}

    def keep(b):
        if b not in keeps:
            keeps.clear()
            keeps[b] = jnp.broadcast_to(by_block[b : b + 1, :columns], (PACK, columns)).astype(jnp.bfloat16)
        return keeps[b]

    for first in range(0, height, PACK):
        if first % high == 0:
            copy(first // high).wait()
        own, edge = first // BS, (first // BS + 1) * BS
        mask = keep(own)
        if edge < first + PACK:
            mask = jnp.where(row < edge - first, mask, keep(own + 1))
        out[first : first + PACK, :columns] = rows[first : first + PACK, :] * mask


def left_side(slab_rows, slab_pattern, width):
    height, columns = slab_rows.shape
    high = 368
    return pl.pallas_call(
        functools.partial(left_kernel, high),
        out_shape=jax.ShapeDtypeStruct((height, width), jnp.bfloat16),
        in_specs=[pl.BlockSpec(memory_space=pltpu.VMEM), pl.BlockSpec(memory_space=pltpu.HBM)],
        out_specs=pl.BlockSpec(memory_space=pltpu.VMEM),
        scratch_shapes=[pltpu.VMEM((height, columns), jnp.bfloat16), pltpu.SemaphoreType.DMA((height // high,))],
        compiler_params=limit(height * (width + columns) * 2),
        cost_estimate=pl.CostEstimate(flops=1, bytes_accessed=1, transcendentals=0),
        name="left_side",
    )(slab_pattern, slab_rows)


def place(slot):
    return slot // 3 * DEPTH + slot % 3 * SLOT


def side_kernel(n_col, groups, left, point, *refs):
    outs, pick = refs[: len(groups)], refs[-1]
    high = 368
    col = lax.broadcasted_iota(jnp.int32, (DEPTH, DEPTH), 1)
    ahead = lax.broadcasted_iota(jnp.int32, (DEPTH, DEPTH), 0) - col
    turn = 0
    for out, slots in zip(outs, groups):
        for first in range(0, len(slots), 3):
            tiles = []
            base = turn % 2 * 3 * DEPTH
            turn += 1
            for t, (mask, step) in enumerate(slots[first : first + 3]):
                start = block_of(n_col, mask, step) * BS
                tile = start // LANES
                tiles.append(pl.multiple_of(tile * LANES, LANES))
                at = t * SLOT
                hit = (ahead == start - tile * LANES - at) & (col >= at) & (col < at + BS)
                pick[base + t * DEPTH : base + (t + 1) * DEPTH, :] = jnp.where(hit, 1.0, 0.0).astype(jnp.bfloat16)
            for at in range(0, left.shape[0], high):
                total = None
                for t, tile in enumerate(tiles):
                    some = pick[base + t * DEPTH : base + (t + 1) * DEPTH, :]
                    part = jnp.dot(left[at : at + high, pl.ds(tile, DEPTH)], some, preferred_element_type=jnp.float32)
                    total = part if total is None else total + part
                out[at : at + high, first // 3 * DEPTH : (first // 3 + 1) * DEPTH] = total.astype(jnp.bfloat16)


def sides(left, n_col, groups, point):
    height = left.shape[0]
    widths = [up(len(slots), 3) // 3 * DEPTH for slots in groups]
    return pl.pallas_call(
        functools.partial(side_kernel, n_col, groups),
        out_shape=[jax.ShapeDtypeStruct((height, width), jnp.bfloat16) for width in widths],
        in_specs=[pl.BlockSpec(memory_space=pltpu.VMEM), pl.BlockSpec(memory_space=pl.ANY)],
        out_specs=[pl.BlockSpec(memory_space=pltpu.VMEM)] * len(groups),
        scratch_shapes=[pltpu.VMEM((6 * DEPTH, DEPTH), jnp.bfloat16)],
        compiler_params=limit(height * (sum(widths) + left.shape[1]) * 2),
        cost_estimate=pl.CostEstimate(flops=1, bytes_accessed=1, transcendentals=0),
        name="sides",
    )(left, point)


def block_of(n_col, mask, step):
    me = lax.axis_index("row")
    return (me ^ jnp.where(me & 1 == 0, mask[0], mask[1])) * n_col + (lax.axis_index("col") ^ step)


def listed(units):
    pieces, places = [], []
    for piece, *_ in units:
        at = next((i for i, p in enumerate(pieces) if p is piece), None)
        if at is None:
            at = len(pieces)
            pieces.append(piece)
        places.append(at)
    return pieces, places


def multiply_kernel(places, with_total, final, left, *refs):
    out, right = refs[len(refs) - 4 :][:2] if final else refs[-2:]
    pieces = refs[with_total:]
    right[...] = jnp.zeros_like(right)
    for slot, (piece, unit) in enumerate(places):
        right[place(slot) : place(slot) + UNIT, :] = pieces[piece][unit * UNIT : (unit + 1) * UNIT, :]
    high = 368
    copies = []
    for at in range(0, left.shape[0], high):
        value = jnp.dot(left[at : at + high, :], right[...], preferred_element_type=jnp.float32)
        if with_total:
            value += refs[0][at : at + high, :]
        if final:
            tiles, sems = refs[-2:]
            tiles[at : at + high, :] = value[:, : tiles.shape[1]].astype(tiles.dtype)
            copies.append(pltpu.make_async_copy(tiles.at[pl.ds(at, high)], out.at[pl.ds(at, high)], sems.at[at // high]))
            copies[-1].start()
        else:
            out[at : at + high, :] = value
    for copy in copies:
        copy.wait()


def multiply(left, total, units, columns=None, after=()):
    height, width = left.shape
    final = columns is not None
    pieces, places = listed(units)
    wide = pieces[0].shape[1]
    operands = [left] + ([] if total is None else [total]) + pieces
    memory = [pltpu.VMEM] * len(operands) + [pl.ANY] * len(after)
    scratch = [pltpu.VMEM((width, wide), jnp.bfloat16)]
    if final:
        scratch += [pltpu.VMEM((height, columns), jnp.bfloat16), pltpu.SemaphoreType.DMA((height // 368,))]
    return pl.pallas_call(
        functools.partial(multiply_kernel, [(at, unit[1]) for at, unit in zip(places, units)], total is not None, final),
        out_shape=jax.ShapeDtypeStruct((height, columns if final else wide), jnp.bfloat16 if final else jnp.float32),
        in_specs=[pl.BlockSpec(memory_space=space) for space in memory],
        out_specs=pl.BlockSpec(memory_space=pltpu.HBM if final else pltpu.VMEM),
        scratch_shapes=scratch,
        input_output_aliases={} if final or total is None else {1: 0},
        compiler_params=limit(width * wide * 2 + height * (wide * 6 + width * 2) + sum(p.size for p in pieces) * 2),
        cost_estimate=pl.CostEstimate(flops=1, bytes_accessed=1, transcendentals=0),
        name="multiply",
    )(*operands, *after)


def mark_kernel(value, out):
    pass


def mark(value, weight=3):
    return pl.pallas_call(
        mark_kernel,
        out_shape=jax.ShapeDtypeStruct(value.shape, value.dtype),
        in_specs=[pl.BlockSpec(memory_space=pl.ANY)],
        out_specs=pl.BlockSpec(memory_space=pl.ANY),
        input_output_aliases={0: 0},
        compiler_params=pltpu.CompilerParams(vmem_limit_bytes=2**20),
        cost_estimate=pl.CostEstimate(flops=weight * 10**9, bytes_accessed=1, transcendentals=0),
        name="mark",
    )(value)


def per_device(n_row, n_col, slab_rows, slab_pattern, owned_rows, owned_pattern, placement):
    columns = owned_rows.shape[1] // n_col
    bits = [1 << b for b in range(1, n_row.bit_length() - 1)]
    moves = list(zip(bits, bits[::-1]))
    last, deep = n_col - 1, len(moves)

    def along_row(value, move):
        return lax.ppermute(value, "row", [(i, i ^ move[i & 1]) for i in range(n_row)])

    def along_col(value, step):
        return lax.ppermute(value, "col", [(i, i ^ step) for i in range(n_col)])

    masks = [(0, 0)]
    for move in moves:
        masks += [(m[0] ^ move[0], m[1] ^ move[1]) for m in masks]

    full = len(masks) - 1

    def unit_of(key):
        value, unit = pieces[key]
        return value if value.shape[0] == UNIT else value[unit * UNIT : (unit + 1) * UNIT]

    def joined(keys):
        value = pieces[keys[0]][0]
        if value.shape[0] == UNIT * len(keys) and all(pieces[k][0] is value and pieces[k][1] == i for i, k in enumerate(keys)):
            return value
        return jnp.concatenate([unit_of(key) for key in keys]) if len(keys) > 1 else unit_of(keys[0])

    def hop(at, keys):
        sent = along_row(joined(keys), moves[at])
        for unit, (step, way) in enumerate(keys):
            pieces[step, way | 1 << at] = (sent, unit)

    def swap(keys):
        other = along_row(joined(keys), (1, 1))
        for unit, key in enumerate(keys):
            swaps[key] = (other, unit)

    def tied(keys, swapped, extra):
        sets = [(pieces, key) for key in keys] + [(swaps, key) for key in swapped]
        arrays = []
        for held, key in sets:
            if not any(held[key][0] is a for a in arrays):
                arrays.append(held[key][0])
        new = lax.optimization_barrier((*arrays, *extra))
        for old, fresh in zip(arrays, new):
            for held in (pieces, swaps):
                for key, (value, unit) in held.items():
                    if value is old:
                        held[key] = (fresh, unit)
        return new[len(arrays) :]

    ways = list(range(len(masks)))
    first, rest = [0, 1], list(range(2, n_col))
    scalars = jnp.concatenate([placement[None], owned_pattern])
    units = right_units(scalars, owned_rows, n_col, list(range(n_col)))

    pieces, swaps = {(0, 0): (units[0], 0)}, {}
    for step in range(1, n_col):
        pieces[step, 0] = (along_col(units[step], step), 0)

    def brought_by(step, way):
        return (step not in first) + way.bit_count() - 1

    def wave(number):
        for at in range(deep):
            keys = [(step, way) for step in rest + first for way in range(1 << at)]
            keys = [key for key in keys if brought_by(*key) == number - 1]
            if keys:
                hop(at, keys)

    def come(number):
        return [(step, way) for step in rest + first for way in ways[1:] if brought_by(step, way) == number]

    def own(keys):
        return [(*pieces[step, way], masks[way], step) for step, way in keys]

    def other(keys):
        return [(*swaps[step, way], crossed(masks[way]), step) for step, way in keys]

    def slots(keys, swapped):
        return [(masks[way], step) for step, way in keys] + [(crossed(masks[way]), step) for step, way in swapped]

    early = [(step, 0) for step in first] + come(0)
    arrived = [(step, 0) for step in rest]
    late = sum([come(number) for number in range(1, deep)], [])
    tail = come(deep)
    ready = early + arrived
    soon = [key for key in late if key[1] <= full // 2 and key[0] in rest]
    then = [key for key in late if key not in soon]
    groups = [(ready, []), (late, ready), ([], late), (tail, tail)]

    left = left_side(slab_rows, slab_pattern, up(slab_rows.shape[1], 2 * LANES))
    left, point = tied([(1, 0)], [], [left, scalars])
    point = mark(point)
    (point,) = tied([(0, 0), (1, 0)], [], [point])
    wave(0)
    (ready_left,) = sides(left, n_col, [slots(*groups[0])], point)
    ready_left, left, point = tied(arrived, [], [ready_left, left, point])
    point = mark(point)
    (point,) = tied(come(0), [], [point])
    for number in range(1, deep):
        wave(number)
    swap(ready)
    lefts = sides(left, n_col, [slots(*group) for group in groups[1:]], point)
    total = multiply(ready_left, None, own(ready))
    total, point, *lefts = tied(soon, [], [total, point, *lefts])
    wave(deep)
    total, point = tied(then, [], [total, point])
    point = mark(point, 10)
    (point,) = tied([], ready, [point])
    swap(late)
    total = multiply(lefts[0], total, own(late) + other(ready), after=[point])
    total, point = tied(tail, [], [total, point])
    swap(tail)
    point = mark(point)
    (point,) = tied([], late, [point])
    total = multiply(lefts[1], total, other(late), after=[point])
    return multiply(lefts[2], total, own(tail) + other(tail), columns)


def solution(mesh):
    return jax.shard_map(
        functools.partial(per_device, mesh.shape["row"], mesh.shape["col"]),
        mesh=mesh,
        in_specs=(
            P("row", None),
            P("row", None),
            P(("row", "col"), None),
            P(("row", "col"), None),
            P(),
        ),
        out_specs=P("row", "col"),
        check_vma=False,
    )
```

time: 108 us -> 45.5 us (0.42)
  local copies, waits for them, and re-layouts: 36.6 us -> 1.53 us
  blocking collectives: 23.6 us -> 0 us
  Pallas kernels: 0 us -> 19.6 us
  starting transfers between devices: 0.01 us -> 14.7 us
  between operations: 13.5 us -> 0.18 us
  matrix products: 12 us -> 0 us
  waiting for transfers between devices: 18.8 us -> 8.22 us
  other arithmetic: 3.19 us -> 0.99 us
    all_to_all x1 -> x0, blocking collectives: 23.6 us -> none  [per_device(): lax.all_to_all(owned_blocks, 'col', split_axis=1, concat_axis=0, tiled=True)]
    mul x2 -> x0, local copies, waits for them, and re-layouts: 21.2 us -> none  [per_device(): slab_rows.reshape(rows_here, BS, depth_blocks, BS) * slab_mask]
    pallas_call x0 -> x12, Pallas kernels: none -> 19.6 us  [the longest x4 11.5 us: multiply(): pl.pallas_call(functools.partial(multiply_kernel, [(at, unit[1]) for at,...]
    all_gather x1 -> x0, waiting for transfers between devices: 18.8 us -> none  [per_device(): lax.all_gather(panel_here, 'row', axis=0, tiled=True)]
    ppermute x0 -> x11, starting transfers between devices: none -> 14.7 us  [the longest x8 9.02 us: along_row(): lax.ppermute(value, 'row', [(i, i ^ move[i & 1]) for i in range(n_row)])]
    dot_general x1 -> x0, matrix products: 12 us -> none  [per_device(): jnp.dot(slab_full, lax.all_gather(panel_here, 'row', axis=0, tiled=True),...]
    ppermute x0 -> x11, waiting for transfers between devices: none -> 8.22 us  [the longest x3 6.33 us: along_col(): return lax.ppermute(value, 'col', [(i, i ^ step) for i in range(n_col)])]
    unnamed x4 -> x15, local copies, waits for them, and re-layouts: 7.32 us -> 1.43 us
  transfers between devices with their start and end apart: 1 -> 11, of which waited for: 1 -> 4; matrix products, arithmetic and copies ran while one was open for 20% -> 1% of each run, Pallas kernels for 0% -> 34%
where the time goes in v2:
time: 45.5 us; the launch traced here: 45.3 us
  Pallas kernels  19.6 us (43%)
  starting transfers between devices  14.7 us (32%)
  waiting for transfers between devices  8.22 us (18%)
  local copies, waits for them, and re-layouts  1.53 us (3%)
  other arithmetic  0.99 us (2%)
    pallas_call x4, Pallas kernels, multiply(): pl.pallas_call(functools.partial(multiply_kernel, [(at, unit[1]) for at,...  11.5 us
    ppermute x8, starting transfers between devices, along_row(): lax.ppermute(value, 'row', [(i, i ^ move[i & 1]) for i in range(n_row)])  9.02 us
    ppermute x3, waiting for transfers between devices, along_col(): return lax.ppermute(value, 'col', [(i, i ^ step) for i in range(n_col)])  6.33 us
    ppermute x3, starting transfers between devices, along_col(): return lax.ppermute(value, 'col', [(i, i ^ step) for i in range(n_col)])  5.68 us
    pallas_call x2, Pallas kernels, sides(): pl.pallas_call(functools.partial(side_kernel, n_col, groups), out_shape=[...  5.14 us
    ppermute x8, waiting for transfers between devices, along_row(): lax.ppermute(value, 'row', [(i, i ^ move[i & 1]) for i in range(n_row)])  1.89 us
    pallas_call x1, Pallas kernels, left_side(): pl.pallas_call(functools.partial(left_kernel, high), out_shape=jax.ShapeD...  1.48 us
    pallas_call x1, Pallas kernels, right_units(): pl.pallas_call(functools.partial(right_kernel, n_col, steps), out_shape=[...  1.48 us
  transfers between devices with their start and end apart: 11, of which 4 were waited for; matrix products, arithmetic and copies ran while one was open for 1% of the time, Pallas kernels for 34%

profile of v2, /device:TPU:0, one launch (start us, length us, event | category | flops | bytes accessed | tf_op | source)
XLA Modules:
  0.0 45.3 jit_solution(11676416095666121888)
XLA Ops:
  0.0 0.0 slice-start
  0.0 0.8 %pad_add_fusion.scalars.value = s32[2,64]{1,0:T(2,128)S(1)} fusion(s32[1,64]{1,0:T(1,128)} %param.8, s32[1,64]{1,0:T(1,128)} %bitcast.3), kind=kLoop, calls=%fused_computation.13 | loop fusion | flops 128 | bytes 1024 | tf_op jit(solution)/shard_map/concatenate | solution.py:329
  0.8 0.0 copy-start.1
  0.8 1.3 %copy-done.1 = bf16[69,4416]{1,0:T(8,128)(2,1)S(1)} copy-done((bf16[69,4416]{1,0:T(8,128)(2,1)S(1)}, bf16[69,4416]{1,0:T(8,128)(2,1)}, u32[]{:S(2)}) %copy-start.1) | copy-done | bytes 609432
  2.1 0.0 slice-start.1
  2.1 0.0 copy-start
  2.1 1.5 %right_units.1 = (bf16[72,1152]{1,0:T(8,128)(2,1)S(1)}, bf16[72,1152]{1,0:T(8,128)(2,1)S(1)}, bf16[72,1152]{1,0:T(8,128)(2,1)S(1)}, bf16[72,1152]{1,0:T(8,128)(2,1)S(1)}) custom-call(s32[2,64]{1,0:T(2,128)S(1)} %pad_add_fusion.scalars.value, bf16[69,4416]{1,0:T(8,128)(2,1)S(1)} %copy-done.1), custom_call_target="tpu_custom_call" | custom-call | flops 8000000000 | tf_op jit(solution)/shard_map/right_units/pallas_call | solution.py:82
  3.6 3.1 %collective-permute-start.2 = (bf16[72,1152]{1,0:T(8,128)(2,1)S(1)}, bf16[72,1152]{1,0:T(8,128)(2,1)S(1)}, u32[]{:S(2)}, u32[]{:S(2)}) collective-permute-start(bf16[72,1152]{1,0:T(8,128)(2,1)S(1)} %get-tuple-element.44), channel_id=1, source_target_pairs={{0,1},{1,0},{2,3},{3,2},{4,5},{5,4},{6,7},{7,6},{8,9},{9,8},{10,11... | collective-permute-start | bytes 497672 | tf_op jit(solution)/shard_map/ppermute | solution.py:285
  6.7 2.6 %collective-permute-start = (bf16[72,1152]{1,0:T(8,128)(2,1)S(1)}, bf16[72,1152]{1,0:T(8,128)(2,1)S(1)}, u32[]{:S(2)}, u32[]{:S(2)}) collective-permute-start(bf16[72,1152]{1,0:T(8,128)(2,1)S(1)} %get-tuple-element.42), channel_id=1, source_target_pairs={{0,2},{1,3},{2,0},{3,1},{4,6},{5,7},{6,4},{7,5},{8,10},{9,11},{10,... | collective-permute-start | bytes 497672 | tf_op jit(solution)/shard_map/ppermute | solution.py:285
  9.3 0.0 collective-permute-start.1
  9.3 0.0 slice-done
  9.3 0.0 slice-done.1
  9.3 0.0 copy-done
  9.3 1.5 %left_side.1.left = bf16[1104,2304]{1,0:T(8,128)(2,1)S(1)} custom-call(s32[16,32]{1,0:T(8,128)S(1)} %copy-done, bf16[1104,2208]{1,0:T(8,128)(2,1)S(1)} %bitcast.2), custom_call_target="tpu_custom_call" | custom-call | flops 1 | bytes 1 | tf_op jit(solution)/shard_map/left_side/pallas_call | solution.py:138
  10.8 2.7 %collective-permute-done.2.refs_1_ = bf16[72,1152]{1,0:T(8,128)(2,1)S(1)} collective-permute-done((bf16[72,1152]{1,0:T(8,128)(2,1)S(1)}, bf16[72,1152]{1,0:T(8,128)(2,1)S(1)}, u32[]{:S(2)}, u32[]{:S(2)}) %collective-permute-start.2) | collective-permute-done | bytes 165920 | tf_op jit(solution)/shard_map/ppermute | solution.py:285
  13.5 1.8 %collective-permute-start.5 = (bf16[144,1152]{1,0:T(8,128)(2,1)S(1)}, bf16[144,1152]{1,0:T(8,128)(2,1)S(1)}, u32[]{:S(2)}, u32[]{:S(2)}) collective-permute-start(bf16[144,1152]{1,0:T(8,128)(2,1)S(1)} %get-tuple-element.82), channel_id=1, source_target_pairs={{0,16},{4,12},{8,24},{12,4},{16,0},{20,28},{24,8},{28,20},{1,17},{... | collective-permute-start | bytes 995336 | tf_op jit(solution)/shard_map/ppermute | solution.py:282
  15.3 1.5 %collective-permute-start.4 = (bf16[144,1152]{1,0:T(8,128)(2,1)S(1)}, bf16[144,1152]{1,0:T(8,128)(2,1)S(1)}, u32[]{:S(2)}, u32[]{:S(2)}) collective-permute-start(bf16[144,1152]{1,0:T(8,128)(2,1)S(1)} %get-tuple-element.82), channel_id=1, source_target_pairs={{0,8},{4,20},{8,0},{12,28},{16,24},{20,4},{24,16},{28,12},{1,9},{5... | collective-permute-start | bytes 995336 | tf_op jit(solution)/shard_map/ppermute | solution.py:282
  16.8 1.4 %sides.2.left = bf16[1104,768]{1,0:T(8,128)(2,1)S(1)} custom-call(bf16[1104,2304]{1,0:T(8,128)(2,1)S(1)} %left_side.1.left, s32[2,64]{1,0:T(2,128)S(1)} %mark.4.point.value), custom_call_target="tpu_custom_call" | custom-call | flops 1 | bytes 1 | tf_op jit(solution)/shard_map/sides/pallas_call | solution.py:184
  18.2 3.7 %collective-permute-done.refs_4_ = bf16[72,1152]{1,0:T(8,128)(2,1)S(1)} collective-permute-done((bf16[72,1152]{1,0:T(8,128)(2,1)S(1)}, bf16[72,1152]{1,0:T(8,128)(2,1)S(1)}, u32[]{:S(2)}, u32[]{:S(2)}) %collective-permute-start) | collective-permute-done | bytes 165920 | tf_op jit(solution)/shard_map/ppermute | solution.py:285
  21.8 0.0 collective-permute-done.1.refs_5_
  21.9 1.6 %collective-permute-start.3 = (bf16[144,1152]{1,0:T(8,128)(2,1)S(1)}, bf16[144,1152]{1,0:T(8,128)(2,1)S(1)}, u32[]{:S(2)}, u32[]{:S(2)}) collective-permute-start(bf16[144,1152]{1,0:T(8,128)(2,1)S(1)} %pad_maximum_fusion.2), channel_id=1, source_target_pairs={{0,8},{4,20},{8,0},{12,28},{16,24},{20,4},{24,16},{28,12},{1,9},{5... | collective-permute-start | bytes 995336 | tf_op jit(solution)/shard_map/ppermute | solution.py:282
  23.4 0.8 %collective-permute-done.5.refs_3_ = bf16[144,1152]{1,0:T(8,128)(2,1)S(1)} collective-permute-done((bf16[144,1152]{1,0:T(8,128)(2,1)S(1)}, bf16[144,1152]{1,0:T(8,128)(2,1)S(1)}, u32[]{:S(2)}, u32[]{:S(2)}) %collective-permute-start.5) | collective-permute-done | bytes 331808 | tf_op jit(solution)/shard_map/ppermute | solution.py:282
  24.2 0.0 collective-permute-done.4.refs_2_
  24.2 0.1 pad_maximum_fusion.1
  24.4 1.8 %collective-permute-start.7 = (bf16[288,1152]{1,0:T(8,128)(2,1)S(1)}, bf16[288,1152]{1,0:T(8,128)(2,1)S(1)}, u32[]{:S(2)}, u32[]{:S(2)}) collective-permute-start(bf16[288,1152]{1,0:T(8,128)(2,1)S(1)} %pad_maximum_fusion.1), channel_id=1, source_target_pairs={{0,16},{4,12},{8,24},{12,4},{16,0},{20,28},{24,8},{28,20},{1,17},{... | collective-permute-start | bytes 1990664 | tf_op jit(solution)/shard_map/ppermute | solution.py:282
  26.3 0.1 collective-permute-start.8
  26.4 2.4 %multiply.4.refs_0_ = f32[1104,1152]{1,0:T(8,128)S(1)} custom-call(bf16[1104,768]{1,0:T(8,128)(2,1)S(1)} %sides.2.left, bf16[72,1152]{1,0:T(8,128)(2,1)S(1)} %get-tuple-element.53.refs_0_, bf16[72,1152]{1,0:T(8,128)(2,1)S(1)} %collective-permute-done.2.refs_1_, bf16[144,1152]{1,0:T(8,128)(2,1)S(1)} %collective-permute-done.4.refs_2_, ...), custom_call_target="tpu_custom_call" | custom-call | flops 1 | bytes 1 | tf_op jit(solution)/shard_map/multiply/pallas_call | solution.py:245
  28.8 3.8 %sides.3 = (bf16[1104,1280]{1,0:T(8,128)(2,1)S(1)}, bf16[1104,512]{1,0:T(8,128)(2,1)S(1)}, bf16[1104,512]{1,0:T(8,128)(2,1)S(1)}) custom-call(bf16[1104,2304]{1,0:T(8,128)(2,1)S(1)} %left_side.1.left, s32[2,64]{1,0:T(2,128)S(1)} %mark.5.point.value), custom_call_target="tpu_custom_call" | custom-call | flops 1 | bytes 1 | tf_op jit(solution)/shard_map/sides/pallas_call | solution.py:184
  32.6 0.0 collective-permute-done.3.refs_1_
  32.6 1.5 %collective-permute-start.6 = (bf16[144,1152]{1,0:T(8,128)(2,1)S(1)}, bf16[144,1152]{1,0:T(8,128)(2,1)S(1)}, u32[]{:S(2)}, u32[]{:S(2)}) collective-permute-start(bf16[144,1152]{1,0:T(8,128)(2,1)S(1)} %collective-permute-done.3.refs_1_), channel_id=1, source_target_pairs={{0,16},{4,12},{8,24},{12,4},{16,0},{20,28},{24,8},{28,20},{1,17},{... | collective-permute-start | bytes 995336 | tf_op jit(solution)/shard_map/ppermute | solution.py:282
  34.2 1.0 %collective-permute-done.7.refs_2_ = bf16[288,1152]{1,0:T(8,128)(2,1)S(1)} collective-permute-done((bf16[288,1152]{1,0:T(8,128)(2,1)S(1)}, bf16[288,1152]{1,0:T(8,128)(2,1)S(1)}, u32[]{:S(2)}, u32[]{:S(2)}) %collective-permute-start.7) | collective-permute-done | bytes 663584 | tf_op jit(solution)/shard_map/ppermute | solution.py:282
  35.2 0.1 pad_maximum_fusion
  35.3 0.7 %collective-permute-start.9 = (bf16[432,1152]{1,0:T(8,128)(2,1)S(1)}, bf16[432,1152]{1,0:T(8,128)(2,1)S(1)}, u32[]{:S(2)}, u32[]{:S(2)}) collective-permute-start(bf16[432,1152]{1,0:T(8,128)(2,1)S(1)} %pad_maximum_fusion), channel_id=1, source_target_pairs={{0,4},{4,0},{8,12},{12,8},{16,20},{20,16},{24,28},{28,24},{1,5},{5... | collective-permute-start | bytes 2985992 | tf_op jit(solution)/shard_map/ppermute | solution.py:282
  36.0 0.0 collective-permute-done.8.refs_3_
  36.0 4.4 %multiply.5.refs_0_ = f32[1104,1152]{1,0:T(8,128)S(1)} custom-call(bf16[1104,1280]{1,0:T(8,128)(2,1)S(1)} %get-tuple-element.66.left, f32[1104,1152]{1,0:T(8,128)S(1)} %multiply.4.refs_0_, bf16[144,1152]{1,0:T(8,128)(2,1)S(1)} %collective-permute-done.3.refs_1_, ...), custom_call_target="tpu_custom_call", output_to_operand_aliasing={{}: (1, {})} | custom-call | flops 1 | bytes 1 | tf_op jit(solution)/shard_map/multiply/pallas_call | solution.py:245
  40.4 0.0 collective-permute-done.6.refs_1_
  40.4 0.1 collective-permute-start.10
  40.5 0.0 collective-permute-done.9.refs_1_
  40.5 2.0 %multiply.6.refs_0_ = f32[1104,1152]{1,0:T(8,128)S(1)} custom-call(bf16[1104,512]{1,0:T(8,128)(2,1)S(1)} %get-tuple-element.64.left, f32[1104,1152]{1,0:T(8,128)S(1)} %multiply.5.refs_0_, bf16[432,1152]{1,0:T(8,128)(2,1)S(1)} %collective-permute-done.9.refs_1_, s32[2,64]{1,0:T(2,128)S(1)} %mark.7.refs_2_), custom_call_target="tpu_custom_call", output_to_operand_aliasing={{}: (1, {})} | custom-call | flops 1 | bytes 1 | tf_op jit(solution)/shard_map/multiply/pallas_call | solution.py:245
  42.6 0.0 collective-permute-done.10.refs_2_
  42.6 2.7 %multiply.7 = bf16[1104,1104]{1,0:T(8,128)(2,1)} custom-call(bf16[1104,512]{1,0:T(8,128)(2,1)S(1)} %get-tuple-element.63.left, f32[1104,1152]{1,0:T(8,128)S(1)} %multiply.6.refs_0_, bf16[144,1152]{1,0:T(8,128)(2,1)S(1)} %collective-permute-done.6.refs_1_, bf16[144,1152]{1,0:T(8,128)(2,1)S(1)} %collective-permute-done.10.refs_2_), custom_call_target="tpu_custom_call" | custom-call | flops 1 | bytes 1 | tf_op jit(solution)/shard_map/multiply/pallas_call | solution.py:245
  (17 shorter events, 0.3 us)
Async XLA Ops:
  0.0 9.3 %slice-start = ((s8[5087232]{0:T(1024)(128)(4,1)}), s8[4194304]{0:T(1024)(128)(4,1)S(1)}, s32[]{:S(2)}) async-start(s8[5087232]{0:T(1024)(128)(4,1)} %bitcast.1), calls=%async_computation | async-start | bytes 8388608
  0.8 1.3 %copy-start.1 = (bf16[69,4416]{1,0:T(8,128)(2,1)S(1)}, bf16[69,4416]{1,0:T(8,128)(2,1)}, u32[]{:S(2)}) copy-start(bf16[69,4416]{1,0:T(8,128)(2,1)} %raw.1) | copy-start | bytes 1828228
  2.1 7.2 %slice-start.1 = ((s8[5087232]{0:T(1024)(128)(4,1)}), s8[892928]{0:T(1024)(128)(4,1)S(1)}, s32[]{:S(2)}) async-start(s8[5087232]{0:T(1024)(128)(4,1)} %bitcast.1), calls=%async_computation.1 | async-start | bytes 1785856
  2.1 7.2 %copy-start = (s32[16,32]{1,0:T(8,128)S(1)}, s32[16,32]{1,0:T(8,128)}, u32[]{:S(2)}) copy-start(s32[16,32]{1,0:T(8,128)} %pattern.1) | copy-start | bytes 6148
  3.6 9.9 %collective-permute-start.2 = (bf16[72,1152]{1,0:T(8,128)(2,1)S(1)}, bf16[72,1152]{1,0:T(8,128)(2,1)S(1)}, u32[]{:S(2)}, u32[]{:S(2)}) collective-permute-start(bf16[72,1152]{1,0:T(8,128)(2,1)S(1)} %get-tuple-element.44), channel_id=1, source_target_pairs={{0,1},{1,0},{2,3},{3,2},{4,5},{5,4},{6,7},{7,6},{8,9},{9,8},{10,11... | collective-permute-start | bytes 497672 | tf_op jit(solution)/shard_map/ppermute | solution.py:285
  6.7 15.2 %collective-permute-start = (bf16[72,1152]{1,0:T(8,128)(2,1)S(1)}, bf16[72,1152]{1,0:T(8,128)(2,1)S(1)}, u32[]{:S(2)}, u32[]{:S(2)}) collective-permute-start(bf16[72,1152]{1,0:T(8,128)(2,1)S(1)} %get-tuple-element.42), channel_id=1, source_target_pairs={{0,2},{1,3},{2,0},{3,1},{4,6},{5,7},{6,4},{7,5},{8,10},{9,11},{10,... | collective-permute-start | bytes 497672 | tf_op jit(solution)/shard_map/ppermute | solution.py:285
  9.3 12.6 %collective-permute-start.1 = (bf16[72,1152]{1,0:T(8,128)(2,1)S(1)}, bf16[72,1152]{1,0:T(8,128)(2,1)S(1)}, u32[]{:S(2)}, u32[]{:S(2)}) collective-permute-start(bf16[72,1152]{1,0:T(8,128)(2,1)S(1)} %get-tuple-element.43), channel_id=1, source_target_pairs={{0,3},{1,2},{2,1},{3,0},{4,7},{5,6},{6,5},{7,4},{8,11},{9,10},{10,... | collective-permute-start | bytes 497672 | tf_op jit(solution)/shard_map/ppermute | solution.py:285
  13.5 10.7 %collective-permute-start.5 = (bf16[144,1152]{1,0:T(8,128)(2,1)S(1)}, bf16[144,1152]{1,0:T(8,128)(2,1)S(1)}, u32[]{:S(2)}, u32[]{:S(2)}) collective-permute-start(bf16[144,1152]{1,0:T(8,128)(2,1)S(1)} %get-tuple-element.82), channel_id=1, source_target_pairs={{0,16},{4,12},{8,24},{12,4},{16,0},{20,28},{24,8},{28,20},{1,17},{... | collective-permute-start | bytes 995336 | tf_op jit(solution)/shard_map/ppermute | solution.py:282
  15.3 8.9 %collective-permute-start.4 = (bf16[144,1152]{1,0:T(8,128)(2,1)S(1)}, bf16[144,1152]{1,0:T(8,128)(2,1)S(1)}, u32[]{:S(2)}, u32[]{:S(2)}) collective-permute-start(bf16[144,1152]{1,0:T(8,128)(2,1)S(1)} %get-tuple-element.82), channel_id=1, source_target_pairs={{0,8},{4,20},{8,0},{12,28},{16,24},{20,4},{24,16},{28,12},{1,9},{5... | collective-permute-start | bytes 995336 | tf_op jit(solution)/shard_map/ppermute | solution.py:282
  21.9 10.7 %collective-permute-start.3 = (bf16[144,1152]{1,0:T(8,128)(2,1)S(1)}, bf16[144,1152]{1,0:T(8,128)(2,1)S(1)}, u32[]{:S(2)}, u32[]{:S(2)}) collective-permute-start(bf16[144,1152]{1,0:T(8,128)(2,1)S(1)} %pad_maximum_fusion.2), channel_id=1, source_target_pairs={{0,8},{4,20},{8,0},{12,28},{16,24},{20,4},{24,16},{28,12},{1,9},{5... | collective-permute-start | bytes 995336 | tf_op jit(solution)/shard_map/ppermute | solution.py:282
  24.4 10.7 %collective-permute-start.7 = (bf16[288,1152]{1,0:T(8,128)(2,1)S(1)}, bf16[288,1152]{1,0:T(8,128)(2,1)S(1)}, u32[]{:S(2)}, u32[]{:S(2)}) collective-permute-start(bf16[288,1152]{1,0:T(8,128)(2,1)S(1)} %pad_maximum_fusion.1), channel_id=1, source_target_pairs={{0,16},{4,12},{8,24},{12,4},{16,0},{20,28},{24,8},{28,20},{1,17},{... | collective-permute-start | bytes 1990664 | tf_op jit(solution)/shard_map/ppermute | solution.py:282
  26.3 9.7 %collective-permute-start.8 = (bf16[576,1152]{1,0:T(8,128)(2,1)S(1)}, bf16[576,1152]{1,0:T(8,128)(2,1)S(1)}, u32[]{:S(2)}, u32[]{:S(2)}) collective-permute-start(bf16[576,1152]{1,0:T(8,128)(2,1)S(1)} %constant_dynamic-update-slice_fusion.2), channel_id=1, source_target_pairs={{0,4},{4,0},{8,12},{12,8},{16,20},{20,16},{24,28},{28,24},{1,5},{5... | collective-permute-start | bytes 3981320 | tf_op jit(solution)/shard_map/ppermute | solution.py:282
  32.6 7.8 %collective-permute-start.6 = (bf16[144,1152]{1,0:T(8,128)(2,1)S(1)}, bf16[144,1152]{1,0:T(8,128)(2,1)S(1)}, u32[]{:S(2)}, u32[]{:S(2)}) collective-permute-start(bf16[144,1152]{1,0:T(8,128)(2,1)S(1)} %collective-permute-done.3.refs_1_), channel_id=1, source_target_pairs={{0,16},{4,12},{8,24},{12,4},{16,0},{20,28},{24,8},{28,20},{1,17},{... | collective-permute-start | bytes 995336 | tf_op jit(solution)/shard_map/ppermute | solution.py:282
  35.3 5.2 %collective-permute-start.9 = (bf16[432,1152]{1,0:T(8,128)(2,1)S(1)}, bf16[432,1152]{1,0:T(8,128)(2,1)S(1)}, u32[]{:S(2)}, u32[]{:S(2)}) collective-permute-start(bf16[432,1152]{1,0:T(8,128)(2,1)S(1)} %pad_maximum_fusion), channel_id=1, source_target_pairs={{0,4},{4,0},{8,12},{12,8},{16,20},{20,16},{24,28},{28,24},{1,5},{5... | collective-permute-start | bytes 2985992 | tf_op jit(solution)/shard_map/ppermute | solution.py:282
  40.4 2.2 %collective-permute-start.10 = (bf16[144,1152]{1,0:T(8,128)(2,1)S(1)}, bf16[144,1152]{1,0:T(8,128)(2,1)S(1)}, u32[]{:S(2)}, u32[]{:S(2)}) collective-permute-start(bf16[144,1152]{1,0:T(8,128)(2,1)S(1)} %collective-permute-done.6.refs_1_), channel_id=1, source_target_pairs={{0,4},{4,0},{8,12},{12,8},{16,20},{20,16},{24,28},{28,24},{1,5},{5... | collective-permute-start | bytes 995336 | tf_op jit(solution)/shard_map/ppermute | solution.py:282

commit v3 on v2

--- a/solution.py
+++ b/solution.py
@@ -9,6 +9,7 @@
 
 BS = 69
 LANES = 128
+BODY = 64
 UNIT = 72
 PACK = 16
 DEPTH = 256
@@ -22,19 +23,14 @@
 def moved(load, start, at, width):
     base = start // LANES
     off = start - base * LANES
-    first = load(base)
-    second = load(base + 1)
+    first, second = load(base), load(base + 1)
+    lane = lax.broadcasted_iota(jnp.int32, first.shape, 1)
     lane_at = at % LANES
-    turn = lax.rem(lane_at - off + LANES, LANES)
-    first = pltpu.roll(first, turn, 1)
-    second = pltpu.roll(second, turn, 1)
-    lane = lax.broadcasted_iota(jnp.int32, first.shape, 1)
-    pieces = []
+    value = pltpu.roll(jnp.where(lane >= off, first, second), lax.rem(lane_at - off + LANES, LANES), 1)
     tile = at // LANES
-    lo, hi = lane_at, min(lane_at + width, LANES)
-    pieces.append((tile, jnp.where(lane < LANES - off + lane_at, first, second), lo, hi))
+    pieces = [(tile, value, lane_at, min(lane_at + width, LANES))]
     if lane_at + width > LANES:
-        pieces.append((tile + 1, jnp.where(lane < lane_at - off, first, second), 0, lane_at + width - LANES))
+        pieces.append((tile + 1, value, 0, lane_at + width - LANES))
     return pieces
 
 
@@ -46,16 +42,80 @@
     return (1 ^ mask[1], 1 ^ mask[0])
 
 
-def tie(values):
-    arrays = [v[0] if isinstance(v, tuple) else v for v in values]
-    arrays = lax.optimization_barrier(tuple(arrays))
-    return tuple((a, v[1]) if isinstance(v, tuple) else a for a, v in zip(arrays, values))
+def unit_size(columns):
+    full, over = columns // LANES, columns % LANES
+    return full * BODY // PACK + pl.cdiv(full, 2) + pl.cdiv(pl.cdiv(3 * over, LANES) * (UNIT // 3), PACK)
+
+
+def pack_unit(out, tiles, columns):
+    full, over = columns // LANES, columns % LANES
+    at = 0
+    for tile in tiles[:full]:
+        for row in range(0, BODY, PACK):
+            out[at] = tile[row : row + PACK].astype(jnp.bfloat16)
+            at += 1
+    for t in range(0, full, 2):
+        pair = [tiles[t][BODY:], tiles[t + 1][BODY:] if t + 1 < full else jnp.zeros_like(tiles[t][BODY:])]
+        out[at] = jnp.concatenate(pair, 0).astype(jnp.bfloat16)
+        at += 1
+    if not over:
+        return
+    third = UNIT // 3
+    lane = lax.broadcasted_iota(jnp.int32, (third, LANES), 1)
+    packed = [jnp.zeros((third, LANES), jnp.float32) for _ in range(pl.cdiv(3 * over, LANES))]
+    for g in range(3):
+        value = tiles[full][g * third : (g + 1) * third]
+        t, shift = g * over // LANES, g * over % LANES
+        if shift:
+            value = pltpu.roll(value, shift, 1)
+        packed[t] = jnp.where((lane >= shift) & (lane < shift + over), value, packed[t])
+        if shift + over > LANES:
+            packed[t + 1] = jnp.where(lane < shift + over - LANES, value, packed[t + 1])
+    rows = jnp.concatenate(packed, 0)
+    if rows.shape[0] % PACK:
+        rows = jnp.concatenate([rows, jnp.zeros((PACK - rows.shape[0] % PACK, LANES), jnp.float32)], 0)
+    for row in range(0, rows.shape[0], PACK):
+        out[at] = rows[row : row + PACK].astype(jnp.bfloat16)
+        at += 1
+
+
+def unpack_unit(right, first, piece, at, columns):
+    full, over = columns // LANES, columns % LANES
+    for t in range(full):
+        for row in range(0, BODY, PACK):
+            right[first + row : first + row + PACK, t * LANES : (t + 1) * LANES] = piece[at]
+            at += 1
+    zero = jnp.zeros((PACK // 2, LANES), jnp.float32)
+    for t in range(0, full, 2):
+        pair = piece[at].astype(jnp.float32)
+        at += 1
+        for k in range(min(2, full - t)):
+            half = jnp.concatenate([pair[k * PACK // 2 : (k + 1) * PACK // 2], zero], 0).astype(jnp.bfloat16)
+            right[first + BODY : first + BODY + PACK, (t + k) * LANES : (t + k + 1) * LANES] = half
+    if not over:
+        return
+    third = UNIT // 3
+    count = pl.cdiv(3 * over, LANES)
+    rows = jnp.concatenate([piece[at + i].astype(jnp.float32) for i in range(pl.cdiv(count * third, PACK))], 0)
+    packed = [rows[i * third : (i + 1) * third] for i in range(count)]
+    lane = lax.broadcasted_iota(jnp.int32, (third, LANES), 1)
+    values = []
+    for g in range(3):
+        t, shift = g * over // LANES, g * over % LANES
+        value = packed[t]
+        if shift:
+            value = pltpu.roll(value, LANES - shift, 1)
+        if shift + over > LANES:
+            value = jnp.where(lane < LANES - shift, value, pltpu.roll(packed[t + 1], LANES - shift, 1))
+        values.append(value)
+    values.append(zero)
+    right[first : first + SLOT, full * LANES : (full + 1) * LANES] = jnp.concatenate(values, 0).astype(jnp.bfloat16)
 
 
 def right_kernel(n_col, steps, scalars, raw, *refs):
     outs, rows = refs[-1 - len(steps) : -1], refs[-1]
     rows[: raw.shape[0], : raw.shape[1]] = raw[...]
-    width = outs[0].shape[1]
+    columns = raw.shape[1] // n_col
     here = scalars.shape[1] // n_col
     me = lax.axis_index("col")
     shape = (UNIT, LANES)
@@ -66,29 +126,28 @@
         return rows[:, pl.ds(pl.multiple_of(tile * LANES, LANES), LANES)].astype(jnp.float32)
 
     for out, step in zip(outs, steps):
-        tiles = [jnp.zeros(shape, jnp.float32) for _ in range(width // LANES)]
+        tiles = [jnp.zeros(shape, jnp.float32) for _ in range(pl.cdiv(columns, LANES))]
         for t in range(here):
             source = scalars[0, (me ^ step) * here + t]
             keep = real & (jnp.full(shape, scalars[1, source]) > 0)
             for tile, value, lo, hi in moved(load, source * BS, t * BS, BS):
                 tiles[tile] = jnp.where((lane >= lo) & (lane < hi) & keep, value, tiles[tile])
-        for at, value in enumerate(tiles):
-            out[:, at * LANES : (at + 1) * LANES] = value.astype(jnp.bfloat16)
-
-
-def right_units(scalars, owned_rows, n_col, steps, after=()):
+        pack_unit(out, tiles, columns)
+
+
+def right_units(scalars, owned_rows, n_col, steps, weight):
     columns = owned_rows.shape[1]
-    width = up(columns // n_col, LANES)
+    size = unit_size(columns // n_col)
     return pl.pallas_call(
         functools.partial(right_kernel, n_col, steps),
-        out_shape=[jax.ShapeDtypeStruct((UNIT, width), jnp.bfloat16)] * len(steps),
-        in_specs=[pl.BlockSpec(memory_space=pltpu.SMEM)] + [pl.BlockSpec(memory_space=pltpu.VMEM)] * (1 + len(after)),
+        out_shape=[jax.ShapeDtypeStruct((size, PACK, LANES), jnp.bfloat16)] * len(steps),
+        in_specs=[pl.BlockSpec(memory_space=pltpu.SMEM)] + [pl.BlockSpec(memory_space=pltpu.VMEM)],
         out_specs=[pl.BlockSpec(memory_space=pltpu.VMEM)] * len(steps),
         scratch_shapes=[pltpu.VMEM((UNIT, up(columns, LANES) + LANES), jnp.bfloat16)],
         compiler_params=limit(2**22),
-        cost_estimate=pl.CostEstimate(flops=8 * 10**9, bytes_accessed=0, transcendentals=0),
+        cost_estimate=pl.CostEstimate(flops=weight, bytes_accessed=1, transcendentals=0),
         name="right_units",
-    )(scalars, owned_rows, *after)
+    )(scalars, owned_rows)
 
 
 def left_kernel(high, pattern, rows_in, out, rows, sems):
@@ -209,22 +268,28 @@
     return pieces, places
 
 
-def multiply_kernel(places, with_total, final, left, *refs):
+def row_tiles(height, final):
+    starts = list(range(0, height, 368))
+    if final and height - starts[-1] == 368:
+        starts.append(height - 128)
+    return [(at, end - at) for at, end in zip(starts, starts[1:] + [height])]
+
+
+def multiply_kernel(places, columns, with_total, final, left, *refs):
     out, right = refs[len(refs) - 4 :][:2] if final else refs[-2:]
     pieces = refs[with_total:]
     right[...] = jnp.zeros_like(right)
     for slot, (piece, unit) in enumerate(places):
-        right[place(slot) : place(slot) + UNIT, :] = pieces[piece][unit * UNIT : (unit + 1) * UNIT, :]
-    high = 368
+        unpack_unit(right, place(slot), pieces[piece], unit * unit_size(columns), columns)
     copies = []
-    for at in range(0, left.shape[0], high):
+    for at, high in row_tiles(left.shape[0], final):
         value = jnp.dot(left[at : at + high, :], right[...], preferred_element_type=jnp.float32)
         if with_total:
             value += refs[0][at : at + high, :]
         if final:
             tiles, sems = refs[-2:]
             tiles[at : at + high, :] = value[:, : tiles.shape[1]].astype(tiles.dtype)
-            copies.append(pltpu.make_async_copy(tiles.at[pl.ds(at, high)], out.at[pl.ds(at, high)], sems.at[at // high]))
+            copies.append(pltpu.make_async_copy(tiles.at[pl.ds(at, high)], out.at[pl.ds(at, high)], sems.at[len(copies)]))
             copies[-1].start()
         else:
             out[at : at + high, :] = value
@@ -232,23 +297,21 @@
         copy.wait()
 
 
-def multiply(left, total, units, columns=None, after=()):
+def multiply(left, total, units, columns, final=False, after=()):
     height, width = left.shape
-    final = columns is not None
     pieces, places = listed(units)
-    wide = pieces[0].shape[1]
+    wide = up(columns, LANES)
     operands = [left] + ([] if total is None else [total]) + pieces
     memory = [pltpu.VMEM] * len(operands) + [pl.ANY] * len(after)
     scratch = [pltpu.VMEM((width, wide), jnp.bfloat16)]
     if final:
-        scratch += [pltpu.VMEM((height, columns), jnp.bfloat16), pltpu.SemaphoreType.DMA((height // 368,))]
+        scratch += [pltpu.VMEM((height, columns), jnp.bfloat16), pltpu.SemaphoreType.DMA((len(row_tiles(height, True)),))]
     return pl.pallas_call(
-        functools.partial(multiply_kernel, [(at, unit[1]) for at, unit in zip(places, units)], total is not None, final),
+        functools.partial(multiply_kernel, [(at, unit[1]) for at, unit in zip(places, units)], columns, total is not None, final),
         out_shape=jax.ShapeDtypeStruct((height, columns if final else wide), jnp.bfloat16 if final else jnp.float32),
         in_specs=[pl.BlockSpec(memory_space=space) for space in memory],
         out_specs=pl.BlockSpec(memory_space=pltpu.HBM if final else pltpu.VMEM),
         scratch_shapes=scratch,
-        input_output_aliases={} if final or total is None else {1: 0},
         compiler_params=limit(width * wide * 2 + height * (wide * 6 + width * 2) + sum(p.size for p in pieces) * 2),
         cost_estimate=pl.CostEstimate(flops=1, bytes_accessed=1, transcendentals=0),
         name="multiply",
@@ -274,6 +337,7 @@
 
 def per_device(n_row, n_col, slab_rows, slab_pattern, owned_rows, owned_pattern, placement):
     columns = owned_rows.shape[1] // n_col
+    size = unit_size(columns)
     bits = [1 << b for b in range(1, n_row.bit_length() - 1)]
     moves = list(zip(bits, bits[::-1]))
     last, deep = n_col - 1, len(moves)
@@ -292,11 +356,11 @@
 
     def unit_of(key):
         value, unit = pieces[key]
-        return value if value.shape[0] == UNIT else value[unit * UNIT : (unit + 1) * UNIT]
+        return value if value.shape[0] == size else value[unit * size : (unit + 1) * size]
 
     def joined(keys):
         value = pieces[keys[0]][0]
-        if value.shape[0] == UNIT * len(keys) and all(pieces[k][0] is value and pieces[k][1] == i for i, k in enumerate(keys)):
+        if value.shape[0] == size * len(keys) and all(pieces[k][0] is value and pieces[k][1] == i for i, k in enumerate(keys)):
             return value
         return jnp.concatenate([unit_of(key) for key in keys]) if len(keys) > 1 else unit_of(keys[0])
 
@@ -327,7 +391,8 @@
     ways = list(range(len(masks)))
     first, rest = [0, 1], list(range(2, n_col))
     scalars = jnp.concatenate([placement[None], owned_pattern])
-    units = right_units(scalars, owned_rows, n_col, list(range(n_col)))
+    units = right_units(scalars, owned_rows, n_col, list(range(1, n_col)), 8 * 10**9)
+    units = right_units(scalars, owned_rows, n_col, [0], 1) + units
 
     pieces, swaps = {(0, 0): (units[0], 0)}, {}
     for step in range(1, n_col):
@@ -362,35 +427,35 @@
     ready = early + arrived
     soon = [key for key in late if key[1] <= full // 2 and key[0] in rest]
     then = [key for key in late if key not in soon]
-    groups = [(ready, []), (late, ready), ([], late), (tail, tail)]
+    groups = [(ready, []), ([], ready), (late, []), ([], late), (tail, tail)]
 
     left = left_side(slab_rows, slab_pattern, up(slab_rows.shape[1], 2 * LANES))
     left, point = tied([(1, 0)], [], [left, scalars])
     point = mark(point)
     (point,) = tied([(0, 0), (1, 0)], [], [point])
     wave(0)
-    (ready_left,) = sides(left, n_col, [slots(*groups[0])], point)
-    ready_left, left, point = tied(arrived, [], [ready_left, left, point])
+    lefts = sides(left, n_col, [slots(*group) for group in groups], point)
+    *lefts, point = tied(arrived, [], [*lefts, point])
     point = mark(point)
     (point,) = tied(come(0), [], [point])
     for number in range(1, deep):
         wave(number)
     swap(ready)
-    lefts = sides(left, n_col, [slots(*group) for group in groups[1:]], point)
-    total = multiply(ready_left, None, own(ready))
-    total, point, *lefts = tied(soon, [], [total, point, *lefts])
+    total = multiply(lefts[0], None, own(ready), columns)
+    total, point = tied(soon, [], [total, point])
     wave(deep)
-    total, point = tied(then, [], [total, point])
     point = mark(point, 10)
-    (point,) = tied([], ready, [point])
+    point, total = tied([], ready, [point, total])
+    total = multiply(lefts[1], total, other(ready), columns, after=[point])
+    (total,) = tied(then, [], [total])
     swap(late)
-    total = multiply(lefts[0], total, own(late) + other(ready), after=[point])
+    total = multiply(lefts[2], total, own(late), columns)
     total, point = tied(tail, [], [total, point])
     swap(tail)
-    point = mark(point)
+    point = mark(point, 10)
     (point,) = tied([], late, [point])
-    total = multiply(lefts[1], total, other(late), after=[point])
-    return multiply(lefts[2], total, own(tail) + other(tail), columns)
+    total = multiply(lefts[3], total, other(late), columns, after=[point])
+    return multiply(lefts[4], total, own(tail) + other(tail), columns, final=True)
 
 
 def solution(mesh):

time: 45.5 us -> 43 us (0.945)
  waiting for transfers between devices: 8.22 us -> 4.61 us
  starting transfers between devices: 14.7 us -> 15.5 us
    ppermute x3, waiting for transfers between devices: 6.33 us -> 1.51 us  [along_col(): return lax.ppermute(value, 'col', [(i, i ^ step) for i in range(n_col)])]
    ppermute x8, waiting for transfers between devices: 1.89 us -> 3.1 us  [along_row(): lax.ppermute(value, 'row', [(i, i ^ move[i & 1]) for i in range(n_row)])]
    ppermute x8, starting transfers between devices: 9.02 us -> 9.81 us  [along_row(): lax.ppermute(value, 'row', [(i, i ^ move[i & 1]) for i in range(n_row)])]
    pallas_call x1 -> x2, Pallas kernels: 1.48 us -> 2.12 us  [right_units(): pl.pallas_call(functools.partial(right_kernel, n_col, steps), out_shape=[...]
    pallas_call x2 -> x1, Pallas kernels: 5.14 us -> 4.92 us  [sides(): pl.pallas_call(functools.partial(side_kernel, n_col, groups), out_shape=[...]
    pallas_call x4 -> x5, Pallas kernels: 11.5 us -> 11.3 us  [multiply(): pl.pallas_call(functools.partial(multiply_kernel, [(at, unit[1]) for at,...]
  transfers between devices with their start and end apart: 11 -> 11, of which waited for: 4 -> 2; matrix products, arithmetic and copies ran while one was open for 1% -> 1% of each run, Pallas kernels for 34% -> 37%
where the time goes in v3:
time: 43 us; the launch traced here: 42.8 us
  Pallas kernels  19.9 us (46%)
  starting transfers between devices  15.5 us (36%)
  waiting for transfers between devices  4.61 us (11%)
  local copies, waits for them, and re-layouts  1.58 us (4%)
  other arithmetic  1.03 us (2%)
    pallas_call x5, Pallas kernels, multiply(): pl.pallas_call(functools.partial(multiply_kernel, [(at, unit[1]) for at,...  11.3 us
    ppermute x8, starting transfers between devices, along_row(): lax.ppermute(value, 'row', [(i, i ^ move[i & 1]) for i in range(n_row)])  9.81 us
    ppermute x3, starting transfers between devices, along_col(): return lax.ppermute(value, 'col', [(i, i ^ step) for i in range(n_col)])  5.67 us
    pallas_call x1, Pallas kernels, sides(): pl.pallas_call(functools.partial(side_kernel, n_col, groups), out_shape=[...  4.92 us
    ppermute x8, waiting for transfers between devices, along_row(): lax.ppermute(value, 'row', [(i, i ^ move[i & 1]) for i in range(n_row)])  3.1 us
    pallas_call x2, Pallas kernels, right_units(): pl.pallas_call(functools.partial(right_kernel, n_col, steps), out_shape=[...  2.12 us
    ppermute x3, waiting for transfers between devices, along_col(): return lax.ppermute(value, 'col', [(i, i ^ step) for i in range(n_col)])  1.51 us
    unnamed x15, local copies, waits for them, and re-layouts  1.49 us
  transfers between devices with their start and end apart: 11, of which 2 were waited for; matrix products, arithmetic and copies ran while one was open for 1% of the time, Pallas kernels for 37%

profile of v3, /device:TPU:0, one launch (start us, length us, event | category | flops | bytes accessed | tf_op | source)
XLA Modules:
  0.0 42.8 jit_solution(4546635494334133665)
XLA Ops:
  0.0 0.0 slice-start
  0.0 0.8 %pad_add_fusion.scalars.value = s32[2,64]{1,0:T(2,128)S(1)} fusion(s32[1,64]{1,0:T(1,128)} %param.8, s32[1,64]{1,0:T(1,128)} %bitcast.3), kind=kLoop, calls=%fused_computation.13 | loop fusion | flops 128 | bytes 1024 | tf_op jit(solution)/shard_map/concatenate | solution.py:393
  0.8 0.0 copy-start
  0.8 1.3 %copy-done = bf16[69,4416]{1,0:T(8,128)(2,1)S(1)} copy-done((bf16[69,4416]{1,0:T(8,128)(2,1)S(1)}, bf16[69,4416]{1,0:T(8,128)(2,1)}, u32[]{:S(2)}) %copy-start) | copy-done | bytes 609432
  2.1 0.0 slice-start.1
  2.1 0.0 copy-start.1
  2.1 1.3 %right_units.2 = (bf16[39,16,128]{2,1,0:T(8,128)(2,1)S(1)}, bf16[39,16,128]{2,1,0:T(8,128)(2,1)S(1)}, bf16[39,16,128]{2,1,0:T(8,128)(2,1)S(1)}) custom-call(s32[2,64]{1,0:T(2,128)S(1)} %pad_add_fusion.scalars.value, bf16[69,4416]{1,0:T(8,128)(2,1)S(1)} %copy-done), custom_call_target="tpu_custom_call" | custom-call | flops 8000000000 | bytes 1 | tf_op jit(solution)/shard_map/right_units/pallas_call | solution.py:141
  3.4 3.1 %collective-permute-start.2 = (bf16[39,16,128]{2,1,0:T(8,128)(2,1)S(1)}, bf16[39,16,128]{2,1,0:T(8,128)(2,1)S(1)}, u32[]{:S(2)}, u32[]{:S(2)}) collective-permute-start(bf16[39,16,128]{2,1,0:T(8,128)(2,1)S(1)} %get-tuple-element.45), channel_id=1, source_target_pairs={{0,1},{1,0},{2,3},{3,2},{4,5},{5,4},{6,7},{7,6},{8,9},{9,8},{10,11... | collective-permute-start | bytes 479240 | tf_op jit(solution)/shard_map/ppermute | solution.py:349
  6.4 2.6 %collective-permute-start = (bf16[39,16,128]{2,1,0:T(8,128)(2,1)S(1)}, bf16[39,16,128]{2,1,0:T(8,128)(2,1)S(1)}, u32[]{:S(2)}, u32[]{:S(2)}) collective-permute-start(bf16[39,16,128]{2,1,0:T(8,128)(2,1)S(1)} %get-tuple-element.43), channel_id=1, source_target_pairs={{0,2},{1,3},{2,0},{3,1},{4,6},{5,7},{6,4},{7,5},{8,10},{9,11},{10,... | collective-permute-start | bytes 479240 | tf_op jit(solution)/shard_map/ppermute | solution.py:349
  9.0 0.0 collective-permute-start.1
  9.0 0.9 %right_units.3.refs_0_ = bf16[39,16,128]{2,1,0:T(8,128)(2,1)S(1)} custom-call(s32[2,64]{1,0:T(2,128)S(1)} %pad_add_fusion.scalars.value, bf16[69,4416]{1,0:T(8,128)(2,1)S(1)} %copy-done), custom_call_target="tpu_custom_call" | custom-call | flops 1 | bytes 1 | tf_op jit(solution)/shard_map/right_units/pallas_call | solution.py:141
  9.9 0.0 slice-done
  9.9 0.0 slice-done.1
  9.9 0.0 copy-done.1
  9.9 1.5 %left_side.1.left = bf16[1104,2304]{1,0:T(8,128)(2,1)S(1)} custom-call(s32[16,32]{1,0:T(8,128)S(1)} %copy-done.1, bf16[1104,2208]{1,0:T(8,128)(2,1)S(1)} %bitcast.2), custom_call_target="tpu_custom_call" | custom-call | flops 1 | bytes 1 | tf_op jit(solution)/shard_map/left_side/pallas_call | solution.py:197
  11.4 1.5 %collective-permute-done.2.refs_1_ = bf16[39,16,128]{2,1,0:T(8,128)(2,1)S(1)} collective-permute-done((bf16[39,16,128]{2,1,0:T(8,128)(2,1)S(1)}, bf16[39,16,128]{2,1,0:T(8,128)(2,1)S(1)}, u32[]{:S(2)}, u32[]{:S(2)}) %collective-permute-start.2) | collective-permute-done | bytes 159776 | tf_op jit(solution)/shard_map/ppermute | solution.py:349
  12.9 0.1 constant_dynamic-update-slice_fusion.4
  13.0 1.8 %collective-permute-start.5 = (bf16[78,16,128]{2,1,0:T(8,128)(2,1)S(1)}, bf16[78,16,128]{2,1,0:T(8,128)(2,1)S(1)}, u32[]{:S(2)}, u32[]{:S(2)}) collective-permute-start(bf16[78,16,128]{2,1,0:T(8,128)(2,1)S(1)} %get-tuple-element.84), channel_id=1, source_target_pairs={{0,16},{4,12},{8,24},{12,4},{16,0},{20,28},{24,8},{28,20},{1,17},{... | collective-permute-start | bytes 958472 | tf_op jit(solution)/shard_map/ppermute | solution.py:346
  14.8 1.5 %collective-permute-start.4 = (bf16[78,16,128]{2,1,0:T(8,128)(2,1)S(1)}, bf16[78,16,128]{2,1,0:T(8,128)(2,1)S(1)}, u32[]{:S(2)}, u32[]{:S(2)}) collective-permute-start(bf16[78,16,128]{2,1,0:T(8,128)(2,1)S(1)} %get-tuple-element.84), channel_id=1, source_target_pairs={{0,8},{4,20},{8,0},{12,28},{16,24},{20,4},{24,16},{28,12},{1,9},{5... | collective-permute-start | bytes 958472 | tf_op jit(solution)/shard_map/ppermute | solution.py:346
  16.3 4.9 %sides.1 = (bf16[1104,768]{1,0:T(8,128)(2,1)S(1)}, bf16[1104,768]{1,0:T(8,128)(2,1)S(1)}, bf16[1104,512]{1,0:T(8,128)(2,1)S(1)}, bf16[1104,512]{1,0:T(8,128)(2,1)S(1)}, bf16[1104,512]{1,0:T(8,128)(2,1)S(1)}) custom-call(bf16[1104,2304]{1,0:T(8,128)(2,1)S(1)} %left_side.1.left, s32[2,64]{1,0:T(2,128)S(1)} %mark.4.point.value), custom_call_target="tpu_custom_call" | custom-call | flops 1 | bytes 1 | tf_op jit(solution)/shard_map/sides/pallas_call | solution.py:243
  21.2 0.0 collective-permute-done.refs_4_
  21.3 0.0 collective-permute-done.1.refs_5_
  21.3 1.5 %collective-permute-start.3 = (bf16[78,16,128]{2,1,0:T(8,128)(2,1)S(1)}, bf16[78,16,128]{2,1,0:T(8,128)(2,1)S(1)}, u32[]{:S(2)}, u32[]{:S(2)}) collective-permute-start(bf16[78,16,128]{2,1,0:T(8,128)(2,1)S(1)} %pad_maximum_fusion.2), channel_id=1, source_target_pairs={{0,8},{4,20},{8,0},{12,28},{16,24},{20,4},{24,16},{28,12},{1,9},{5... | collective-permute-start | bytes 958472 | tf_op jit(solution)/shard_map/ppermute | solution.py:346
  22.8 0.0 collective-permute-done.5.refs_3_
  22.8 0.0 collective-permute-done.4.refs_2_
  23.0 0.1 collective-permute-start.8
  23.1 0.1 pad_maximum_fusion.1
  23.1 1.6 %collective-permute-start.7 = (bf16[156,16,128]{2,1,0:T(8,128)(2,1)S(1)}, bf16[156,16,128]{2,1,0:T(8,128)(2,1)S(1)}, u32[]{:S(2)}, u32[]{:S(2)}) collective-permute-start(bf16[156,16,128]{2,1,0:T(8,128)(2,1)S(1)} %pad_maximum_fusion.1), channel_id=1, source_target_pairs={{0,16},{4,12},{8,24},{12,4},{16,0},{20,28},{24,8},{28,20},{1,17},{... | collective-permute-start | bytes 1916936 | tf_op jit(solution)/shard_map/ppermute | solution.py:346
  24.7 2.5 %multiply.5.refs_0_ = f32[1104,1152]{1,0:T(8,128)S(1)} custom-call(bf16[1104,768]{1,0:T(8,128)(2,1)S(1)} %get-tuple-element.59.left, bf16[39,16,128]{2,1,0:T(8,128)(2,1)S(1)} %right_units.3.refs_0_, bf16[39,16,128]{2,1,0:T(8,128)(2,1)S(1)} %collective-permute-done.2.refs_1_, bf16[78,16,128]{2,1,0:T(8,128)(2,1)S(1)} %collective-permute-done.4.refs_2_, ...), custom_call_target="tpu_custom_call" | custom-call | flops 1 | bytes 1 | tf_op jit(solution)/shard_map/multiply/pallas_call | solution.py:309
  27.3 3.1 %collective-permute-done.3.refs_1_ = bf16[78,16,128]{2,1,0:T(8,128)(2,1)S(1)} collective-permute-done((bf16[78,16,128]{2,1,0:T(8,128)(2,1)S(1)}, bf16[78,16,128]{2,1,0:T(8,128)(2,1)S(1)}, u32[]{:S(2)}, u32[]{:S(2)}) %collective-permute-start.3) | collective-permute-done | bytes 319520 | tf_op jit(solution)/shard_map/ppermute | solution.py:346
  30.4 1.5 %collective-permute-start.6 = (bf16[78,16,128]{2,1,0:T(8,128)(2,1)S(1)}, bf16[78,16,128]{2,1,0:T(8,128)(2,1)S(1)}, u32[]{:S(2)}, u32[]{:S(2)}) collective-permute-start(bf16[78,16,128]{2,1,0:T(8,128)(2,1)S(1)} %collective-permute-done.3.refs_1_), channel_id=1, source_target_pairs={{0,16},{4,12},{8,24},{12,4},{16,0},{20,28},{24,8},{28,20},{1,17},{... | collective-permute-start | bytes 958472 | tf_op jit(solution)/shard_map/ppermute | solution.py:346
  31.9 0.0 collective-permute-done.8.refs_1_
  31.9 2.6 %multiply.6.refs_0_ = f32[1104,1152]{1,0:T(8,128)S(1)} custom-call(bf16[1104,768]{1,0:T(8,128)(2,1)S(1)} %get-tuple-element.68.left, f32[1104,1152]{1,0:T(8,128)S(1)} %multiply.5.refs_0_, bf16[312,16,128]{2,1,0:T(8,128)(2,1)S(1)} %collective-permute-done.8.refs_1_, s32[2,64]{1,0:T(2,128)S(1)} %mark.6.refs_2_.value), custom_call_target="tpu_custom_call" | custom-call | flops 1 | bytes 1 | tf_op jit(solution)/shard_map/multiply/pallas_call | solution.py:309
  34.5 0.0 collective-permute-done.7.refs_2_
  34.5 0.1 pad_maximum_fusion
  34.7 0.9 %collective-permute-start.9 = (bf16[234,16,128]{2,1,0:T(8,128)(2,1)S(1)}, bf16[234,16,128]{2,1,0:T(8,128)(2,1)S(1)}, u32[]{:S(2)}, u32[]{:S(2)}) collective-permute-start(bf16[234,16,128]{2,1,0:T(8,128)(2,1)S(1)} %pad_maximum_fusion), channel_id=1, source_target_pairs={{0,4},{4,0},{8,12},{12,8},{16,20},{20,16},{24,28},{28,24},{1,5},{5... | collective-permute-start | bytes 2875400 | tf_op jit(solution)/shard_map/ppermute | solution.py:346
  35.6 1.9 %multiply.7.refs_0_ = f32[1104,1152]{1,0:T(8,128)S(1)} custom-call(bf16[1104,512]{1,0:T(8,128)(2,1)S(1)} %get-tuple-element.67.left, f32[1104,1152]{1,0:T(8,128)S(1)} %multiply.6.refs_0_, bf16[78,16,128]{2,1,0:T(8,128)(2,1)S(1)} %collective-permute-done.3.refs_1_, bf16[156,16,128]{2,1,0:T(8,128)(2,1)S(1)} %collective-permute-done.7.refs_2_), custom_call_target="tpu_custom_call" | custom-call | flops 1 | bytes 1 | tf_op jit(solution)/shard_map/multiply/pallas_call | solution.py:309
  37.5 0.0 collective-permute-done.6.refs_1_
  37.5 1.0 %collective-permute-start.10 = (bf16[78,16,128]{2,1,0:T(8,128)(2,1)S(1)}, bf16[78,16,128]{2,1,0:T(8,128)(2,1)S(1)}, u32[]{:S(2)}, u32[]{:S(2)}) collective-permute-start(bf16[78,16,128]{2,1,0:T(8,128)(2,1)S(1)} %collective-permute-done.6.refs_1_), channel_id=1, source_target_pairs={{0,4},{4,0},{8,12},{12,8},{16,20},{20,16},{24,28},{28,24},{1,5},{5... | collective-permute-start | bytes 958472 | tf_op jit(solution)/shard_map/ppermute | solution.py:346
  38.4 0.0 collective-permute-done.9.refs_1_
  38.5 1.8 %multiply.8.refs_0_ = f32[1104,1152]{1,0:T(8,128)S(1)} custom-call(bf16[1104,512]{1,0:T(8,128)(2,1)S(1)} %get-tuple-element.56.left, f32[1104,1152]{1,0:T(8,128)S(1)} %multiply.7.refs_0_, bf16[234,16,128]{2,1,0:T(8,128)(2,1)S(1)} %collective-permute-done.9.refs_1_, s32[2,64]{1,0:T(2,128)S(1)} %mark.7.refs_2_), custom_call_target="tpu_custom_call" | custom-call | flops 1 | bytes 1 | tf_op jit(solution)/shard_map/multiply/pallas_call | solution.py:309
  40.2 0.0 collective-permute-done.10.refs_2_
  40.2 2.6 %multiply.9 = bf16[1104,1104]{1,0:T(8,128)(2,1)} custom-call(bf16[1104,512]{1,0:T(8,128)(2,1)S(1)} %get-tuple-element.55.left, f32[1104,1152]{1,0:T(8,128)S(1)} %multiply.8.refs_0_, bf16[78,16,128]{2,1,0:T(8,128)(2,1)S(1)} %collective-permute-done.6.refs_1_, bf16[78,16,128]{2,1,0:T(8,128)(2,1)S(1)} %collective-permute-done.10.refs_2_), custom_call_target="tpu_custom_call" | custom-call | flops 1 | bytes 1 | tf_op jit(solution)/shard_map/multiply/pallas_call | solution.py:309
  (16 shorter events, 0.3 us)
Async XLA Ops:
  0.0 9.9 %slice-start = ((s8[5087232]{0:T(1024)(128)(4,1)}), s8[4194304]{0:T(1024)(128)(4,1)S(1)}, s32[]{:S(2)}) async-start(s8[5087232]{0:T(1024)(128)(4,1)} %bitcast.1), calls=%async_computation | async-start | bytes 8388608
  0.8 1.3 %copy-start = (bf16[69,4416]{1,0:T(8,128)(2,1)S(1)}, bf16[69,4416]{1,0:T(8,128)(2,1)}, u32[]{:S(2)}) copy-start(bf16[69,4416]{1,0:T(8,128)(2,1)} %raw.3) | copy-start | bytes 1828228
  2.1 7.8 %slice-start.1 = ((s8[5087232]{0:T(1024)(128)(4,1)}), s8[892928]{0:T(1024)(128)(4,1)S(1)}, s32[]{:S(2)}) async-start(s8[5087232]{0:T(1024)(128)(4,1)} %bitcast.1), calls=%async_computation.1 | async-start | bytes 1785856
  2.1 7.8 %copy-start.1 = (s32[16,32]{1,0:T(8,128)S(1)}, s32[16,32]{1,0:T(8,128)}, u32[]{:S(2)}) copy-start(s32[16,32]{1,0:T(8,128)} %pattern.1) | copy-start | bytes 6148
  3.4 9.5 %collective-permute-start.2 = (bf16[39,16,128]{2,1,0:T(8,128)(2,1)S(1)}, bf16[39,16,128]{2,1,0:T(8,128)(2,1)S(1)}, u32[]{:S(2)}, u32[]{:S(2)}) collective-permute-start(bf16[39,16,128]{2,1,0:T(8,128)(2,1)S(1)} %get-tuple-element.45), channel_id=1, source_target_pairs={{0,1},{1,0},{2,3},{3,2},{4,5},{5,4},{6,7},{7,6},{8,9},{9,8},{10,11... | collective-permute-start | bytes 479240 | tf_op jit(solution)/shard_map/ppermute | solution.py:349
  6.4 14.8 %collective-permute-start = (bf16[39,16,128]{2,1,0:T(8,128)(2,1)S(1)}, bf16[39,16,128]{2,1,0:T(8,128)(2,1)S(1)}, u32[]{:S(2)}, u32[]{:S(2)}) collective-permute-start(bf16[39,16,128]{2,1,0:T(8,128)(2,1)S(1)} %get-tuple-element.43), channel_id=1, source_target_pairs={{0,2},{1,3},{2,0},{3,1},{4,6},{5,7},{6,4},{7,5},{8,10},{9,11},{10,... | collective-permute-start | bytes 479240 | tf_op jit(solution)/shard_map/ppermute | solution.py:349
  9.0 12.2 %collective-permute-start.1 = (bf16[39,16,128]{2,1,0:T(8,128)(2,1)S(1)}, bf16[39,16,128]{2,1,0:T(8,128)(2,1)S(1)}, u32[]{:S(2)}, u32[]{:S(2)}) collective-permute-start(bf16[39,16,128]{2,1,0:T(8,128)(2,1)S(1)} %get-tuple-element.44), channel_id=1, source_target_pairs={{0,3},{1,2},{2,1},{3,0},{4,7},{5,6},{6,5},{7,4},{8,11},{9,10},{10,... | collective-permute-start | bytes 479240 | tf_op jit(solution)/shard_map/ppermute | solution.py:349
  13.0 9.8 %collective-permute-start.5 = (bf16[78,16,128]{2,1,0:T(8,128)(2,1)S(1)}, bf16[78,16,128]{2,1,0:T(8,128)(2,1)S(1)}, u32[]{:S(2)}, u32[]{:S(2)}) collective-permute-start(bf16[78,16,128]{2,1,0:T(8,128)(2,1)S(1)} %get-tuple-element.84), channel_id=1, source_target_pairs={{0,16},{4,12},{8,24},{12,4},{16,0},{20,28},{24,8},{28,20},{1,17},{... | collective-permute-start | bytes 958472 | tf_op jit(solution)/shard_map/ppermute | solution.py:346
  14.8 8.0 %collective-permute-start.4 = (bf16[78,16,128]{2,1,0:T(8,128)(2,1)S(1)}, bf16[78,16,128]{2,1,0:T(8,128)(2,1)S(1)}, u32[]{:S(2)}, u32[]{:S(2)}) collective-permute-start(bf16[78,16,128]{2,1,0:T(8,128)(2,1)S(1)} %get-tuple-element.84), channel_id=1, source_target_pairs={{0,8},{4,20},{8,0},{12,28},{16,24},{20,4},{24,16},{28,12},{1,9},{5... | collective-permute-start | bytes 958472 | tf_op jit(solution)/shard_map/ppermute | solution.py:346
  21.3 9.1 %collective-permute-start.3 = (bf16[78,16,128]{2,1,0:T(8,128)(2,1)S(1)}, bf16[78,16,128]{2,1,0:T(8,128)(2,1)S(1)}, u32[]{:S(2)}, u32[]{:S(2)}) collective-permute-start(bf16[78,16,128]{2,1,0:T(8,128)(2,1)S(1)} %pad_maximum_fusion.2), channel_id=1, source_target_pairs={{0,8},{4,20},{8,0},{12,28},{16,24},{20,4},{24,16},{28,12},{1,9},{5... | collective-permute-start | bytes 958472 | tf_op jit(solution)/shard_map/ppermute | solution.py:346
  23.0 8.9 %collective-permute-start.8 = (bf16[312,16,128]{2,1,0:T(8,128)(2,1)S(1)}, bf16[312,16,128]{2,1,0:T(8,128)(2,1)S(1)}, u32[]{:S(2)}, u32[]{:S(2)}) collective-permute-start(bf16[312,16,128]{2,1,0:T(8,128)(2,1)S(1)} %constant_dynamic-update-slice_fusion.2), channel_id=1, source_target_pairs={{0,4},{4,0},{8,12},{12,8},{16,20},{20,16},{24,28},{28,24},{1,5},{5... | collective-permute-start | bytes 3833864 | tf_op jit(solution)/shard_map/ppermute | solution.py:346
  23.1 11.3 %collective-permute-start.7 = (bf16[156,16,128]{2,1,0:T(8,128)(2,1)S(1)}, bf16[156,16,128]{2,1,0:T(8,128)(2,1)S(1)}, u32[]{:S(2)}, u32[]{:S(2)}) collective-permute-start(bf16[156,16,128]{2,1,0:T(8,128)(2,1)S(1)} %pad_maximum_fusion.1), channel_id=1, source_target_pairs={{0,16},{4,12},{8,24},{12,4},{16,0},{20,28},{24,8},{28,20},{1,17},{... | collective-permute-start | bytes 1916936 | tf_op jit(solution)/shard_map/ppermute | solution.py:346
  30.4 7.1 %collective-permute-start.6 = (bf16[78,16,128]{2,1,0:T(8,128)(2,1)S(1)}, bf16[78,16,128]{2,1,0:T(8,128)(2,1)S(1)}, u32[]{:S(2)}, u32[]{:S(2)}) collective-permute-start(bf16[78,16,128]{2,1,0:T(8,128)(2,1)S(1)} %collective-permute-done.3.refs_1_), channel_id=1, source_target_pairs={{0,16},{4,12},{8,24},{12,4},{16,0},{20,28},{24,8},{28,20},{1,17},{... | collective-permute-start | bytes 958472 | tf_op jit(solution)/shard_map/ppermute | solution.py:346
  34.7 3.8 %collective-permute-start.9 = (bf16[234,16,128]{2,1,0:T(8,128)(2,1)S(1)}, bf16[234,16,128]{2,1,0:T(8,128)(2,1)S(1)}, u32[]{:S(2)}, u32[]{:S(2)}) collective-permute-start(bf16[234,16,128]{2,1,0:T(8,128)(2,1)S(1)} %pad_maximum_fusion), channel_id=1, source_target_pairs={{0,4},{4,0},{8,12},{12,8},{16,20},{20,16},{24,28},{28,24},{1,5},{5... | collective-permute-start | bytes 2875400 | tf_op jit(solution)/shard_map/ppermute | solution.py:346
  37.5 2.7 %collective-permute-start.10 = (bf16[78,16,128]{2,1,0:T(8,128)(2,1)S(1)}, bf16[78,16,128]{2,1,0:T(8,128)(2,1)S(1)}, u32[]{:S(2)}, u32[]{:S(2)}) collective-permute-start(bf16[78,16,128]{2,1,0:T(8,128)(2,1)S(1)} %collective-permute-done.6.refs_1_), channel_id=1, source_target_pairs={{0,4},{4,0},{8,12},{12,8},{16,20},{20,16},{24,28},{28,24},{1,5},{5... | collective-permute-start | bytes 958472 | tf_op jit(solution)/shard_map/ppermute | solution.py:346

commit v4 on v3

--- a/solution.py
+++ b/solution.py
@@ -13,6 +13,7 @@
 UNIT = 72
 PACK = 16
 DEPTH = 256
+CODE = 1 << 16
 SLOT = 80
 
 
@@ -44,7 +45,7 @@
 
 def unit_size(columns):
     full, over = columns // LANES, columns % LANES
-    return full * BODY // PACK + pl.cdiv(full, 2) + pl.cdiv(pl.cdiv(3 * over, LANES) * (UNIT // 3), PACK)
+    return full * BODY // PACK + pl.cdiv(full, PACK // (BS - BODY)) + pl.cdiv(pl.cdiv(3 * over, LANES) * (UNIT // 3), PACK)
 
 
 def pack_unit(out, tiles, columns):
@@ -54,9 +55,12 @@
         for row in range(0, BODY, PACK):
             out[at] = tile[row : row + PACK].astype(jnp.bfloat16)
             at += 1
-    for t in range(0, full, 2):
-        pair = [tiles[t][BODY:], tiles[t + 1][BODY:] if t + 1 < full else jnp.zeros_like(tiles[t][BODY:])]
-        out[at] = jnp.concatenate(pair, 0).astype(jnp.bfloat16)
+    few = BS - BODY
+    for t in range(0, full, PACK // few):
+        rows = jnp.zeros((PACK, LANES), jnp.float32)
+        for k, tile in enumerate(tiles[t : min(full, t + PACK // few)]):
+            rows += pltpu.roll(jnp.concatenate([tile[BODY:], jnp.zeros((PACK + BODY - UNIT, LANES), jnp.float32)], 0), k * few, 0)
+        out[at] = rows.astype(jnp.bfloat16)
         at += 1
     if not over:
         return
@@ -85,13 +89,15 @@
         for row in range(0, BODY, PACK):
             right[first + row : first + row + PACK, t * LANES : (t + 1) * LANES] = piece[at]
             at += 1
-    zero = jnp.zeros((PACK // 2, LANES), jnp.float32)
-    for t in range(0, full, 2):
-        pair = piece[at].astype(jnp.float32)
+    few = BS - BODY
+    row = lax.broadcasted_iota(jnp.int32, (PACK, LANES), 0)
+    for t in range(0, full, PACK // few):
+        rows = piece[at].astype(jnp.float32)
         at += 1
-        for k in range(min(2, full - t)):
-            half = jnp.concatenate([pair[k * PACK // 2 : (k + 1) * PACK // 2], zero], 0).astype(jnp.bfloat16)
-            right[first + BODY : first + BODY + PACK, (t + k) * LANES : (t + k + 1) * LANES] = half
+        for k in range(min(PACK // few, full - t)):
+            mine = pltpu.roll(rows, PACK - k * few, 0) if k else rows
+            mine = jnp.where(row < few, mine, 0.0).astype(jnp.bfloat16)
+            right[first + BODY : first + BODY + PACK, (t + k) * LANES : (t + k + 1) * LANES] = mine
     if not over:
         return
     third = UNIT // 3
@@ -108,7 +114,7 @@
         if shift + over > LANES:
             value = jnp.where(lane < LANES - shift, value, pltpu.roll(packed[t + 1], LANES - shift, 1))
         values.append(value)
-    values.append(zero)
+    values.append(jnp.zeros((SLOT - UNIT, LANES), jnp.float32))
     right[first : first + SLOT, full * LANES : (full + 1) * LANES] = jnp.concatenate(values, 0).astype(jnp.bfloat16)
 
 
@@ -116,7 +122,7 @@
     outs, rows = refs[-1 - len(steps) : -1], refs[-1]
     rows[: raw.shape[0], : raw.shape[1]] = raw[...]
     columns = raw.shape[1] // n_col
-    here = scalars.shape[1] // n_col
+    here = scalars.shape[0] // n_col
     me = lax.axis_index("col")
     shape = (UNIT, LANES)
     lane = lax.broadcasted_iota(jnp.int32, shape, 1)
@@ -128,8 +134,8 @@
     for out, step in zip(outs, steps):
         tiles = [jnp.zeros(shape, jnp.float32) for _ in range(pl.cdiv(columns, LANES))]
         for t in range(here):
-            source = scalars[0, (me ^ step) * here + t]
-            keep = real & (jnp.full(shape, scalars[1, source]) > 0)
+            source = scalars[(me ^ step) * here + t] & (CODE - 1)
+            keep = real & (jnp.full(shape, scalars[source]) >= CODE)
             for tile, value, lo, hi in moved(load, source * BS, t * BS, BS):
                 tiles[tile] = jnp.where((lane >= lo) & (lane < hi) & keep, value, tiles[tile])
         pack_unit(out, tiles, columns)
@@ -278,7 +284,9 @@
 def multiply_kernel(places, columns, with_total, final, left, *refs):
     out, right = refs[len(refs) - 4 :][:2] if final else refs[-2:]
     pieces = refs[with_total:]
-    right[...] = jnp.zeros_like(right)
+    for first in range(0, right.shape[0], DEPTH):
+        used = min(3, len(places) - first // DEPTH * 3) * SLOT
+        right[first + used : first + DEPTH, :] = jnp.zeros((DEPTH - used, right.shape[1]), right.dtype)
     for slot, (piece, unit) in enumerate(places):
         unpack_unit(right, place(slot), pieces[piece], unit * unit_size(columns), columns)
     copies = []
@@ -390,7 +398,7 @@
 
     ways = list(range(len(masks)))
     first, rest = [0, 1], list(range(2, n_col))
-    scalars = jnp.concatenate([placement[None], owned_pattern])
+    scalars = placement + owned_pattern[0] * CODE
     units = right_units(scalars, owned_rows, n_col, list(range(1, n_col)), 8 * 10**9)
     units = right_units(scalars, owned_rows, n_col, [0], 1) + units
 
@@ -427,7 +435,8 @@
     ready = early + arrived
     soon = [key for key in late if key[1] <= full // 2 and key[0] in rest]
     then = [key for key in late if key not in soon]
-    groups = [(ready, []), ([], ready), (late, []), ([], late), (tail, tail)]
+    near = [(0, 0), (1, 0)]
+    groups = [(ready, near), ([], [key for key in ready if key not in near]), (late, []), ([], late), (tail, tail)]
 
     left = left_side(slab_rows, slab_pattern, up(slab_rows.shape[1], 2 * LANES))
     left, point = tied([(1, 0)], [], [left, scalars])
@@ -440,19 +449,22 @@
     (point,) = tied(come(0), [], [point])
     for number in range(1, deep):
         wave(number)
-    swap(ready)
-    total = multiply(lefts[0], None, own(ready), columns)
+    swap(near)
+    swap([key for key in ready if key not in near])
+    total = multiply(lefts[0], None, own(ready) + other(near), columns)
     total, point = tied(soon, [], [total, point])
+    point = mark(point, 10)
+    (point,) = tied(soon, [], [point])
     wave(deep)
-    point = mark(point, 10)
-    point, total = tied([], ready, [point, total])
-    total = multiply(lefts[1], total, other(ready), columns, after=[point])
+    point = mark(point, 5)
+    point, total = tied([], [key for key in ready if key not in near], [point, total])
+    total = multiply(lefts[1], total, other([key for key in ready if key not in near]), columns, after=[point])
     (total,) = tied(then, [], [total])
     swap(late)
     total = multiply(lefts[2], total, own(late), columns)
     total, point = tied(tail, [], [total, point])
     swap(tail)
-    point = mark(point, 10)
+    point = mark(point, 8)
     (point,) = tied([], late, [point])
     total = multiply(lefts[3], total, other(late), columns, after=[point])
     return multiply(lefts[4], total, own(tail) + other(tail), columns, final=True)

time: 43 us -> 42.4 us (0.986); the launches traced: 42.8 us -> 41.7 us
  Pallas kernels: 19.9 us -> 19.4 us
    concatenate x1 -> x0, other arithmetic: 0.83 us -> none  [per_device(): scalars = jnp.concatenate([placement[None], owned_pattern])]
    add x0 -> x1, other arithmetic: none -> 0.67 us  [per_device(): scalars = placement + owned_pattern[0] * CODE]
    unnamed x15 -> x12, local copies, waits for them, and re-layouts: 1.49 us -> 1.2 us
    ppermute x8 -> x9, starting transfers between devices: 9.81 us -> 9.56 us  [along_row(): lax.ppermute(value, 'row', [(i, i ^ move[i & 1]) for i in range(n_row)])]
    ppermute x8 -> x9, waiting for transfers between devices: 3.1 us -> 3.34 us  [along_row(): lax.ppermute(value, 'row', [(i, i ^ move[i & 1]) for i in range(n_row)])]
  transfers between devices with their start and end apart: 11 -> 12, of which waited for: 2 -> 4; matrix products, arithmetic and copies ran while one was open for 1% -> 1% of each run, Pallas kernels for 37% -> 38%
where the time goes in v4:
time: 42.4 us; the launch traced here: 41.7 us
  Pallas kernels  19.4 us (46%)
  starting transfers between devices  15.2 us (36%)
  waiting for transfers between devices  4.69 us (11%)
  local copies, waits for them, and re-layouts  1.31 us (3%)
  other arithmetic  0.87 us (2%)
    pallas_call x5, Pallas kernels, multiply(): pl.pallas_call(functools.partial(multiply_kernel, [(at, unit[1]) for at,...  11 us
    ppermute x9, starting transfers between devices, along_row(): lax.ppermute(value, 'row', [(i, i ^ move[i & 1]) for i in range(n_row)])  9.56 us
    ppermute x3, starting transfers between devices, along_col(): return lax.ppermute(value, 'col', [(i, i ^ step) for i in range(n_col)])  5.67 us
    pallas_call x1, Pallas kernels, sides(): pl.pallas_call(functools.partial(side_kernel, n_col, groups), out_shape=[...  4.92 us
    ppermute x9, waiting for transfers between devices, along_row(): lax.ppermute(value, 'row', [(i, i ^ move[i & 1]) for i in range(n_row)])  3.34 us
    pallas_call x2, Pallas kernels, right_units(): pl.pallas_call(functools.partial(right_kernel, n_col, steps), out_shape=[...  2.02 us
    pallas_call x1, Pallas kernels, left_side(): pl.pallas_call(functools.partial(left_kernel, high), out_shape=jax.ShapeD...  1.48 us
    ppermute x3, waiting for transfers between devices, along_col(): return lax.ppermute(value, 'col', [(i, i ^ step) for i in range(n_col)])  1.35 us
  transfers between devices with their start and end apart: 12, of which 4 were waited for; matrix products, arithmetic and copies ran while one was open for 1% of the time, Pallas kernels for 38%

profile of v4, /device:TPU:0, one launch (start us, length us, event | category | flops | bytes accessed | tf_op | source)
XLA Modules:
  0.0 41.7 jit_solution(6376422866122599953)
XLA Ops:
  0.0 0.7 %bitcast_add_fusion.scalars.value = s32[64]{0:T(128)S(1)} fusion(s32[64]{0:T(128)} %param.9, s32[1,64]{1,0:T(1,128)} %param.8), kind=kLoop, calls=%fused_computation.11 | loop fusion | flops 128 | bytes 768 | tf_op jit(solution)/shard_map/add | solution.py:401
  0.7 0.0 copy-start.1
  0.7 1.1 %copy-done.1 = bf16[69,4416]{1,0:T(8,128)(2,1)S(1)} copy-done((bf16[69,4416]{1,0:T(8,128)(2,1)S(1)}, bf16[69,4416]{1,0:T(8,128)(2,1)}, u32[]{:S(2)}) %copy-start.1) | copy-done | bytes 609432
  1.8 0.0 copy-start
  1.8 0.0 copy-start.2
  1.8 1.2 %right_units.2 = (bf16[38,16,128]{2,1,0:T(8,128)(2,1)S(1)}, bf16[38,16,128]{2,1,0:T(8,128)(2,1)S(1)}, bf16[38,16,128]{2,1,0:T(8,128)(2,1)S(1)}) custom-call(s32[64]{0:T(128)S(1)} %bitcast_add_fusion.scalars.value, bf16[69,4416]{1,0:T(8,128)(2,1)S(1)} %copy-done.1), custom_call_target="tpu_custom_call" | custom-call | flops 8000000000 | bytes 1 | tf_op jit(solution)/shard_map/right_units/pallas_call | solution.py:147
  3.0 3.1 %collective-permute-start.2 = (bf16[38,16,128]{2,1,0:T(8,128)(2,1)S(1)}, bf16[38,16,128]{2,1,0:T(8,128)(2,1)S(1)}, u32[]{:S(2)}, u32[]{:S(2)}) collective-permute-start(bf16[38,16,128]{2,1,0:T(8,128)(2,1)S(1)} %get-tuple-element.47), channel_id=1, source_target_pairs={{0,1},{1,0},{2,3},{3,2},{4,5},{5,4},{6,7},{7,6},{8,9},{9,8},{10,11... | collective-permute-start | bytes 466952 | tf_op jit(solution)/shard_map/ppermute | solution.py:357
  6.0 2.6 %collective-permute-start = (bf16[38,16,128]{2,1,0:T(8,128)(2,1)S(1)}, bf16[38,16,128]{2,1,0:T(8,128)(2,1)S(1)}, u32[]{:S(2)}, u32[]{:S(2)}) collective-permute-start(bf16[38,16,128]{2,1,0:T(8,128)(2,1)S(1)} %get-tuple-element.45), channel_id=1, source_target_pairs={{0,2},{1,3},{2,0},{3,1},{4,6},{5,7},{6,4},{7,5},{8,10},{9,11},{10,... | collective-permute-start | bytes 466952 | tf_op jit(solution)/shard_map/ppermute | solution.py:357
  8.6 0.0 collective-permute-start.1
  8.6 0.8 %right_units.3.refs_0_ = bf16[38,16,128]{2,1,0:T(8,128)(2,1)S(1)} custom-call(s32[64]{0:T(128)S(1)} %bitcast_add_fusion.scalars.value, bf16[69,4416]{1,0:T(8,128)(2,1)S(1)} %copy-done.1), custom_call_target="tpu_custom_call" | custom-call | flops 1 | bytes 1 | tf_op jit(solution)/shard_map/right_units/pallas_call | solution.py:147
  9.5 0.0 copy-done
  9.5 0.0 copy-done.2
  9.5 1.5 %left_side.1.left = bf16[1104,2304]{1,0:T(8,128)(2,1)S(1)} custom-call(s32[16,32]{1,0:T(8,128)S(1)} %copy-done.2, bf16[1104,2208]{1,0:T(8,128)(2,1)S(1)} %copy-done), custom_call_target="tpu_custom_call" | custom-call | flops 1 | bytes 1 | tf_op jit(solution)/shard_map/left_side/pallas_call | solution.py:203
  11.0 1.3 %collective-permute-done.2.refs_1_ = bf16[38,16,128]{2,1,0:T(8,128)(2,1)S(1)} collective-permute-done((bf16[38,16,128]{2,1,0:T(8,128)(2,1)S(1)}, bf16[38,16,128]{2,1,0:T(8,128)(2,1)S(1)}, u32[]{:S(2)}, u32[]{:S(2)}) %collective-permute-start.2) | collective-permute-done | bytes 155680 | tf_op jit(solution)/shard_map/ppermute | solution.py:357
  12.3 0.1 collective-permute-start.6
  12.4 1.8 %collective-permute-start.5 = (bf16[76,16,128]{2,1,0:T(8,128)(2,1)S(1)}, bf16[76,16,128]{2,1,0:T(8,128)(2,1)S(1)}, u32[]{:S(2)}, u32[]{:S(2)}) collective-permute-start(bf16[76,16,128]{2,1,0:T(8,128)(2,1)S(1)} %constant_dynamic-update-slice_fusion), channel_id=1, source_target_pairs={{0,16},{4,12},{8,24},{12,4},{16,0},{20,28},{24,8},{28,20},{1,17},{... | collective-permute-start | bytes 933896 | tf_op jit(solution)/shard_map/ppermute | solution.py:354
  14.2 1.5 %collective-permute-start.4 = (bf16[76,16,128]{2,1,0:T(8,128)(2,1)S(1)}, bf16[76,16,128]{2,1,0:T(8,128)(2,1)S(1)}, u32[]{:S(2)}, u32[]{:S(2)}) collective-permute-start(bf16[76,16,128]{2,1,0:T(8,128)(2,1)S(1)} %constant_dynamic-update-slice_fusion), channel_id=1, source_target_pairs={{0,8},{4,20},{8,0},{12,28},{16,24},{20,4},{24,16},{28,12},{1,9},{5... | collective-permute-start | bytes 933896 | tf_op jit(solution)/shard_map/ppermute | solution.py:354
  15.7 4.9 %sides.1 = (bf16[1104,1024]{1,0:T(8,128)(2,1)S(1)}, bf16[1104,512]{1,0:T(8,128)(2,1)S(1)}, bf16[1104,512]{1,0:T(8,128)(2,1)S(1)}, bf16[1104,512]{1,0:T(8,128)(2,1)S(1)}, bf16[1104,512]{1,0:T(8,128)(2,1)S(1)}) custom-call(bf16[1104,2304]{1,0:T(8,128)(2,1)S(1)} %left_side.1.left, s32[64]{0:T(128)S(1)} %mark.5.point.value), custom_call_target="tpu_custom_call" | custom-call | flops 1 | bytes 1 | tf_op jit(solution)/shard_map/sides/pallas_call | solution.py:249
  20.6 0.0 collective-permute-done.refs_4_
  20.7 0.0 collective-permute-done.1.refs_5_
  20.7 1.4 %collective-permute-start.3 = (bf16[76,16,128]{2,1,0:T(8,128)(2,1)S(1)}, bf16[76,16,128]{2,1,0:T(8,128)(2,1)S(1)}, u32[]{:S(2)}, u32[]{:S(2)}) collective-permute-start(bf16[76,16,128]{2,1,0:T(8,128)(2,1)S(1)} %pad_maximum_fusion.2), channel_id=1, source_target_pairs={{0,8},{4,20},{8,0},{12,28},{16,24},{20,4},{24,16},{28,12},{1,9},{5... | collective-permute-start | bytes 933896 | tf_op jit(solution)/shard_map/ppermute | solution.py:354
  22.2 0.0 collective-permute-done.5.refs_3_
  22.2 0.0 collective-permute-done.4.refs_2_
  22.2 0.1 pad_maximum_fusion.1
  22.3 1.8 %collective-permute-start.8 = (bf16[152,16,128]{2,1,0:T(8,128)(2,1)S(1)}, bf16[152,16,128]{2,1,0:T(8,128)(2,1)S(1)}, u32[]{:S(2)}, u32[]{:S(2)}) collective-permute-start(bf16[152,16,128]{2,1,0:T(8,128)(2,1)S(1)} %pad_maximum_fusion.1), channel_id=1, source_target_pairs={{0,16},{4,12},{8,24},{12,4},{16,0},{20,28},{24,8},{28,20},{1,17},{... | collective-permute-start | bytes 1867784 | tf_op jit(solution)/shard_map/ppermute | solution.py:354
  24.2 0.1 collective-permute-start.9
  24.3 0.0 collective-permute-done.6.refs_6_
  24.3 3.2 %multiply.5.refs_0_ = f32[1104,1152]{1,0:T(8,128)S(1)} custom-call(bf16[1104,1024]{1,0:T(8,128)(2,1)S(1)} %get-tuple-element.61.left, bf16[38,16,128]{2,1,0:T(8,128)(2,1)S(1)} %right_units.3.refs_0_, bf16[38,16,128]{2,1,0:T(8,128)(2,1)S(1)} %collective-permute-done.2.refs_1_, bf16[76,16,128]{2,1,0:T(8,128)(2,1)S(1)} %collective-permute-done.4.refs_2_, ...), custom_call_target="tpu_custom_call" | custom-call | flops 1 | bytes 1 | tf_op jit(solution)/shard_map/multiply/pallas_call | solution.py:317
  27.5 2.5 %collective-permute-done.3.refs_1_ = bf16[76,16,128]{2,1,0:T(8,128)(2,1)S(1)} collective-permute-done((bf16[76,16,128]{2,1,0:T(8,128)(2,1)S(1)}, bf16[76,16,128]{2,1,0:T(8,128)(2,1)S(1)}, u32[]{:S(2)}, u32[]{:S(2)}) %collective-permute-start.3) | collective-permute-done | bytes 311328 | tf_op jit(solution)/shard_map/ppermute | solution.py:354
  30.1 1.0 %collective-permute-start.7 = (bf16[76,16,128]{2,1,0:T(8,128)(2,1)S(1)}, bf16[76,16,128]{2,1,0:T(8,128)(2,1)S(1)}, u32[]{:S(2)}, u32[]{:S(2)}) collective-permute-start(bf16[76,16,128]{2,1,0:T(8,128)(2,1)S(1)} %collective-permute-done.3.refs_1_), channel_id=1, source_target_pairs={{0,16},{4,12},{8,24},{12,4},{16,0},{20,28},{24,8},{28,20},{1,17},{... | collective-permute-start | bytes 933896 | tf_op jit(solution)/shard_map/ppermute | solution.py:354
  31.1 0.0 collective-permute-done.9.refs_1_
  31.1 1.7 %multiply.6.refs_0_ = f32[1104,1152]{1,0:T(8,128)S(1)} custom-call(bf16[1104,512]{1,0:T(8,128)(2,1)S(1)} %get-tuple-element.72.left, f32[1104,1152]{1,0:T(8,128)S(1)} %multiply.5.refs_0_, bf16[228,16,128]{2,1,0:T(8,128)(2,1)S(1)} %collective-permute-done.9.refs_1_, s32[64]{0:T(128)S(1)} %mark.8.refs_2_.value), custom_call_target="tpu_custom_call" | custom-call | flops 1 | bytes 1 | tf_op jit(solution)/shard_map/multiply/pallas_call | solution.py:317
  32.9 0.4 collective-permute-done.8.refs_2_
  33.3 0.1 pad_maximum_fusion
  33.4 1.3 %collective-permute-start.10 = (bf16[228,16,128]{2,1,0:T(8,128)(2,1)S(1)}, bf16[228,16,128]{2,1,0:T(8,128)(2,1)S(1)}, u32[]{:S(2)}, u32[]{:S(2)}) collective-permute-start(bf16[228,16,128]{2,1,0:T(8,128)(2,1)S(1)} %pad_maximum_fusion), channel_id=1, source_target_pairs={{0,4},{4,0},{8,12},{12,8},{16,20},{20,16},{24,28},{28,24},{1,5},{5... | collective-permute-start | bytes 2801672 | tf_op jit(solution)/shard_map/ppermute | solution.py:354
  34.7 1.8 %multiply.7.refs_0_ = f32[1104,1152]{1,0:T(8,128)S(1)} custom-call(bf16[1104,512]{1,0:T(8,128)(2,1)S(1)} %get-tuple-element.71.left, f32[1104,1152]{1,0:T(8,128)S(1)} %multiply.6.refs_0_, bf16[76,16,128]{2,1,0:T(8,128)(2,1)S(1)} %collective-permute-done.3.refs_1_, bf16[152,16,128]{2,1,0:T(8,128)(2,1)S(1)} %collective-permute-done.8.refs_2_), custom_call_target="tpu_custom_call" | custom-call | flops 1 | bytes 1 | tf_op jit(solution)/shard_map/multiply/pallas_call | solution.py:317
  36.5 0.4 collective-permute-done.7.refs_1_
  37.0 0.5 %collective-permute-start.11 = (bf16[76,16,128]{2,1,0:T(8,128)(2,1)S(1)}, bf16[76,16,128]{2,1,0:T(8,128)(2,1)S(1)}, u32[]{:S(2)}, u32[]{:S(2)}) collective-permute-start(bf16[76,16,128]{2,1,0:T(8,128)(2,1)S(1)} %collective-permute-done.7.refs_1_), channel_id=1, source_target_pairs={{0,4},{4,0},{8,12},{12,8},{16,20},{20,16},{24,28},{28,24},{1,5},{5... | collective-permute-start | bytes 933896 | tf_op jit(solution)/shard_map/ppermute | solution.py:354
  37.5 0.0 collective-permute-done.10.refs_1_
  37.5 1.7 %multiply.8.refs_0_ = f32[1104,1152]{1,0:T(8,128)S(1)} custom-call(bf16[1104,512]{1,0:T(8,128)(2,1)S(1)} %get-tuple-element.58.left, f32[1104,1152]{1,0:T(8,128)S(1)} %multiply.7.refs_0_, bf16[228,16,128]{2,1,0:T(8,128)(2,1)S(1)} %collective-permute-done.10.refs_1_, s32[64]{0:T(128)S(1)} %mark.9.refs_2_), custom_call_target="tpu_custom_call" | custom-call | flops 1 | bytes 1 | tf_op jit(solution)/shard_map/multiply/pallas_call | solution.py:317
  39.2 0.0 collective-permute-done.11.refs_2_
  39.2 2.5 %multiply.9 = bf16[1104,1104]{1,0:T(8,128)(2,1)} custom-call(bf16[1104,512]{1,0:T(8,128)(2,1)S(1)} %get-tuple-element.57.left, f32[1104,1152]{1,0:T(8,128)S(1)} %multiply.8.refs_0_, bf16[76,16,128]{2,1,0:T(8,128)(2,1)S(1)} %collective-permute-done.7.refs_1_, bf16[76,16,128]{2,1,0:T(8,128)(2,1)S(1)} %collective-permute-done.11.refs_2_), custom_call_target="tpu_custom_call" | custom-call | flops 1 | bytes 1 | tf_op jit(solution)/shard_map/multiply/pallas_call | solution.py:317
  (17 shorter events, 0.3 us)
Async XLA Ops:
  0.7 1.1 %copy-start.1 = (bf16[69,4416]{1,0:T(8,128)(2,1)S(1)}, bf16[69,4416]{1,0:T(8,128)(2,1)}, u32[]{:S(2)}) copy-start(bf16[69,4416]{1,0:T(8,128)(2,1)} %raw.3) | copy-start | bytes 1828228
  1.8 7.7 %copy-start = (bf16[1104,2208]{1,0:T(8,128)(2,1)S(1)}, bf16[1104,2208]{1,0:T(8,128)(2,1)}, u32[]{:S(2)}) copy-start(bf16[1104,2208]{1,0:T(8,128)(2,1)} %rows_in.1) | copy-start | bytes 14625796
  1.8 7.7 %copy-start.2 = (s32[16,32]{1,0:T(8,128)S(1)}, s32[16,32]{1,0:T(8,128)}, u32[]{:S(2)}) copy-start(s32[16,32]{1,0:T(8,128)} %pattern.1) | copy-start | bytes 6148
  3.0 9.3 %collective-permute-start.2 = (bf16[38,16,128]{2,1,0:T(8,128)(2,1)S(1)}, bf16[38,16,128]{2,1,0:T(8,128)(2,1)S(1)}, u32[]{:S(2)}, u32[]{:S(2)}) collective-permute-start(bf16[38,16,128]{2,1,0:T(8,128)(2,1)S(1)} %get-tuple-element.47), channel_id=1, source_target_pairs={{0,1},{1,0},{2,3},{3,2},{4,5},{5,4},{6,7},{7,6},{8,9},{9,8},{10,11... | collective-permute-start | bytes 466952 | tf_op jit(solution)/shard_map/ppermute | solution.py:357
  6.0 14.6 %collective-permute-start = (bf16[38,16,128]{2,1,0:T(8,128)(2,1)S(1)}, bf16[38,16,128]{2,1,0:T(8,128)(2,1)S(1)}, u32[]{:S(2)}, u32[]{:S(2)}) collective-permute-start(bf16[38,16,128]{2,1,0:T(8,128)(2,1)S(1)} %get-tuple-element.45), channel_id=1, source_target_pairs={{0,2},{1,3},{2,0},{3,1},{4,6},{5,7},{6,4},{7,5},{8,10},{9,11},{10,... | collective-permute-start | bytes 466952 | tf_op jit(solution)/shard_map/ppermute | solution.py:357
  8.6 12.0 %collective-permute-start.1 = (bf16[38,16,128]{2,1,0:T(8,128)(2,1)S(1)}, bf16[38,16,128]{2,1,0:T(8,128)(2,1)S(1)}, u32[]{:S(2)}, u32[]{:S(2)}) collective-permute-start(bf16[38,16,128]{2,1,0:T(8,128)(2,1)S(1)} %get-tuple-element.46), channel_id=1, source_target_pairs={{0,3},{1,2},{2,1},{3,0},{4,7},{5,6},{6,5},{7,4},{8,11},{9,10},{10,... | collective-permute-start | bytes 466952 | tf_op jit(solution)/shard_map/ppermute | solution.py:357
  12.3 12.0 %collective-permute-start.6 = (bf16[76,16,128]{2,1,0:T(8,128)(2,1)S(1)}, bf16[76,16,128]{2,1,0:T(8,128)(2,1)S(1)}, u32[]{:S(2)}, u32[]{:S(2)}) collective-permute-start(bf16[76,16,128]{2,1,0:T(8,128)(2,1)S(1)} %constant_dynamic-update-slice_fusion), channel_id=1, source_target_pairs={{0,4},{4,0},{8,12},{12,8},{16,20},{20,16},{24,28},{28,24},{1,5},{5... | collective-permute-start | bytes 933896 | tf_op jit(solution)/shard_map/ppermute | solution.py:354
  12.4 9.7 %collective-permute-start.5 = (bf16[76,16,128]{2,1,0:T(8,128)(2,1)S(1)}, bf16[76,16,128]{2,1,0:T(8,128)(2,1)S(1)}, u32[]{:S(2)}, u32[]{:S(2)}) collective-permute-start(bf16[76,16,128]{2,1,0:T(8,128)(2,1)S(1)} %constant_dynamic-update-slice_fusion), channel_id=1, source_target_pairs={{0,16},{4,12},{8,24},{12,4},{16,0},{20,28},{24,8},{28,20},{1,17},{... | collective-permute-start | bytes 933896 | tf_op jit(solution)/shard_map/ppermute | solution.py:354
  14.2 8.0 %collective-permute-start.4 = (bf16[76,16,128]{2,1,0:T(8,128)(2,1)S(1)}, bf16[76,16,128]{2,1,0:T(8,128)(2,1)S(1)}, u32[]{:S(2)}, u32[]{:S(2)}) collective-permute-start(bf16[76,16,128]{2,1,0:T(8,128)(2,1)S(1)} %constant_dynamic-update-slice_fusion), channel_id=1, source_target_pairs={{0,8},{4,20},{8,0},{12,28},{16,24},{20,4},{24,16},{28,12},{1,9},{5... | collective-permute-start | bytes 933896 | tf_op jit(solution)/shard_map/ppermute | solution.py:354
  20.7 9.3 %collective-permute-start.3 = (bf16[76,16,128]{2,1,0:T(8,128)(2,1)S(1)}, bf16[76,16,128]{2,1,0:T(8,128)(2,1)S(1)}, u32[]{:S(2)}, u32[]{:S(2)}) collective-permute-start(bf16[76,16,128]{2,1,0:T(8,128)(2,1)S(1)} %pad_maximum_fusion.2), channel_id=1, source_target_pairs={{0,8},{4,20},{8,0},{12,28},{16,24},{20,4},{24,16},{28,12},{1,9},{5... | collective-permute-start | bytes 933896 | tf_op jit(solution)/shard_map/ppermute | solution.py:354
  22.3 11.0 %collective-permute-start.8 = (bf16[152,16,128]{2,1,0:T(8,128)(2,1)S(1)}, bf16[152,16,128]{2,1,0:T(8,128)(2,1)S(1)}, u32[]{:S(2)}, u32[]{:S(2)}) collective-permute-start(bf16[152,16,128]{2,1,0:T(8,128)(2,1)S(1)} %pad_maximum_fusion.1), channel_id=1, source_target_pairs={{0,16},{4,12},{8,24},{12,4},{16,0},{20,28},{24,8},{28,20},{1,17},{... | collective-permute-start | bytes 1867784 | tf_op jit(solution)/shard_map/ppermute | solution.py:354
  24.2 6.9 %collective-permute-start.9 = (bf16[228,16,128]{2,1,0:T(8,128)(2,1)S(1)}, bf16[228,16,128]{2,1,0:T(8,128)(2,1)S(1)}, u32[]{:S(2)}, u32[]{:S(2)}) collective-permute-start(bf16[228,16,128]{2,1,0:T(8,128)(2,1)S(1)} %constant_dynamic-update-slice_fusion.2), channel_id=1, source_target_pairs={{0,4},{4,0},{8,12},{12,8},{16,20},{20,16},{24,28},{28,24},{1,5},{5... | collective-permute-start | bytes 2801672 | tf_op jit(solution)/shard_map/ppermute | solution.py:354
  30.1 6.9 %collective-permute-start.7 = (bf16[76,16,128]{2,1,0:T(8,128)(2,1)S(1)}, bf16[76,16,128]{2,1,0:T(8,128)(2,1)S(1)}, u32[]{:S(2)}, u32[]{:S(2)}) collective-permute-start(bf16[76,16,128]{2,1,0:T(8,128)(2,1)S(1)} %collective-permute-done.3.refs_1_), channel_id=1, source_target_pairs={{0,16},{4,12},{8,24},{12,4},{16,0},{20,28},{24,8},{28,20},{1,17},{... | collective-permute-start | bytes 933896 | tf_op jit(solution)/shard_map/ppermute | solution.py:354
  33.4 4.1 %collective-permute-start.10 = (bf16[228,16,128]{2,1,0:T(8,128)(2,1)S(1)}, bf16[228,16,128]{2,1,0:T(8,128)(2,1)S(1)}, u32[]{:S(2)}, u32[]{:S(2)}) collective-permute-start(bf16[228,16,128]{2,1,0:T(8,128)(2,1)S(1)} %pad_maximum_fusion), channel_id=1, source_target_pairs={{0,4},{4,0},{8,12},{12,8},{16,20},{20,16},{24,28},{28,24},{1,5},{5... | collective-permute-start | bytes 2801672 | tf_op jit(solution)/shard_map/ppermute | solution.py:354
  37.0 2.3 %collective-permute-start.11 = (bf16[76,16,128]{2,1,0:T(8,128)(2,1)S(1)}, bf16[76,16,128]{2,1,0:T(8,128)(2,1)S(1)}, u32[]{:S(2)}, u32[]{:S(2)}) collective-permute-start(bf16[76,16,128]{2,1,0:T(8,128)(2,1)S(1)} %collective-permute-done.7.refs_1_), channel_id=1, source_target_pairs={{0,4},{4,0},{8,12},{12,8},{16,20},{20,16},{24,28},{28,24},{1,5},{5... | collective-permute-start | bytes 933896 | tf_op jit(solution)/shard_map/ppermute | solution.py:354

commit v5 on v4

--- a/solution.py
+++ b/solution.py
@@ -436,7 +436,8 @@
     soon = [key for key in late if key[1] <= full // 2 and key[0] in rest]
     then = [key for key in late if key not in soon]
     near = [(0, 0), (1, 0)]
-    groups = [(ready, near), ([], [key for key in ready if key not in near]), (late, []), ([], late), (tail, tail)]
+    far = [key for key in ready if key not in near]
+    groups = [(ready, near), (soon, far), (then, soon), (tail, then), ([], tail)]
 
     left = left_side(slab_rows, slab_pattern, up(slab_rows.shape[1], 2 * LANES))
     left, point = tied([(1, 0)], [], [left, scalars])
@@ -458,16 +459,17 @@
     wave(deep)
     point = mark(point, 5)
     point, total = tied([], [key for key in ready if key not in near], [point, total])
-    total = multiply(lefts[1], total, other([key for key in ready if key not in near]), columns, after=[point])
+    total = multiply(lefts[1], total, own(soon) + other(far), columns, after=[point])
     (total,) = tied(then, [], [total])
-    swap(late)
-    total = multiply(lefts[2], total, own(late), columns)
+    swap(soon)
+    swap(then)
+    total = multiply(lefts[2], total, own(then) + other(soon), columns)
     total, point = tied(tail, [], [total, point])
     swap(tail)
-    point = mark(point, 8)
-    (point,) = tied([], late, [point])
-    total = multiply(lefts[3], total, other(late), columns, after=[point])
-    return multiply(lefts[4], total, own(tail) + other(tail), columns, final=True)
+    point = mark(point, 5)
+    (point,) = tied([], then, [point])
+    total = multiply(lefts[3], total, own(tail) + other(then), columns, after=[point])
+    return multiply(lefts[4], total, other(tail), columns, final=True)
 
 
 def solution(mesh):

time: 42.4 us -> 41.8 us (0.986)
    ppermute x9 -> x10, starting transfers between devices: 9.56 us -> 9.13 us  [along_row(): lax.ppermute(value, 'row', [(i, i ^ move[i & 1]) for i in range(n_row)])]
    ppermute x9 -> x10, waiting for transfers between devices: 3.34 us -> 3.33 us  [along_row(): lax.ppermute(value, 'row', [(i, i ^ move[i & 1]) for i in range(n_row)])]
  transfers between devices with their start and end apart: 12 -> 13, of which waited for: 4 -> 3; matrix products, arithmetic and copies ran while one was open for 1% -> 1% of each run, Pallas kernels for 38% -> 40%
where the time goes in v5:
time: 41.8 us; the launch traced here: 41.3 us
  Pallas kernels  19.6 us (47%)
  starting transfers between devices  14.8 us (35%)
  waiting for transfers between devices  4.68 us (11%)
  local copies, waits for them, and re-layouts  1.25 us (3%)
  other arithmetic  0.77 us (2%)
    pallas_call x5, Pallas kernels, multiply(): pl.pallas_call(functools.partial(multiply_kernel, [(at, unit[1]) for at,...  11.1 us
    ppermute x10, starting transfers between devices, along_row(): lax.ppermute(value, 'row', [(i, i ^ move[i & 1]) for i in range(n_row)])  9.13 us
    ppermute x3, starting transfers between devices, along_col(): return lax.ppermute(value, 'col', [(i, i ^ step) for i in range(n_col)])  5.67 us
    pallas_call x1, Pallas kernels, sides(): pl.pallas_call(functools.partial(side_kernel, n_col, groups), out_shape=[...  4.95 us
    ppermute x10, waiting for transfers between devices, along_row(): lax.ppermute(value, 'row', [(i, i ^ move[i & 1]) for i in range(n_row)])  3.33 us
    pallas_call x2, Pallas kernels, right_units(): pl.pallas_call(functools.partial(right_kernel, n_col, steps), out_shape=[...  2.02 us
    pallas_call x1, Pallas kernels, left_side(): pl.pallas_call(functools.partial(left_kernel, high), out_shape=jax.ShapeD...  1.48 us
    ppermute x3, waiting for transfers between devices, along_col(): return lax.ppermute(value, 'col', [(i, i ^ step) for i in range(n_col)])  1.35 us
  transfers between devices with their start and end apart: 13, of which 3 were waited for; matrix products, arithmetic and copies ran while one was open for 1% of the time, Pallas kernels for 40%

profile of v5, /device:TPU:0, one launch (start us, length us, event | category | flops | bytes accessed | tf_op | source)
XLA Modules:
  0.0 41.3 jit_solution(7608889940438950829)
XLA Ops:
  0.0 0.7 %bitcast_add_fusion.scalars.value = s32[64]{0:T(128)S(1)} fusion(s32[64]{0:T(128)} %param.9, s32[1,64]{1,0:T(1,128)} %param.8), kind=kLoop, calls=%fused_computation.10 | loop fusion | flops 128 | bytes 768 | tf_op jit(solution)/shard_map/add | solution.py:401
  0.7 0.0 copy-start.1
  0.7 1.1 %copy-done.1 = bf16[69,4416]{1,0:T(8,128)(2,1)S(1)} copy-done((bf16[69,4416]{1,0:T(8,128)(2,1)S(1)}, bf16[69,4416]{1,0:T(8,128)(2,1)}, u32[]{:S(2)}) %copy-start.1) | copy-done | bytes 609432
  1.8 0.0 copy-start
  1.8 0.0 copy-start.2
  1.8 1.2 %right_units.2 = (bf16[38,16,128]{2,1,0:T(8,128)(2,1)S(1)}, bf16[38,16,128]{2,1,0:T(8,128)(2,1)S(1)}, bf16[38,16,128]{2,1,0:T(8,128)(2,1)S(1)}) custom-call(s32[64]{0:T(128)S(1)} %bitcast_add_fusion.scalars.value, bf16[69,4416]{1,0:T(8,128)(2,1)S(1)} %copy-done.1), custom_call_target="tpu_custom_call" | custom-call | flops 8000000000 | bytes 1 | tf_op jit(solution)/shard_map/right_units/pallas_call | solution.py:147
  3.0 3.1 %collective-permute-start.2 = (bf16[38,16,128]{2,1,0:T(8,128)(2,1)S(1)}, bf16[38,16,128]{2,1,0:T(8,128)(2,1)S(1)}, u32[]{:S(2)}, u32[]{:S(2)}) collective-permute-start(bf16[38,16,128]{2,1,0:T(8,128)(2,1)S(1)} %get-tuple-element.47), channel_id=1, source_target_pairs={{0,1},{1,0},{2,3},{3,2},{4,5},{5,4},{6,7},{7,6},{8,9},{9,8},{10,11... | collective-permute-start | bytes 466952 | tf_op jit(solution)/shard_map/ppermute | solution.py:357
  6.0 2.6 %collective-permute-start = (bf16[38,16,128]{2,1,0:T(8,128)(2,1)S(1)}, bf16[38,16,128]{2,1,0:T(8,128)(2,1)S(1)}, u32[]{:S(2)}, u32[]{:S(2)}) collective-permute-start(bf16[38,16,128]{2,1,0:T(8,128)(2,1)S(1)} %get-tuple-element.45), channel_id=1, source_target_pairs={{0,2},{1,3},{2,0},{3,1},{4,6},{5,7},{6,4},{7,5},{8,10},{9,11},{10,... | collective-permute-start | bytes 466952 | tf_op jit(solution)/shard_map/ppermute | solution.py:357
  8.6 0.0 collective-permute-start.1
  8.6 0.8 %right_units.3.refs_0_ = bf16[38,16,128]{2,1,0:T(8,128)(2,1)S(1)} custom-call(s32[64]{0:T(128)S(1)} %bitcast_add_fusion.scalars.value, bf16[69,4416]{1,0:T(8,128)(2,1)S(1)} %copy-done.1), custom_call_target="tpu_custom_call" | custom-call | flops 1 | bytes 1 | tf_op jit(solution)/shard_map/right_units/pallas_call | solution.py:147
  9.5 0.0 copy-done
  9.5 0.0 copy-done.2
  9.5 1.5 %left_side.1.left = bf16[1104,2304]{1,0:T(8,128)(2,1)S(1)} custom-call(s32[16,32]{1,0:T(8,128)S(1)} %copy-done.2, bf16[1104,2208]{1,0:T(8,128)(2,1)S(1)} %copy-done), custom_call_target="tpu_custom_call" | custom-call | flops 1 | bytes 1 | tf_op jit(solution)/shard_map/left_side/pallas_call | solution.py:203
  11.0 1.3 %collective-permute-done.2.refs_1_ = bf16[38,16,128]{2,1,0:T(8,128)(2,1)S(1)} collective-permute-done((bf16[38,16,128]{2,1,0:T(8,128)(2,1)S(1)}, bf16[38,16,128]{2,1,0:T(8,128)(2,1)S(1)}, u32[]{:S(2)}, u32[]{:S(2)}) %collective-permute-start.2) | collective-permute-done | bytes 155680 | tf_op jit(solution)/shard_map/ppermute | solution.py:357
  12.3 0.1 collective-permute-start.6
  12.4 1.8 %collective-permute-start.5 = (bf16[76,16,128]{2,1,0:T(8,128)(2,1)S(1)}, bf16[76,16,128]{2,1,0:T(8,128)(2,1)S(1)}, u32[]{:S(2)}, u32[]{:S(2)}) collective-permute-start(bf16[76,16,128]{2,1,0:T(8,128)(2,1)S(1)} %constant_dynamic-update-slice_fusion), channel_id=1, source_target_pairs={{0,16},{4,12},{8,24},{12,4},{16,0},{20,28},{24,8},{28,20},{1,17},{... | collective-permute-start | bytes 933896 | tf_op jit(solution)/shard_map/ppermute | solution.py:354
  14.2 1.5 %collective-permute-start.4 = (bf16[76,16,128]{2,1,0:T(8,128)(2,1)S(1)}, bf16[76,16,128]{2,1,0:T(8,128)(2,1)S(1)}, u32[]{:S(2)}, u32[]{:S(2)}) collective-permute-start(bf16[76,16,128]{2,1,0:T(8,128)(2,1)S(1)} %constant_dynamic-update-slice_fusion), channel_id=1, source_target_pairs={{0,8},{4,20},{8,0},{12,28},{16,24},{20,4},{24,16},{28,12},{1,9},{5... | collective-permute-start | bytes 933896 | tf_op jit(solution)/shard_map/ppermute | solution.py:354
  15.7 4.9 %sides.1 = (bf16[1104,1024]{1,0:T(8,128)(2,1)S(1)}, bf16[1104,768]{1,0:T(8,128)(2,1)S(1)}, bf16[1104,512]{1,0:T(8,128)(2,1)S(1)}, bf16[1104,512]{1,0:T(8,128)(2,1)S(1)}, bf16[1104,256]{1,0:T(8,128)(2,1)S(1)}) custom-call(bf16[1104,2304]{1,0:T(8,128)(2,1)S(1)} %left_side.1.left, s32[64]{0:T(128)S(1)} %mark.5.point.value), custom_call_target="tpu_custom_call" | custom-call | flops 1 | bytes 1 | tf_op jit(solution)/shard_map/sides/pallas_call | solution.py:249
  20.7 0.0 collective-permute-done.refs_4_
  20.7 0.0 collective-permute-done.1.refs_5_
  20.7 1.4 %collective-permute-start.3 = (bf16[76,16,128]{2,1,0:T(8,128)(2,1)S(1)}, bf16[76,16,128]{2,1,0:T(8,128)(2,1)S(1)}, u32[]{:S(2)}, u32[]{:S(2)}) collective-permute-start(bf16[76,16,128]{2,1,0:T(8,128)(2,1)S(1)} %pad_maximum_fusion.1), channel_id=1, source_target_pairs={{0,8},{4,20},{8,0},{12,28},{16,24},{20,4},{24,16},{28,12},{1,9},{5... | collective-permute-start | bytes 933896 | tf_op jit(solution)/shard_map/ppermute | solution.py:354
  22.2 0.0 collective-permute-done.5.refs_3_
  22.2 0.0 collective-permute-done.4.refs_2_
  22.2 0.1 pad_maximum_fusion
  22.3 1.8 %collective-permute-start.8 = (bf16[152,16,128]{2,1,0:T(8,128)(2,1)S(1)}, bf16[152,16,128]{2,1,0:T(8,128)(2,1)S(1)}, u32[]{:S(2)}, u32[]{:S(2)}) collective-permute-start(bf16[152,16,128]{2,1,0:T(8,128)(2,1)S(1)} %pad_maximum_fusion), channel_id=1, source_target_pairs={{0,16},{4,12},{8,24},{12,4},{16,0},{20,28},{24,8},{28,20},{1,17},{... | collective-permute-start | bytes 1867784 | tf_op jit(solution)/shard_map/ppermute | solution.py:354
  24.2 0.1 collective-permute-start.9
  24.3 0.0 collective-permute-done.6.refs_6_
  24.3 3.2 %multiply.5.refs_0_ = f32[1104,1152]{1,0:T(8,128)S(1)} custom-call(bf16[1104,1024]{1,0:T(8,128)(2,1)S(1)} %get-tuple-element.61.left, bf16[38,16,128]{2,1,0:T(8,128)(2,1)S(1)} %right_units.3.refs_0_, bf16[38,16,128]{2,1,0:T(8,128)(2,1)S(1)} %collective-permute-done.2.refs_1_, bf16[76,16,128]{2,1,0:T(8,128)(2,1)S(1)} %collective-permute-done.4.refs_2_, ...), custom_call_target="tpu_custom_call" | custom-call | flops 1 | bytes 1 | tf_op jit(solution)/shard_map/multiply/pallas_call | solution.py:317
  27.5 2.6 %collective-permute-done.3.refs_1_ = bf16[76,16,128]{2,1,0:T(8,128)(2,1)S(1)} collective-permute-done((bf16[76,16,128]{2,1,0:T(8,128)(2,1)S(1)}, bf16[76,16,128]{2,1,0:T(8,128)(2,1)S(1)}, u32[]{:S(2)}, u32[]{:S(2)}) %collective-permute-start.3) | collective-permute-done | bytes 311328 | tf_op jit(solution)/shard_map/ppermute | solution.py:354
  30.1 0.0 collective-permute-start.10
  30.1 1.0 %collective-permute-start.7 = (bf16[76,16,128]{2,1,0:T(8,128)(2,1)S(1)}, bf16[76,16,128]{2,1,0:T(8,128)(2,1)S(1)}, u32[]{:S(2)}, u32[]{:S(2)}) collective-permute-start(bf16[76,16,128]{2,1,0:T(8,128)(2,1)S(1)} %collective-permute-done.3.refs_1_), channel_id=1, source_target_pairs={{0,16},{4,12},{8,24},{12,4},{16,0},{20,28},{24,8},{28,20},{1,17},{... | collective-permute-start | bytes 933896 | tf_op jit(solution)/shard_map/ppermute | solution.py:354
  31.1 0.0 collective-permute-done.9.refs_2_
  31.1 2.5 %multiply.6.refs_0_ = f32[1104,1152]{1,0:T(8,128)S(1)} custom-call(bf16[1104,768]{1,0:T(8,128)(2,1)S(1)} %get-tuple-element.72.left, f32[1104,1152]{1,0:T(8,128)S(1)} %multiply.5.refs_0_, bf16[76,16,128]{2,1,0:T(8,128)(2,1)S(1)} %collective-permute-done.3.refs_1_, bf16[228,16,128]{2,1,0:T(8,128)(2,1)S(1)} %collective-permute-done.9.refs_2_, ...), custom_call_target="tpu_custom_call" | custom-call | flops 1 | bytes 1 | tf_op jit(solution)/shard_map/multiply/pallas_call | solution.py:317
  33.6 0.0 collective-permute-done.8.refs_1_
  33.6 1.0 %collective-permute-start.11 = (bf16[152,16,128]{2,1,0:T(8,128)(2,1)S(1)}, bf16[152,16,128]{2,1,0:T(8,128)(2,1)S(1)}, u32[]{:S(2)}, u32[]{:S(2)}) collective-permute-start(bf16[152,16,128]{2,1,0:T(8,128)(2,1)S(1)} %collective-permute-done.8.refs_1_), channel_id=1, source_target_pairs={{0,4},{4,0},{8,12},{12,8},{16,20},{20,16},{24,28},{28,24},{1,5},{5... | collective-permute-start | bytes 1867784 | tf_op jit(solution)/shard_map/ppermute | solution.py:354
  34.6 0.0 collective-permute-done.10.refs_2_
  34.6 1.7 %multiply.7.refs_0_ = f32[1104,1152]{1,0:T(8,128)S(1)} custom-call(bf16[1104,512]{1,0:T(8,128)(2,1)S(1)} %get-tuple-element.71.left, f32[1104,1152]{1,0:T(8,128)S(1)} %multiply.6.refs_0_, bf16[152,16,128]{2,1,0:T(8,128)(2,1)S(1)} %collective-permute-done.8.refs_1_, bf16[76,16,128]{2,1,0:T(8,128)(2,1)S(1)} %collective-permute-done.10.refs_2_), custom_call_target="tpu_custom_call" | custom-call | flops 1 | bytes 1 | tf_op jit(solution)/shard_map/multiply/pallas_call | solution.py:317
  36.3 0.7 %collective-permute-done.7.refs_1_ = bf16[76,16,128]{2,1,0:T(8,128)(2,1)S(1)} collective-permute-done((bf16[76,16,128]{2,1,0:T(8,128)(2,1)S(1)}, bf16[76,16,128]{2,1,0:T(8,128)(2,1)S(1)}, u32[]{:S(2)}, u32[]{:S(2)}) %collective-permute-start.7) | collective-permute-done | bytes 311328 | tf_op jit(solution)/shard_map/ppermute | solution.py:354
  37.0 0.5 %collective-permute-start.12 = (bf16[76,16,128]{2,1,0:T(8,128)(2,1)S(1)}, bf16[76,16,128]{2,1,0:T(8,128)(2,1)S(1)}, u32[]{:S(2)}, u32[]{:S(2)}) collective-permute-start(bf16[76,16,128]{2,1,0:T(8,128)(2,1)S(1)} %collective-permute-done.7.refs_1_), channel_id=1, source_target_pairs={{0,4},{4,0},{8,12},{12,8},{16,20},{20,16},{24,28},{28,24},{1,5},{5... | collective-permute-start | bytes 933896 | tf_op jit(solution)/shard_map/ppermute | solution.py:354
  37.5 0.0 collective-permute-done.11.refs_2_
  37.5 1.7 %multiply.8.refs_0_ = f32[1104,1152]{1,0:T(8,128)S(1)} custom-call(bf16[1104,512]{1,0:T(8,128)(2,1)S(1)} %get-tuple-element.58.left, f32[1104,1152]{1,0:T(8,128)S(1)} %multiply.7.refs_0_, bf16[76,16,128]{2,1,0:T(8,128)(2,1)S(1)} %collective-permute-done.7.refs_1_, bf16[152,16,128]{2,1,0:T(8,128)(2,1)S(1)} %collective-permute-done.11.refs_2_, s32[64]{0:T(128)S(1)} %mark.9.refs_3_), custom_call_target="tpu_custom_call" | custom-call | flops 1 | bytes 1 | tf_op jit(solution)/shard_map/multiply/pallas_call | solution.py:317
  39.2 0.0 collective-permute-done.12.refs_1_
  39.3 2.0 %multiply.9 = bf16[1104,1104]{1,0:T(8,128)(2,1)} custom-call(bf16[1104,256]{1,0:T(8,128)(2,1)S(1)} %get-tuple-element.57.left, f32[1104,1152]{1,0:T(8,128)S(1)} %multiply.8.refs_0_, bf16[76,16,128]{2,1,0:T(8,128)(2,1)S(1)} %collective-permute-done.12.refs_1_), custom_call_target="tpu_custom_call" | custom-call | flops 1 | bytes 1 | tf_op jit(solution)/shard_map/multiply/pallas_call | solution.py:317
  (14 shorter events, 0.2 us)
Async XLA Ops:
  0.7 1.1 %copy-start.1 = (bf16[69,4416]{1,0:T(8,128)(2,1)S(1)}, bf16[69,4416]{1,0:T(8,128)(2,1)}, u32[]{:S(2)}) copy-start(bf16[69,4416]{1,0:T(8,128)(2,1)} %raw.3) | copy-start | bytes 1828228
  1.8 7.7 %copy-start = (bf16[1104,2208]{1,0:T(8,128)(2,1)S(1)}, bf16[1104,2208]{1,0:T(8,128)(2,1)}, u32[]{:S(2)}) copy-start(bf16[1104,2208]{1,0:T(8,128)(2,1)} %rows_in.1) | copy-start | bytes 14625796
  1.8 7.7 %copy-start.2 = (s32[16,32]{1,0:T(8,128)S(1)}, s32[16,32]{1,0:T(8,128)}, u32[]{:S(2)}) copy-start(s32[16,32]{1,0:T(8,128)} %pattern.1) | copy-start | bytes 6148
  3.0 9.3 %collective-permute-start.2 = (bf16[38,16,128]{2,1,0:T(8,128)(2,1)S(1)}, bf16[38,16,128]{2,1,0:T(8,128)(2,1)S(1)}, u32[]{:S(2)}, u32[]{:S(2)}) collective-permute-start(bf16[38,16,128]{2,1,0:T(8,128)(2,1)S(1)} %get-tuple-element.47), channel_id=1, source_target_pairs={{0,1},{1,0},{2,3},{3,2},{4,5},{5,4},{6,7},{7,6},{8,9},{9,8},{10,11... | collective-permute-start | bytes 466952 | tf_op jit(solution)/shard_map/ppermute | solution.py:357
  6.0 14.6 %collective-permute-start = (bf16[38,16,128]{2,1,0:T(8,128)(2,1)S(1)}, bf16[38,16,128]{2,1,0:T(8,128)(2,1)S(1)}, u32[]{:S(2)}, u32[]{:S(2)}) collective-permute-start(bf16[38,16,128]{2,1,0:T(8,128)(2,1)S(1)} %get-tuple-element.45), channel_id=1, source_target_pairs={{0,2},{1,3},{2,0},{3,1},{4,6},{5,7},{6,4},{7,5},{8,10},{9,11},{10,... | collective-permute-start | bytes 466952 | tf_op jit(solution)/shard_map/ppermute | solution.py:357
  8.6 12.1 %collective-permute-start.1 = (bf16[38,16,128]{2,1,0:T(8,128)(2,1)S(1)}, bf16[38,16,128]{2,1,0:T(8,128)(2,1)S(1)}, u32[]{:S(2)}, u32[]{:S(2)}) collective-permute-start(bf16[38,16,128]{2,1,0:T(8,128)(2,1)S(1)} %get-tuple-element.46), channel_id=1, source_target_pairs={{0,3},{1,2},{2,1},{3,0},{4,7},{5,6},{6,5},{7,4},{8,11},{9,10},{10,... | collective-permute-start | bytes 466952 | tf_op jit(solution)/shard_map/ppermute | solution.py:357
  12.3 12.0 %collective-permute-start.6 = (bf16[76,16,128]{2,1,0:T(8,128)(2,1)S(1)}, bf16[76,16,128]{2,1,0:T(8,128)(2,1)S(1)}, u32[]{:S(2)}, u32[]{:S(2)}) collective-permute-start(bf16[76,16,128]{2,1,0:T(8,128)(2,1)S(1)} %constant_dynamic-update-slice_fusion), channel_id=1, source_target_pairs={{0,4},{4,0},{8,12},{12,8},{16,20},{20,16},{24,28},{28,24},{1,5},{5... | collective-permute-start | bytes 933896 | tf_op jit(solution)/shard_map/ppermute | solution.py:354
  12.4 9.7 %collective-permute-start.5 = (bf16[76,16,128]{2,1,0:T(8,128)(2,1)S(1)}, bf16[76,16,128]{2,1,0:T(8,128)(2,1)S(1)}, u32[]{:S(2)}, u32[]{:S(2)}) collective-permute-start(bf16[76,16,128]{2,1,0:T(8,128)(2,1)S(1)} %constant_dynamic-update-slice_fusion), channel_id=1, source_target_pairs={{0,16},{4,12},{8,24},{12,4},{16,0},{20,28},{24,8},{28,20},{1,17},{... | collective-permute-start | bytes 933896 | tf_op jit(solution)/shard_map/ppermute | solution.py:354
  14.2 8.0 %collective-permute-start.4 = (bf16[76,16,128]{2,1,0:T(8,128)(2,1)S(1)}, bf16[76,16,128]{2,1,0:T(8,128)(2,1)S(1)}, u32[]{:S(2)}, u32[]{:S(2)}) collective-permute-start(bf16[76,16,128]{2,1,0:T(8,128)(2,1)S(1)} %constant_dynamic-update-slice_fusion), channel_id=1, source_target_pairs={{0,8},{4,20},{8,0},{12,28},{16,24},{20,4},{24,16},{28,12},{1,9},{5... | collective-permute-start | bytes 933896 | tf_op jit(solution)/shard_map/ppermute | solution.py:354
  20.7 9.4 %collective-permute-start.3 = (bf16[76,16,128]{2,1,0:T(8,128)(2,1)S(1)}, bf16[76,16,128]{2,1,0:T(8,128)(2,1)S(1)}, u32[]{:S(2)}, u32[]{:S(2)}) collective-permute-start(bf16[76,16,128]{2,1,0:T(8,128)(2,1)S(1)} %pad_maximum_fusion.1), channel_id=1, source_target_pairs={{0,8},{4,20},{8,0},{12,28},{16,24},{20,4},{24,16},{28,12},{1,9},{5... | collective-permute-start | bytes 933896 | tf_op jit(solution)/shard_map/ppermute | solution.py:354
  22.3 11.3 %collective-permute-start.8 = (bf16[152,16,128]{2,1,0:T(8,128)(2,1)S(1)}, bf16[152,16,128]{2,1,0:T(8,128)(2,1)S(1)}, u32[]{:S(2)}, u32[]{:S(2)}) collective-permute-start(bf16[152,16,128]{2,1,0:T(8,128)(2,1)S(1)} %pad_maximum_fusion), channel_id=1, source_target_pairs={{0,16},{4,12},{8,24},{12,4},{16,0},{20,28},{24,8},{28,20},{1,17},{... | collective-permute-start | bytes 1867784 | tf_op jit(solution)/shard_map/ppermute | solution.py:354
  24.2 6.9 %collective-permute-start.9 = (bf16[228,16,128]{2,1,0:T(8,128)(2,1)S(1)}, bf16[228,16,128]{2,1,0:T(8,128)(2,1)S(1)}, u32[]{:S(2)}, u32[]{:S(2)}) collective-permute-start(bf16[228,16,128]{2,1,0:T(8,128)(2,1)S(1)} %constant_dynamic-update-slice_fusion.2), channel_id=1, source_target_pairs={{0,4},{4,0},{8,12},{12,8},{16,20},{20,16},{24,28},{28,24},{1,5},{5... | collective-permute-start | bytes 2801672 | tf_op jit(solution)/shard_map/ppermute | solution.py:354
  30.1 4.5 %collective-permute-start.10 = (bf16[76,16,128]{2,1,0:T(8,128)(2,1)S(1)}, bf16[76,16,128]{2,1,0:T(8,128)(2,1)S(1)}, u32[]{:S(2)}, u32[]{:S(2)}) collective-permute-start(bf16[76,16,128]{2,1,0:T(8,128)(2,1)S(1)} %collective-permute-done.3.refs_1_), channel_id=1, source_target_pairs={{0,4},{4,0},{8,12},{12,8},{16,20},{20,16},{24,28},{28,24},{1,5},{5... | collective-permute-start | bytes 933896 | tf_op jit(solution)/shard_map/ppermute | solution.py:354
  30.1 6.9 %collective-permute-start.7 = (bf16[76,16,128]{2,1,0:T(8,128)(2,1)S(1)}, bf16[76,16,128]{2,1,0:T(8,128)(2,1)S(1)}, u32[]{:S(2)}, u32[]{:S(2)}) collective-permute-start(bf16[76,16,128]{2,1,0:T(8,128)(2,1)S(1)} %collective-permute-done.3.refs_1_), channel_id=1, source_target_pairs={{0,16},{4,12},{8,24},{12,4},{16,0},{20,28},{24,8},{28,20},{1,17},{... | collective-permute-start | bytes 933896 | tf_op jit(solution)/shard_map/ppermute | solution.py:354
  33.6 3.9 %collective-permute-start.11 = (bf16[152,16,128]{2,1,0:T(8,128)(2,1)S(1)}, bf16[152,16,128]{2,1,0:T(8,128)(2,1)S(1)}, u32[]{:S(2)}, u32[]{:S(2)}) collective-permute-start(bf16[152,16,128]{2,1,0:T(8,128)(2,1)S(1)} %collective-permute-done.8.refs_1_), channel_id=1, source_target_pairs={{0,4},{4,0},{8,12},{12,8},{16,20},{20,16},{24,28},{28,24},{1,5},{5... | collective-permute-start | bytes 1867784 | tf_op jit(solution)/shard_map/ppermute | solution.py:354
  37.0 2.2 %collective-permute-start.12 = (bf16[76,16,128]{2,1,0:T(8,128)(2,1)S(1)}, bf16[76,16,128]{2,1,0:T(8,128)(2,1)S(1)}, u32[]{:S(2)}, u32[]{:S(2)}) collective-permute-start(bf16[76,16,128]{2,1,0:T(8,128)(2,1)S(1)} %collective-permute-done.7.refs_1_), channel_id=1, source_target_pairs={{0,4},{4,0},{8,12},{12,8},{16,20},{20,16},{24,28},{28,24},{1,5},{5... | collective-permute-start | bytes 933896 | tf_op jit(solution)/shard_map/ppermute | solution.py:354
